TPU v7x, 32 devices: a whole 2x2x4 slice. The times are simulated.
32 devices in a mesh: section: 4 (over x, core), seq: 8 (over z, y).
Axes of the slice: x: 2, y: 2, z: 4, core: 2. Of those that a mesh axis runs over, the one named last changes fastest.
Arguments:
- saved_section_input: bfloat16 [4, 1024, 1024], P('section', 'seq'), may hold values from -6 to 6
- out_cot: bfloat16 [4, 1024, 1024], P('section', 'seq'), may hold values from -6 to 6
- kernel_weight: bfloat16 [4, 2, 3, 64, 16, 32], P('section'), may hold values from -0.875 to 0.875
- blend_weight: bfloat16 [4, 2, 1024, 1024], P('section'), may hold values from -0.1875 to 0.1875
- hazard_head: bfloat16 [1024, 64], replicated, may hold values from -0.75 to 0.75
- labels: int32 [1024], P('seq'), may hold values from 0 to 63
- events: int32 [1024], P('seq'), may hold values 0 or 1
Outputs:
- input_grad: bfloat16 [4, 1024, 1024], P('section', 'seq')
- next_cot: bfloat16 [4, 1024, 1024], P('section', 'seq')
- mix_grad: float32 [4, 1024, 2, 1024], P('section', 'seq')
- conv_grad: float32 [4, 2, 3, 64, 16, 32], P('section', None, None, 'seq')
All inputs are finite; a program needn't handle non-finite values. No bound on the sum of `events` on one device may be relied on, other than what follows from the above.
Results may differ from a plain program's by a relative error of at most 0.006.
Values may be sent and summed in bfloat16 or wider, within the bound.
No kernel may reach another device: no remote copies, remote signals or barrier semaphores. Data moves between devices by JAX's collectives and lax.ppermute only.
A program may use at most 64 MiB of HBM per device.

v0:
```python
import jax
import jax.numpy as jnp
from jax import lax
from jax.sharding import PartitionSpec as P

SPAN = 2


exact_mode = lax.Precision.HIGHEST


def from_behind(value, axis, steps):
    count = lax.axis_size(axis)
    leading, last = (max(0, -steps), min(count, count - steps))
    return lax.ppermute(value, axis, [(source, source + steps) for source in range(leading, last)])


def gate_values(preact, group_size):
    filt = preact[..., :group_size].astype(jnp.float32)
    gate_part = preact[..., group_size:].astype(jnp.float32)
    return jnp.tanh(filt) * jax.nn.sigmoid(gate_part)


def gate_grad(preact, dgated, group_size):
    filt = jnp.tanh(preact[..., :group_size].astype(jnp.float32))
    gate_part = jax.nn.sigmoid(preact[..., group_size:].astype(jnp.float32))
    return jnp.concatenate(
        [dgated * gate_part * (1.0 - filt * filt), dgated * filt * gate_part * (1.0 - gate_part)],
        axis=-1,
    )


def layer_forward_pass(tap_list, weight_set, mix_matrix, groups, group_size):
    row_count, channels = tap_list[0].shape
    summed = jnp.zeros((row_count, groups, 2 * group_size), jnp.float32)
    for k in range(3):
        summed = summed + jnp.einsum(
            "rgi,gio->rgo",
            tap_list[k].reshape(row_count, groups, group_size),
            weight_set[k],
            preferred_element_type=jnp.float32,
        )
    preact = summed.astype(jnp.bfloat16)
    gated = gate_values(preact, group_size).reshape(row_count, channels).astype(jnp.bfloat16)
    output = (
        tap_list[0].astype(jnp.float32)
        + jnp.dot(gated, mix_matrix, preferred_element_type=jnp.float32)
    ).astype(jnp.bfloat16)
    return (preact, gated, output)


def transpose_tap(dpre, weight_set, k):
    return jnp.einsum("rgo,gio->rgi", dpre, weight_set[k].astype(jnp.float32), precision=exact_mode)


def weight_terms(tap_list, dpre, groups, group_size):
    row_count = dpre.shape[0]
    return jnp.stack(
        [
            jnp.einsum(
                "rgi,rgo->gio",
                tap.reshape(row_count, groups, group_size).astype(jnp.float32),
                dpre,
                precision=exact_mode,
            )
            for tap in tap_list
        ]
    )


def body(saved_section_input, out_cot, kernel_weight, blend_weight, hazard_head, labels, events):
    first_input = saved_section_input[0]
    row_count, channels = first_input.shape
    weights = kernel_weight[0]
    mixes = blend_weight[0]
    groups = weights.shape[2]
    group_size = weights.shape[3]
    short_reach = row_count // 8
    edge_rows = from_behind(first_input[row_count - 2 * short_reach :], "seq", 1)
    extended = jnp.concatenate([edge_rows, first_input], axis=0)
    taps_short = [
        extended[2 * short_reach - k * short_reach : 2 * short_reach - k * short_reach + row_count]
        for k in range(3)
    ]
    pre_short, gated_short, middle = layer_forward_pass(
        taps_short, weights[0], mixes[0], groups, group_size
    )
    near_rows = from_behind(middle, "seq", SPAN)
    far_rows = from_behind(middle, "seq", 2 * SPAN)
    taps_long = [middle, near_rows, far_rows]
    pre_long, gated_long, top = layer_forward_pass(
        taps_long, weights[1], mixes[1], groups, group_size
    )
    section_index = lax.axis_index("section")
    is_last = section_index == lax.axis_size("section") - 1
    logits = jnp.dot(top, hazard_head, preferred_element_type=jnp.float32)
    hazard = jax.nn.sigmoid(logits)
    bin_ids = lax.broadcasted_iota(jnp.int32, logits.shape, 1)
    below = (bin_ids <= labels[:, None]).astype(jnp.float32)
    at_label = (bin_ids == labels[:, None]).astype(jnp.float32) * events[:, None].astype(
        jnp.float32
    )
    dlogit = (hazard * below - at_label).astype(jnp.bfloat16)
    loss_cot = jnp.dot(dlogit, hazard_head.T, preferred_element_type=jnp.float32)
    upstream_gradient = (out_cot[0].astype(jnp.float32) + jnp.where(is_last, loss_cot, 0.0)).astype(
        jnp.bfloat16
    )
    dgated_long = jnp.dot(
        upstream_gradient, mixes[1].T, preferred_element_type=jnp.float32
    ).reshape(row_count, groups, group_size)
    dpre_long = gate_grad(pre_long, dgated_long, group_size)
    near_cot = from_behind(dpre_long, "seq", -SPAN)
    far_cot = from_behind(dpre_long, "seq", -2 * SPAN)
    convolution_wide = (
        transpose_tap(dpre_long, weights[1], 0)
        + transpose_tap(near_cot, weights[1], 1)
        + transpose_tap(far_cot, weights[1], 2)
    )
    between_gradient = (
        upstream_gradient.astype(jnp.float32) + convolution_wide.reshape(row_count, channels)
    ).astype(jnp.bfloat16)
    dgated_short = jnp.dot(
        between_gradient, mixes[0].T, preferred_element_type=jnp.float32
    ).reshape(row_count, groups, group_size)
    dpre_short = gate_grad(pre_short, dgated_short, group_size)
    next_rows = from_behind(dpre_short[: 2 * short_reach].astype(jnp.bfloat16), "seq", -1).astype(
        jnp.float32
    )
    extended_back = jnp.concatenate([dpre_short, next_rows], axis=0)
    convolution_narrow = transpose_tap(dpre_short, weights[0], 0)
    for k in range(1, 3):
        convolution_narrow = convolution_narrow + transpose_tap(
            extended_back[k * short_reach : k * short_reach + row_count], weights[0], k
        )
    input_gradient_rows = (
        between_gradient.astype(jnp.float32) + convolution_narrow.reshape(row_count, channels)
    ).astype(jnp.bfloat16)
    received = from_behind(input_gradient_rows, "section", -1)
    next_cot = jnp.where(is_last, upstream_gradient, received)
    mix_share = lax.psum_scatter(
        jnp.stack(
            [
                jnp.dot(gated_short.T, between_gradient, preferred_element_type=jnp.float32),
                jnp.dot(gated_long.T, upstream_gradient, preferred_element_type=jnp.float32),
            ],
            axis=1,
        ),
        "seq",
        scatter_dimension=0,
        tiled=True,
    )
    conv_terms = jnp.stack(
        [
            weight_terms(taps_short, dpre_short, groups, group_size),
            weight_terms(taps_long, dpre_long, groups, group_size),
        ]
    )
    conv_share = lax.psum_scatter(conv_terms, "seq", scatter_dimension=2, tiled=True)
    return (input_gradient_rows[None], next_cot[None], mix_share[None], conv_share[None])


def solution(mesh):
    return jax.shard_map(
        body,
        mesh=mesh,
        in_specs=(
            P("section", "seq", None),
            P("section", "seq", None),
            P("section", None, None, None, None, None),
            P("section", None, None, None),
            P(),
            P("seq"),
            P("seq"),
        ),
        out_specs=(
            P("section", "seq", None),
            P("section", "seq", None),
            P("section", "seq", None, None),
            P("section", None, None, "seq", None, None),
        ),
        check_vma=False,
    )
```

profile of v0, /device:TPU:1, one launch (start us, length us, event | category | flops | bytes accessed | tf_op | source)
XLA Modules:
  0.0 364.1 jit_solution(12235754357760212293)
XLA Ops:
  7.2 0.9 slice_bitcast_fusion
  8.1 4.1 %collective-permute-start = (bf16[32,1024]{1,0:T(8,128)(2,1)S(1)}, bf16[32,1024]{1,0:T(8,128)(2,1)S(1)}, u32[]{:S(2)}, u32[]{:S(2)}) collective-permute-start(bf16[32,1024]{1,0:T(8,128)(2,1)S(1)} %slice_bitcast_fusion), channel_id=1, source_target_pairs={{0,1},{1,2},{2,3},{3,4},{4,5},{5,6},{6,7},{8,9},{9,10},{10,11},{11... | collective-permute-start | bytes 196616 | tf_op jit(solution)/shard_map/ppermute | solution.py:15
  12.2 4.7 %fusion.79 = (bf16[1,1,1024,1024]{3,2,1,0:T(8,128)(2,1)}, bf16[1,1,1024,1024]{3,2,1,0:T(8,128)(2,1)}) fusion(bf16[1,2,1024,1024]{3,2,1,0:T(8,128)(2,1)} %param.10), kind=kLoop, calls=%fused_computation.102 | loop fusion | bytes 8388608 | tf_op jit(solution)/shard_map/slice | solution.py:92
  17.6 0.9 copy.87
  21.1 1.2 fusion.7
  22.3 1.2 multiply_convert_fusion.1
  23.5 1.2 fusion.20
  24.7 1.1 copy.61
  25.8 4.9 %collective-permute-start.2 = (bf16[128,1024]{1,0:T(8,128)(2,1)}, bf16[128,1024]{1,0:T(8,128)(2,1)}, u32[]{:S(2)}, u32[]{:S(2)}) collective-permute-start(bf16[128,1024]{1,0:T(8,128)(2,1)} %fusion.20), channel_id=1, source_target_pairs={{0,4},{1,5},{2,6},{3,7},{8,12},{9,13},{10,14},{11,15},{16,20},{17,... | collective-permute-start | bytes 786440 | tf_op jit(solution)/shard_map/ppermute | solution.py:15
  30.8 3.2 collective-permute-start.1
  34.4 6.3 %collective-permute-done.1 = bf16[128,1024]{1,0:T(8,128)(2,1)S(1)} collective-permute-done((bf16[128,1024]{1,0:T(8,128)(2,1)}, bf16[128,1024]{1,0:T(8,128)(2,1)S(1)}, u32[]{:S(2)}, u32[]{:S(2)}) %collective-permute-start.1) | collective-permute-done | bytes 262176 | tf_op jit(solution)/shard_map/ppermute | solution.py:15
  41.3 1.1 copy.65
  42.4 1.3 fusion.8
  44.0 0.5 copy-done.19
  44.5 2.3 fusion.44
  47.1 2.4 subtract_multiply_fusion.3
  49.6 1.3 collective-permute-start.3
  50.9 1.5 collective-permute-start.4
  52.4 1.7 convolution_bitcast_fusion.7
  54.2 1.7 convolution_bitcast_fusion.6
  55.9 1.7 convolution_bitcast_fusion.5
  57.6 0.6 fusion.62
  58.2 24.6 %collective-permute-done.3 = f32[128,64,32]{0,2,1:T(8,128)S(1)} collective-permute-done((f32[128,64,32]{0,2,1:T(8,128)S(1)}, f32[128,64,32]{0,2,1:T(8,128)S(1)}, u32[]{:S(2)}, u32[]{:S(2)}) %collective-permute-start.3) | collective-permute-done | bytes 1048608 | tf_op jit(solution)/shard_map/ppermute | solution.py:15
  82.8 0.6 convolution_add_fusion.5
  83.4 46.1 %collective-permute-done.4 = f32[128,64,32]{0,2,1:T(8,128)S(1)} collective-permute-done((f32[128,64,32]{0,2,1:T(8,128)S(1)}, f32[128,64,32]{0,2,1:T(8,128)S(1)}, u32[]{:S(2)}, u32[]{:S(2)}) %collective-permute-start.4) | collective-permute-done | bytes 1048608 | tf_op jit(solution)/shard_map/ppermute | solution.py:15
  129.6 0.6 convolution_add_fusion.4
  130.5 2.4 subtract_multiply_fusion.1
  132.9 0.9 convolution_bitcast_fusion.9
  133.9 0.9 convolution_bitcast_fusion.8
  134.8 0.9 convolution_bitcast_fusion.10
  136.1 1.9 copy_bitcast_fusion
  138.0 3.8 %reshape.82 = f32[64,3072]{1,0:T(8,128)} reshape(f32[64,2,3,16,32]{4,3,2,1,0:T(8,128)} %copy_bitcast_fusion) | data formatting | bytes 1572864
  141.9 0.7 convolution_bitcast_fusion
  142.8 0.7 convolution_bitcast_fusion.1
  143.5 4.1 %pad_maximum_fusion = f32[1024,2,1024]{2,0,1:T(8,128)} fusion(f32[1024,1,1024]{2,0,1:T(8,128)S(1)} %convolution_bitcast_fusion, f32[1024,1,1024]{2,0,1:T(8,128)S(1)} %convolution_bitcast_fusion.1), kind=kLoop, calls=%fused_computation | loop fusion | flops 2097152 | bytes 16777216 | tf_op jit(solution)/shard_map/stack | solution.py:141
  147.7 1.5 collective-permute-start.5
  149.2 0.6 fusion.52
  149.8 13.3 %collective-permute-done.5 = bf16[32,64,32]{0,2,1:T(8,128)(2,1)S(1)} collective-permute-done((bf16[32,64,32]{0,2,1:T(8,128)(2,1)S(1)}, bf16[32,64,32]{0,2,1:T(8,128)(2,1)S(1)}, u32[]{:S(2)}, u32[]{:S(2)}) %collective-permute-start.5) | collective-permute-done | bytes 131104 | tf_op jit(solution)/shard_map/ppermute | solution.py:15
  163.5 0.7 convolution_add_fusion.3
  164.4 0.7 convolution_add_fusion.2
  165.5 3.8 %collective-permute-start.6 = (bf16[128,1024]{1,0:T(8,128)(2,1)S(1)}, bf16[128,1024]{1,0:T(8,128)(2,1)S(1)}, u32[]{:S(2)}, u32[]{:S(2)}) collective-permute-start(bf16[128,1024]{1,0:T(8,128)(2,1)S(1)} %add_convert_fusion), channel_id=1, source_target_pairs={{8,0},{16,8},{24,16},{9,1},{17,9},{25,17},{10,2},{18,10},{26,18},{... | collective-permute-start | bytes 786440 | tf_op jit(solution)/shard_map/ppermute | solution.py:15
  169.2 5.2 %collective-permute-done.6 = bf16[128,1024]{1,0:T(8,128)(2,1)S(1)} collective-permute-done((bf16[128,1024]{1,0:T(8,128)(2,1)S(1)}, bf16[128,1024]{1,0:T(8,128)(2,1)S(1)}, u32[]{:S(2)}, u32[]{:S(2)}) %collective-permute-start.6) | collective-permute-done | bytes 262176 | tf_op jit(solution)/shard_map/ppermute | solution.py:15
  174.4 0.7 select_bitcast_fusion
  175.1 25.2 %reduce-scatter.7.cloned.1.call-done = f32[8,3072]{1,0:T(8,128)} async-done(((f32[64,3072]{1,0:T(8,128)}), f32[8,3072]{1,0:T(8,128)}) %reduce-scatter.7.cloned.1.call-update) | async-done | bytes 98320
  200.3 1.0 reshape.83
  201.4 0.8 copy_bitcast_fusion.1
  202.1 152.1 %reduce-scatter.5.cloned.1.call-done = f32[128,2,1024]{2,0,1:T(8,128)} async-done(((f32[1024,2,1024]{2,0,1:T(8,128)}), f32[128,2,1024]{2,0,1:T(8,128)}) %reduce-scatter.5.cloned.1.call-update) | async-done | bytes 1048592 | tf_op jit(solution)/shard_map/reduce_scatter | solution.py:140
  354.2 3.0 copy.75
  (86 shorter events, 6.3 us)
Async XLA Ops:
  7.2 37.4 %copy-start = (bf16[1024,64]{0,1:T(8,128)(2,1)S(1)}, bf16[1024,64]{0,1:T(8,128)(2,1)}, u32[]{:S(2)}) copy-start(bf16[1024,64]{0,1:T(8,128)(2,1)} %param.11) | copy-start | bytes 393220
  7.2 193.1 %reduce-scatter.7.cloned.1.call-start = ((), (), s32[]{:S(2)}) async-start(), calls=%async_computation.3 | async-start | bytes 884736
  8.1 8.9 %copy-start.22 = (bf16[1,2,3,64,16,32]{3,5,4,2,1,0:T(8,128)(2,1)S(1)}, bf16[1,2,3,64,16,32]{3,5,4,2,1,0:T(8,128)(2,1)}, u32[]{:S(2)}) copy-start(bf16[1,2,3,64,16,32]{3,5,4,2,1,0:T(8,128)(2,1)} %param.9) | copy-start | bytes 1179652
  8.1 8.9 %copy-start.2 = (bf16[1,128,1024]{2,1,0:T(8,128)(2,1)S(1)}, bf16[1,128,1024]{2,1,0:T(8,128)(2,1)}, u32[]{:S(2)}) copy-start(bf16[1,128,1024]{2,1,0:T(8,128)(2,1)} %param.7) | copy-start | bytes 786436
  8.1 11.8 %collective-permute-start = (bf16[32,1024]{1,0:T(8,128)(2,1)S(1)}, bf16[32,1024]{1,0:T(8,128)(2,1)S(1)}, u32[]{:S(2)}, u32[]{:S(2)}) collective-permute-start(bf16[32,1024]{1,0:T(8,128)(2,1)S(1)} %slice_bitcast_fusion), channel_id=1, source_target_pairs={{0,1},{1,2},{2,3},{3,4},{4,5},{5,6},{6,7},{8,9},{9,10},{10,11},{11... | collective-permute-start | bytes 196616 | tf_op jit(solution)/shard_map/ppermute | solution.py:15
  17.0 0.7 copy-start.25
  19.1 14.9 %copy-start.5 = (bf16[1,1,1,64,16,32]{5,4,3,2,1,0:T(8,128)(2,1)}, bf16[1,1,1,64,16,32]{5,4,3,2,1,0:T(8,128)(2,1)S(1)}, u32[]{:S(2)}) copy-start(bf16[1,1,1,64,16,32]{5,4,3,2,1,0:T(8,128)(2,1)S(1)} %copy.85) | copy-start | bytes 196612
  19.3 1.7 copy-start.11
  20.1 1.0 copy-start.14
  20.3 0.8 copy-start.3
  20.7 2.8 copy-start.1
  23.5 10.9 %copy-start.9 = (bf16[128,64,16]{0,2,1:T(8,128)(2,1)}, bf16[128,64,16]{0,2,1:T(8,128)(2,1)S(1)}, u32[]{:S(2)}) copy-start(bf16[128,64,16]{0,2,1:T(8,128)(2,1)S(1)} %multiply_convert_fusion.1) | copy-start | bytes 786436
  25.8 15.0 %copy-start.7 = (bf16[128,1024]{0,1:T(8,128)(2,1)}, bf16[128,1024]{0,1:T(8,128)(2,1)S(1)}, u32[]{:S(2)}) copy-start(bf16[128,1024]{0,1:T(8,128)(2,1)S(1)} %copy.61) | copy-start | bytes 786436
  25.8 15.4 %collective-permute-start.2 = (bf16[128,1024]{1,0:T(8,128)(2,1)}, bf16[128,1024]{1,0:T(8,128)(2,1)}, u32[]{:S(2)}, u32[]{:S(2)}) collective-permute-start(bf16[128,1024]{1,0:T(8,128)(2,1)} %fusion.20), channel_id=1, source_target_pairs={{0,4},{1,5},{2,6},{3,7},{8,12},{9,13},{10,14},{11,15},{16,20},{17,... | collective-permute-start | bytes 786440 | tf_op jit(solution)/shard_map/ppermute | solution.py:15
  30.8 9.9 %collective-permute-start.1 = (bf16[128,1024]{1,0:T(8,128)(2,1)}, bf16[128,1024]{1,0:T(8,128)(2,1)S(1)}, u32[]{:S(2)}, u32[]{:S(2)}) collective-permute-start(bf16[128,1024]{1,0:T(8,128)(2,1)} %fusion.20), channel_id=1, source_target_pairs={{0,2},{1,3},{2,4},{3,5},{4,6},{5,7},{8,10},{9,11},{10,12},{11,13},... | collective-permute-start | bytes 786440 | tf_op jit(solution)/shard_map/ppermute | solution.py:15
  41.2 3.3 copy-start.26
  43.7 0.8 copy-start.19
  43.7 3.1 copy-start.23
  44.0 5.5 %copy-start.20 = (bf16[128,64,16]{0,2,1:T(8,128)(2,1)}, bf16[128,64,16]{0,2,1:T(8,128)(2,1)S(1)}, u32[]{:S(2)}) copy-start(bf16[128,64,16]{0,2,1:T(8,128)(2,1)S(1)} %multiply_convert_fusion) | copy-start | bytes 786436
  49.5 2.9 copy-start.8
  49.6 33.2 %collective-permute-start.3 = (f32[128,64,32]{0,2,1:T(8,128)S(1)}, f32[128,64,32]{0,2,1:T(8,128)S(1)}, u32[]{:S(2)}, u32[]{:S(2)}) collective-permute-start(f32[128,64,32]{0,2,1:T(8,128)S(1)} %pad_maximum_fusion.4), channel_id=1, source_target_pairs={{2,0},{3,1},{4,2},{5,3},{6,4},{7,5},{10,8},{11,9},{12,10},{13,11},... | collective-permute-start | bytes 3145736 | tf_op jit(solution)/shard_map/ppermute | solution.py:15
  50.9 78.6 %collective-permute-start.4 = (f32[128,64,32]{0,2,1:T(8,128)S(1)}, f32[128,64,32]{0,2,1:T(8,128)S(1)}, u32[]{:S(2)}, u32[]{:S(2)}) collective-permute-start(f32[128,64,32]{0,2,1:T(8,128)S(1)} %pad_maximum_fusion.4), channel_id=1, source_target_pairs={{4,0},{5,1},{6,2},{7,3},{12,8},{13,9},{14,10},{15,11},{20,16},{21,... | collective-permute-start | bytes 3145736 | tf_op jit(solution)/shard_map/ppermute | solution.py:15
  54.2 3.5 copy-start.6
  57.6 71.9 %copy-start.13 = (bf16[1,1,1,64,16,32]{5,4,3,2,1,0:T(8,128)(2,1)S(1)}, bf16[1,1,1,64,16,32]{5,4,3,2,1,0:T(8,128)(2,1)}, u32[]{:S(2)}) copy-start(bf16[1,1,1,64,16,32]{5,4,3,2,1,0:T(8,128)(2,1)} %copy.87) | copy-start | bytes 196612
  130.4 2.5 copy-start.4
  130.4 3.4 copy-start.15
  133.9 1.9 copy-start.16
  133.9 1.9 copy-start.17
  133.9 1.9 copy-start.18
  138.0 3.8 %copy-start.21 = (bf16[128,64,16]{0,2,1:T(8,128)(2,1)S(1)}, bf16[128,64,16]{0,2,1:T(8,128)(2,1)}, u32[]{:S(2)}) copy-start(bf16[128,64,16]{0,2,1:T(8,128)(2,1)} %copy-done.20) | copy-start | bytes 786436
  141.8 1.0 copy-start.10
  141.8 212.4 %reduce-scatter.5.cloned.1.call-start = ((), (), s32[]{:S(2)}) async-start(), calls=%async_computation.2 | async-start | bytes 9437184 | tf_op jit(solution)/shard_map/reduce_scatter | solution.py:140
  147.7 15.4 %collective-permute-start.5 = (bf16[32,64,32]{0,2,1:T(8,128)(2,1)S(1)}, bf16[32,64,32]{0,2,1:T(8,128)(2,1)S(1)}, u32[]{:S(2)}, u32[]{:S(2)}) collective-permute-start(bf16[32,64,32]{0,2,1:T(8,128)(2,1)S(1)} %fusion.48), channel_id=1, source_target_pairs={{1,0},{2,1},{3,2},{4,3},{5,4},{6,5},{7,6},{9,8},{10,9},{11,10},{12... | collective-permute-start | bytes 393224 | tf_op jit(solution)/shard_map/ppermute | solution.py:15
  163.5 1.0 copy-start.12
  165.4 191.8 %copy-start.24 = (bf16[128,1024]{1,0:T(8,128)(2,1)}, bf16[128,1024]{1,0:T(8,128)(2,1)S(1)}, u32[]{:S(2)}) copy-start(bf16[128,1024]{1,0:T(8,128)(2,1)S(1)} %add_convert_fusion) | copy-start | bytes 786436
  165.5 8.9 %collective-permute-start.6 = (bf16[128,1024]{1,0:T(8,128)(2,1)S(1)}, bf16[128,1024]{1,0:T(8,128)(2,1)S(1)}, u32[]{:S(2)}, u32[]{:S(2)}) collective-permute-start(bf16[128,1024]{1,0:T(8,128)(2,1)S(1)} %add_convert_fusion), channel_id=1, source_target_pairs={{8,0},{16,8},{24,16},{9,1},{17,9},{25,17},{10,2},{18,10},{26,18},{... | collective-permute-start | bytes 786440 | tf_op jit(solution)/shard_map/ppermute | solution.py:15
Sparse Core Ops, SparseCore 0:
  141.9 58.3 reduce-scatter.6
  204.4 149.7 reduce-scatter.4
where the time goes:
time: 365 us; the launch traced here: 364 us
  waiting for transfers between devices  273 us (75%)
  matrix products  25.8 us (7%)
  local copies, waits for them, and re-layouts  21.2 us (6%)
  starting transfers between devices  20.4 us (6%)
  between operations  14.7 us (4%)
  other arithmetic  9.26 us (3%)
    reduce_scatter x1, waiting for transfers between devices, body(): lax.psum_scatter(jnp.stack([jnp.dot(gated_short.T, between_gradient, pref...  152 us
    ppermute x7, waiting for transfers between devices, from_behind(): lax.ppermute(value, axis, [(source, source + steps) for source in range(l...  95.5 us
    unnamed x3, waiting for transfers between devices  25.2 us
    ppermute x7, starting transfers between devices, from_behind(): lax.ppermute(value, axis, [(source, source + steps) for source in range(l...  20.3 us
    unnamed x64, local copies, waits for them, and re-layouts  11.6 us
    dot_general x6, matrix products, weight_terms(): jnp.einsum('rgi,rgo->gio', tap.reshape(row_count, groups, group_size).ast...  7.99 us
  transfers between devices with their start and end apart: 9, of which 7 were waited for; matrix products, arithmetic and copies ran while one was open for 7% of the time, Pallas kernels for 0%

commit v1 on v0

v1 whole, which is shorter than its diff:
```python
import functools

import jax
import jax.numpy as jnp
from jax import lax
from jax.experimental import pallas as pl
from jax.experimental.pallas import tpu as pltpu
from jax.sharding import PartitionSpec as P

SPAN = 2
SLAB = 128
F32 = jnp.float32
BF16 = jnp.bfloat16
HALO = 32
REACH = 16


def nn(a, b):
    return lax.dot_general(a, b, (((1,), (0,)), ((), ())), preferred_element_type=F32)


def nt(a, b):
    return lax.dot_general(a, b, (((1,), (1,)), ((), ())), preferred_element_type=F32)


def tn(a, b, precision=None):
    return lax.dot_general(a, b, (((0,), (0,)), ((), ())), preferred_element_type=F32, precision=precision)


def sigmoid(x):
    return 0.5 * jnp.tanh(0.5 * x) + 0.5


def lanes(slab, width=SLAB):
    return pl.ds(pl.multiple_of(slab * width, width), width)


def same_group(group_size):
    rows = lax.broadcasted_iota(jnp.int32, (SLAB, 2 * SLAB), 0) // group_size
    columns = lax.broadcasted_iota(jnp.int32, (SLAB, 2 * SLAB), 1) % SLAB // group_size
    return rows == columns


def spread(group_size, shift, width):
    o = lax.broadcasted_iota(jnp.int32, (width, 2 * SLAB), 0) - shift
    column = lax.broadcasted_iota(jnp.int32, (width, 2 * SLAB), 1)
    return (o == column % group_size + jnp.where(column >= SLAB, group_size, 0)).astype(F32)


def conv(taps, weight):
    acc = nn(jnp.concatenate(taps[:2], axis=1), weight[: 2 * SLAB]) + nn(taps[2], weight[2 * SLAB :])
    return acc.astype(BF16)


def gates(pre):
    pre = pre.astype(F32)
    return jnp.tanh(pre[:, :SLAB]), sigmoid(pre[:, SLAB:])


def gate_grad(tanh, sig, dgated):
    one = dgated * sig
    return jnp.concatenate(
        [(one * (1.0 - tanh * tanh)).astype(BF16), (one * tanh * (1.0 - sig)).astype(BF16)], axis=1
    )


def chunks(blocks, step):
    some = min(blocks, 4)
    if some == blocks:
        step(0, blocks)
    else:
        pl.loop(0, blocks // some)(lambda i: step(i * some, some))


def weight_kernel(group_size, w_ref, out_ref):
    layers, slabs = out_ref.shape[:2]
    one_hot = spread(group_size, 0, 2 * group_size).astype(BF16)
    keep = same_group(group_size)
    for layer in range(layers):
        for k in range(3):
            def one(slab, carry, layer=layer, k=k):
                row = pl.multiple_of((layer * 3 + k) * slabs * SLAB + slab * SLAB, SLAB)
                tiled = nn(w_ref[pl.ds(row, SLAB), :], one_hot)
                out_ref[layer, slab, k * SLAB : (k + 1) * SLAB, :] = jnp.where(keep, tiled, 0.0).astype(BF16)
                return carry
            lax.fori_loop(0, slabs, one, 0)


def forward_kernel(blocks, meta, *refs):
    inputs, tails = refs[:blocks], refs[blocks : 2 * blocks]
    codes, weights, mixes, head, x_ref, mid_ref, pre_ref, gated_ref, dlogit_ref, short_ref = refs[2 * blocks :]
    row_count, channels = inputs[0].shape
    slabs = channels // SLAB
    y = meta[1]
    for p in range(blocks):
        z = meta[3 + p]
        x_ref[z, HALO:, :] = inputs[p][...]
        x_ref[z + 1 - y, :HALO, :] = tails[p][...]

    @pl.when(y == 0)
    def _():
        x_ref[0, :HALO, :] = jnp.zeros((HALO, channels), BF16)

    mid_ref[0:SPAN] = jnp.zeros((SPAN, row_count, channels), BF16)

    def short(first, count):
        rows = count * row_count
        here = pl.ds(first, count)

        def one(slab, carry):
            taps = [
                x_ref[here, HALO - k * REACH : HALO - k * REACH + row_count, lanes(slab)].reshape(rows, SLAB)
                for k in range(3)
            ]
            tanh, sig = gates(conv(taps, weights[0, slab]))
            short_ref[:rows, lanes(slab)] = (tanh * sig).astype(BF16)
            return carry

        lax.fori_loop(0, slabs, one, 0)

        def mix(j, carry):
            column = lanes(j, 256)
            value = x_ref[here, HALO:, column].reshape(rows, 256).astype(F32) + nn(short_ref[:rows, :], mixes[0, :, column])
            mid_ref[pl.ds(first + SPAN, count), :, column] = value.astype(BF16).reshape(count, row_count, 256)
            return carry

        lax.fori_loop(0, channels // 256, mix, 0)

    chunks(blocks, short)

    def long(first, count):
        rows = count * row_count
        here = pl.ds(first, count)

        def one(slab, carry):
            taps = [mid_ref[pl.ds(first + 2 - k, count), :, lanes(slab)].reshape(rows, SLAB) for k in range(3)]
            pre = conv(taps, weights[1, slab])
            pre_ref[here, :, lanes(slab, 2 * SLAB)] = pre.reshape(count, row_count, 2 * SLAB)
            tanh, sig = gates(pre)
            gated_ref[here, :, lanes(slab)] = (tanh * sig).astype(BF16).reshape(count, row_count, SLAB)
            return carry

        lax.fori_loop(0, slabs, one, 0)

    chunks(blocks, long)

    @pl.when(meta[2] == 1)
    def _():
        def hazard(z, carry):
            top = (mid_ref[z + SPAN].astype(F32) + nn(gated_ref[z], mixes[1])).astype(BF16)
            logits = lax.dot_general(head[...], top, (((0,), (1,)), ((), ())), preferred_element_type=F32)
            bins = lax.broadcasted_iota(jnp.int32, logits.shape, 0)
            code = codes[z * SPAN + y]
            label, event = code[0:1, :], code[1:2, :].astype(F32)
            dlogit = jnp.where(bins <= label, jax.nn.sigmoid(logits), 0.0) - jnp.where(bins == label, event, 0.0)
            dlogit_ref[z] = dlogit.astype(BF16)
            return carry

        lax.fori_loop(0, blocks, hazard, 0)

    @pl.when(meta[2] == 0)
    def _():
        dlogit_ref[...] = jnp.zeros(dlogit_ref.shape, BF16)


def weight_sums(group_size, taps, dpre):
    keep = same_group(group_size)
    total = jnp.zeros((SLAB, SLAB), F32)
    for k, tap in enumerate(taps):
        product = jnp.where(keep, tn(tap, dpre), 0.0)
        total = total + lax.dot_general(
            product,
            spread(group_size, 2 * group_size * k, SLAB),
            (((1,), (1,)), ((), ())),
            preferred_element_type=F32,
            precision=lax.Precision.HIGHEST,
        )
    return total


def split_pair(meta, pair, first, total_ref, own_ref, send_ref):
    share = pair // SPAN
    begin = meta[0] * pair - first
    own = pl.multiple_of(begin + meta[1] * share, share)
    other = pl.multiple_of(begin + (1 - meta[1]) * share, share)
    own_ref[...] = total_ref[pl.ds(own, share), :]
    send_ref[...] = total_ref[pl.ds(other, share), :].astype(BF16)


def long_kernel(blocks, group_size, meta, *refs):
    cots = refs[:blocks]
    (mid_ref, pre_ref, gated_ref, dlogit_ref, weights, mixes, head,
     g_ref, between_ref, own_ref, send_ref, d_ref, total_ref) = refs[blocks:]
    row_count, channels = cots[0].shape
    slabs = channels // SLAB
    pair = channels // blocks
    wide = max(pair, SLAB)
    first_slab = meta[0] * pair // SLAB

    @pl.when(meta[2] == 0)
    def _():
        for p in range(blocks):
            g_ref[meta[3 + p]] = cots[p][...]

    @pl.when(meta[2] == 1)
    def _():
        for p in range(blocks):
            z = meta[3 + p]
            loss = lax.dot_general(dlogit_ref[z], head[...], (((0,), (1,)), ((), ())), preferred_element_type=F32)
            g_ref[z] = (cots[p][...].astype(F32) + loss).astype(BF16)

    d_ref[blocks:] = jnp.zeros((SPAN,) + d_ref.shape[1:], BF16)

    def dpre(first, count):
        rows = count * row_count
        here = pl.ds(first, count)

        def one(j, carry):
            dgated = nt(g_ref[here].reshape(rows, channels), mixes[1, lanes(j, 2 * SLAB), :])
            for half in range(2):
                slab = j * 2 + half
                column = lanes(slab, 2 * SLAB)
                tanh, sig = gates(pre_ref[here, :, column].reshape(rows, 2 * SLAB))
                d_ref[here, :, column] = gate_grad(tanh, sig, dgated[:, half * SLAB : (half + 1) * SLAB]).reshape(
                    count, row_count, 2 * SLAB
                )
            return carry

        lax.fori_loop(0, slabs // 2, one, 0)

    chunks(blocks, dpre)

    def back(first, count):
        rows = count * row_count
        here = pl.ds(first, count)

        def one(slab, carry):
            total = g_ref[here, :, lanes(slab)].reshape(rows, SLAB).astype(F32)
            for k in range(3):
                later = d_ref[pl.ds(first + k, count), :, lanes(slab, 2 * SLAB)].reshape(rows, 2 * SLAB)
                total = total + nt(later, weights[1, slab, k * SLAB : (k + 1) * SLAB, :])
            between_ref[here, :, lanes(slab)] = total.astype(BF16).reshape(count, row_count, SLAB)
            return carry

        lax.fori_loop(0, slabs, one, 0)

    chunks(blocks, back)
    all_rows = blocks * row_count
    for i in range(wide // SLAB):
        slab = first_slab + i
        here = slice(i * SLAB, (i + 1) * SLAB)
        total_ref[here, :channels] = tn(
            gated_ref[:, :, lanes(slab)].reshape(all_rows, SLAB), g_ref[...].reshape(all_rows, channels)
        )
        taps = [mid_ref[2 - k : 2 - k + blocks, :, lanes(slab)].reshape(all_rows, SLAB) for k in range(3)]
        total_ref[here, channels:] = weight_sums(
            group_size, taps, d_ref[:blocks, :, lanes(slab, 2 * SLAB)].reshape(all_rows, 2 * SLAB)
        )
    split_pair(meta, pair, first_slab * SLAB, total_ref, own_ref, send_ref)


def own_kernel(meta, x_ref, between_ref, weights, mixes, push_ref, sum_ref, ex_ref):
    row_count, channels = sum_ref.shape
    slabs = channels // SLAB
    z = meta[0]

    def one(j, carry):
        dgated = nt(between_ref[z], mixes[0, lanes(j, 2 * SLAB), :])
        for half in range(2):
            slab = j * 2 + half
            taps = [x_ref[z, HALO - k * REACH : HALO - k * REACH + row_count, lanes(slab)] for k in range(3)]
            tanh, sig = gates(conv(taps, weights[0, slab]))
            dpre = gate_grad(tanh, sig, dgated[:, half * SLAB : (half + 1) * SLAB])
            moved = [nt(dpre, weights[0, slab, k * SLAB : (k + 1) * SLAB, :]) for k in range(3)]
            ex_ref[:HALO, :] = jnp.zeros((HALO, SLAB), F32)
            ex_ref[HALO:, :] = between_ref[z, :, lanes(slab)].astype(F32) + moved[0]
            for k in range(1, 3):
                ex_ref[HALO - k * REACH : HALO - k * REACH + row_count, :] += moved[k]
            push_ref[:, lanes(slab)] = ex_ref[:HALO, :].astype(BF16)
            sum_ref[:, lanes(slab)] = ex_ref[HALO:, :]
        return carry

    lax.fori_loop(0, slabs // 2, one, 0)


def short_kernel(blocks, group_size, meta, x_ref, between_ref, weights, mixes, own_ref, send_ref, total_ref):
    row_count, channels = between_ref.shape[1:]
    pair = channels // blocks
    wide = max(pair, SLAB)
    first_slab = meta[0] * pair // SLAB
    rows = blocks * row_count
    between = between_ref[...].reshape(rows, channels)
    for i in range(wide // SLAB):
        slab = first_slab + i
        here = slice(i * SLAB, (i + 1) * SLAB)
        taps = [
            x_ref[:blocks, HALO - k * REACH : HALO - k * REACH + row_count, lanes(slab)].reshape(rows, SLAB)
            for k in range(3)
        ]
        tanh, sig = gates(conv(taps, weights[0, slab]))
        dpre = gate_grad(tanh, sig, nt(between, mixes[0, lanes(slab), :]))
        total_ref[here, :channels] = tn((tanh * sig).astype(BF16), between)
        total_ref[here, channels:] = weight_sums(group_size, taps, dpre)
    split_pair(meta, pair, first_slab * SLAB, total_ref, own_ref, send_ref)


def finish_kernel(group_size, own0, own1, got0, got1, mix_ref, conv_ref):
    channels = mix_ref.shape[2]
    width = 2 * group_size
    for layer, (own, got) in enumerate(((own0, got0), (own1, got1))):
        total = own[...] + got[...].astype(F32)
        mix_ref[:, layer, :] = total[:, :channels]
        for k in range(3):
            conv_ref[layer, k] = total[:, channels + width * k : channels + width * (k + 1)]


VMEM = pl.BlockSpec(memory_space=pltpu.VMEM)
SMEM = pl.BlockSpec(memory_space=pltpu.SMEM)


def call(kernel, outs, scalars, arrays, scratch=(), name=None, flops=10**8):
    return pl.pallas_call(
        kernel,
        out_shape=[jax.ShapeDtypeStruct(shape, kind) for shape, kind in outs],
        in_specs=[SMEM] * len(scalars) + [VMEM] * len(arrays),
        out_specs=[VMEM] * len(outs),
        scratch_shapes=[pltpu.VMEM(shape, kind) for shape, kind in scratch],
        compiler_params=pltpu.CompilerParams(vmem_limit_bytes=56 * 1024 * 1024),
        cost_estimate=pl.CostEstimate(
            flops=flops, bytes_accessed=sum(a.size * a.dtype.itemsize for a in arrays), transcendentals=0
        ),
        name=name,
    )(*scalars, *arrays)


def body(saved_section_input, out_cot, kernel_weight, blend_weight, hazard_head, labels, events):
    first_input, cot = saved_section_input[0], out_cot[0]
    row_count, channels = first_input.shape
    seq = lax.axis_size("seq")
    blocks = seq // SPAN
    groups, group_size = kernel_weight.shape[3:5]
    slabs = channels // SLAB
    share = channels // seq

    ring = [0] + list(range(1, blocks, 2)) + [b for b in range(blocks - 1, 0, -1) if b % 2 == 0]
    hops = list(zip(ring, ring[1:] + ring[:1]))
    before = {target: source for source, target in hops}
    order = []
    for z in range(blocks):
        arrivals = [z]
        for _ in range(blocks - 1):
            arrivals.append(before[arrivals[-1]])
        order.append(arrivals)

    def step(value):
        return lax.ppermute(
            value, "seq", [(a * SPAN + y, b * SPAN + y) for a, b in hops for y in range(SPAN)]
        )

    def swap(value):
        return lax.ppermute(value, "seq", [(b, b + 1 - 2 * (b % 2)) for b in range(seq)])

    place = lax.axis_index("seq")
    section = lax.axis_index("section")
    is_last = section == lax.axis_size("section") - 1
    z = place // SPAN
    meta = jnp.concatenate(
        [jnp.stack([z, place % SPAN, is_last.astype(jnp.int32)]).astype(jnp.int32), jnp.asarray(order, jnp.int32)[z]]
    )

    inputs, cots = [first_input], [cot]
    tails = [swap(first_input[row_count - HALO :])]
    for _ in range(blocks - 1):
        inputs.append(step(inputs[-1]))
        cots.append(step(cots[-1]))
        tails.append(swap(inputs[-1][row_count - HALO :]))
    codes = lax.all_gather(jnp.stack([labels, events]), "seq")

    (weights,) = call(
        functools.partial(weight_kernel, group_size),
        [((2, slabs, 3 * SLAB, 2 * SLAB), BF16)],
        [],
        [kernel_weight[0].reshape(-1, 2 * group_size)],
        name="weights",
    )
    mixes = blend_weight[0]
    x, mid, pre, gated, dlogit = call(
        functools.partial(forward_kernel, blocks),
        [
            ((blocks + 1, HALO + row_count, channels), BF16),
            ((blocks + SPAN, row_count, channels), BF16),
            ((blocks, row_count, 2 * channels), BF16),
            ((blocks, row_count, channels), BF16),
            ((blocks, hazard_head.shape[1], row_count), BF16),
        ],
        [meta],
        [*inputs, *tails, codes, weights, mixes, hazard_head],
        [((min(blocks, 4) * row_count, channels), BF16)],
        name="forward",
        flops=10**10,
    )
    sums = ((share, channels + SLAB), F32)
    sent = ((share, channels + SLAB), BF16)
    total = ((max(channels // blocks, SLAB), channels + SLAB), F32)
    g, between, own1, send1 = call(
        functools.partial(long_kernel, blocks, group_size),
        [((blocks, row_count, channels), BF16), ((blocks, row_count, channels), BF16), sums, sent],
        [meta],
        [*cots, mid, pre, gated, dlogit, weights, mixes, hazard_head],
        [((blocks + SPAN, row_count, 2 * channels), BF16), total],
        name="long_backward",
        flops=10**10,
    )
    got1 = swap(send1)
    push, own_sum = call(
        own_kernel,
        [((HALO, channels), BF16), ((row_count, channels), F32)],
        [meta],
        [x, between, weights, mixes],
        [((HALO + row_count, SLAB), F32)],
        name="own_backward",
        flops=10**9,
    )
    pushed = lax.ppermute(push, "seq", [(b, b - 1) for b in range(1, seq)])
    own0, send0 = call(
        functools.partial(short_kernel, blocks, group_size),
        [sums, sent],
        [meta],
        [x, between, weights, mixes],
        [total],
        name="short_backward",
        flops=10**9,
    )
    got0 = swap(send0)
    input_gradient = jnp.concatenate(
        [own_sum[: row_count - HALO], own_sum[row_count - HALO :] + pushed.astype(F32)], axis=0
    ).astype(BF16)
    count = lax.axis_size("section")
    received = lax.ppermute(input_gradient, "section", [(s, s - 1) for s in range(1, count)])
    next_cot = jnp.where(is_last, lax.dynamic_index_in_dim(g, z, keepdims=False), received)
    mix_share, conv_share = call(
        functools.partial(finish_kernel, group_size),
        [((share, 2, channels), F32), ((2, 3, share, 2 * group_size), F32)],
        [],
        [own0, own1, got0, got1],
        name="finish",
    )
    conv_share = conv_share.reshape(2, 3, share // group_size, group_size, 2 * group_size)
    return (input_gradient[None], next_cot[None], mix_share[None], conv_share[None])


def solution(mesh):
    return jax.shard_map(
        body,
        mesh=mesh,
        in_specs=(
            P("section", "seq", None),
            P("section", "seq", None),
            P("section", None, None, None, None, None),
            P("section", None, None, None),
            P(),
            P("seq"),
            P("seq"),
        ),
        out_specs=(
            P("section", "seq", None),
            P("section", "seq", None),
            P("section", "seq", None, None),
            P("section", None, None, "seq", None, None),
        ),
        check_vma=False,
    )
```

time: 365 us -> 130 us (0.36)
  waiting for transfers between devices: 273 us -> 18.3 us
  Pallas kernels: 0 us -> 54.5 us
  matrix products: 25.8 us -> 0 us
  blocking collectives: 0 us -> 17.3 us
  between operations: 14.7 us -> 0.8 us
  local copies, waits for them, and re-layouts: 21.2 us -> 9.57 us
  other arithmetic: 9.26 us -> 3.8 us
  starting transfers between devices: 20.4 us -> 24.6 us
    reduce_scatter x1 -> x0, waiting for transfers between devices: 152 us -> none  [body(): lax.psum_scatter(jnp.stack([jnp.dot(gated_short.T, between_gradient, pref...]
    ppermute x7 -> x14, waiting for transfers between devices: 95.5 us -> 18.3 us  [the longest x6 15 us: step(): lax.ppermute(value, 'seq', [(a * SPAN + y, b * SPAN + y) for a, b in hops...]
    pallas_call x0 -> x6, Pallas kernels: none -> 54.5 us  [call(): pl.pallas_call(kernel, out_shape=[jax.ShapeDtypeStruct(shape, kind) for s...]
    dot_general x25 -> x0, matrix products: 25.8 us -> none  [the longest x6 7.99 us: weight_terms(): jnp.einsum('rgi,rgo->gio', tap.reshape(row_count, groups, group_size).ast...]
    unnamed x3 -> x0, waiting for transfers between devices: 25.2 us -> none
    all_gather x0 -> x1, blocking collectives: none -> 17.3 us  [body(): codes = lax.all_gather(jnp.stack([labels, events]), 'seq')]
    unnamed x64 -> x28, local copies, waits for them, and re-layouts: 11.6 us -> 6.93 us
    another operation x3 -> x1, other arithmetic: 4.53 us -> 0.02 us  [the longest x1 4.13 us: body(): jnp.stack([jnp.dot(gated_short.T, between_gradient, preferred_element_typ...]
  transfers between devices with their start and end apart: 9 -> 14, of which waited for: 7 -> 7; matrix products, arithmetic and copies ran while one was open for 7% -> 7% of each run, Pallas kernels for 0% -> 32%
where the time goes in v1:
time: 130 us; the launch traced here: 129 us
  Pallas kernels  54.5 us (42%)
  starting transfers between devices  24.6 us (19%)
  waiting for transfers between devices  18.3 us (14%)
  blocking collectives  17.3 us (13%)
  local copies, waits for them, and re-layouts  9.57 us (7%)
  other arithmetic  3.8 us (3%)
    pallas_call x6, Pallas kernels, call(): pl.pallas_call(kernel, out_shape=[jax.ShapeDtypeStruct(shape, kind) for s...  54.5 us
    all_gather x1, blocking collectives, body(): codes = lax.all_gather(jnp.stack([labels, events]), 'seq')  17.3 us
    ppermute x6, waiting for transfers between devices, step(): lax.ppermute(value, 'seq', [(a * SPAN + y, b * SPAN + y) for a, b in hops...  15 us
    ppermute x1, starting transfers between devices, body(): lax.ppermute(input_gradient, 'section', [(s, s - 1) for s in range(1, cou...  12.3 us
    unnamed x28, local copies, waits for them, and re-layouts  6.93 us
    ppermute x6, starting transfers between devices, step(): lax.ppermute(value, 'seq', [(a * SPAN + y, b * SPAN + y) for a, b in hops...  5.54 us
    ppermute x6, starting transfers between devices, swap(): lax.ppermute(value, 'seq', [(b, b + 1 - 2 * (b % 2)) for b in range(seq)])  5.48 us
  transfers between devices with their start and end apart: 14, of which 7 were waited for; matrix products, arithmetic and copies ran while one was open for 7% of the time, Pallas kernels for 32%

profile of v1, /device:TPU:1, one launch (start us, length us, event | category | flops | bytes accessed | tf_op | source)
XLA Modules:
  0.0 128.9 jit_solution(8376196445183287517)
XLA Ops:
  0.6 2.2 %collective-permute-start = (bf16[128,1024]{1,0:T(8,128)(2,1)}, bf16[128,1024]{1,0:T(8,128)(2,1)S(1)}, u32[]{:S(2)}, u32[]{:S(2)}) collective-permute-start(bf16[128,1024]{1,0:T(8,128)(2,1)} %bitcast.32), channel_id=1, source_target_pairs={{0,2},{1,3},{2,6},{3,7},{6,4},{7,5},{4,0},{5,1},{8,10},{9,11},{10,... | collective-permute-start | bytes 786440 | tf_op jit(solution)/shard_map/ppermute | solution.py:356
  2.8 7.3 %collective-permute-done.refs_1_ = bf16[128,1024]{1,0:T(8,128)(2,1)S(1)} collective-permute-done((bf16[128,1024]{1,0:T(8,128)(2,1)}, bf16[128,1024]{1,0:T(8,128)(2,1)S(1)}, u32[]{:S(2)}, u32[]{:S(2)}) %collective-permute-start) | collective-permute-done | bytes 262176 | tf_op jit(solution)/shard_map/ppermute | solution.py:356
  10.1 0.3 collective-permute-start.1
  10.4 3.0 %collective-permute-start.7 = (bf16[128,1024]{1,0:T(8,128)(2,1)}, bf16[128,1024]{1,0:T(8,128)(2,1)S(1)}, u32[]{:S(2)}, u32[]{:S(2)}) collective-permute-start(bf16[128,1024]{1,0:T(8,128)(2,1)} %bitcast.38), channel_id=1, source_target_pairs={{0,2},{1,3},{2,6},{3,7},{6,4},{7,5},{4,0},{5,1},{8,10},{9,11},{10,... | collective-permute-start | bytes 786440 | tf_op jit(solution)/shard_map/ppermute | solution.py:356
  13.4 4.1 %collective-permute-done.1.refs_2_ = bf16[128,1024]{1,0:T(8,128)(2,1)S(1)} collective-permute-done((bf16[128,1024]{1,0:T(8,128)(2,1)S(1)}, bf16[128,1024]{1,0:T(8,128)(2,1)S(1)}, u32[]{:S(2)}, u32[]{:S(2)}) %collective-permute-start.1) | collective-permute-done | bytes 262176 | tf_op jit(solution)/shard_map/ppermute | solution.py:356
  17.5 0.0 collective-permute-start.2
  17.5 0.9 slice_bitcast_fusion
  18.4 1.1 collective-permute-start.3
  19.5 3.6 %collective-permute-done.7.refs_1_ = bf16[128,1024]{1,0:T(8,128)(2,1)S(1)} collective-permute-done((bf16[128,1024]{1,0:T(8,128)(2,1)}, bf16[128,1024]{1,0:T(8,128)(2,1)S(1)}, u32[]{:S(2)}, u32[]{:S(2)}) %collective-permute-start.7) | collective-permute-done | bytes 262176 | tf_op jit(solution)/shard_map/ppermute | solution.py:356
  23.2 0.0 collective-permute-start.8
  23.2 0.8 add_bitcast_fusion
  24.0 1.7 %copy.16.refs_11_.refs_10_ = bf16[1024,64]{1,0:T(8,128)(2,1)} copy(bf16[1024,64]{0,1:T(8,128)(2,1)} %param.12) | data formatting | bytes 262144 | tf_op args[4]
  25.7 3.0 %copy.15 = bf16[1,2,3,64,16,32]{5,4,3,2,1,0:T(8,128)(2,1)} copy(bf16[1,2,3,64,16,32]{3,5,4,2,1,0:T(8,128)(2,1)} %param.10) | data formatting | bytes 786432 | tf_op args[2]
  28.7 17.3 %all-gather.1.refs_8_ = s32[8,2,128]{2,1,0:T(2,128)} all-gather(s32[1,2,128]{2,1,0:T(2,128)S(1)} %add_bitcast_fusion), channel_id=2, replica_groups=mesh['section'=4,'seq'=8] {'seq'}, dimensions={0}, use_global_device_ids=true | all-gather | bytes 9216 | tf_op jit(solution)/shard_map/all_gather | solution.py:377
  46.0 9.5 %weights.1.refs_9_.refs_8_ = bf16[2,8,384,256]{3,2,1,0:T(8,128)(2,1)} custom-call(bf16[6144,32]{1,0:T(8,128)(2,1)} %bitcast.30), custom_call_target="tpu_custom_call" | custom-call | flops 100000000 | bytes 393216 | tf_op jit(solution)/shard_map/weights/pallas_call | solution.py:322
  55.6 0.7 dynamic-slice_bitcast_fusion
  56.3 0.1 collective-permute-start.4
  56.4 1.5 %collective-permute-start.5 = (bf16[32,1024]{1,0:T(8,128)(2,1)S(1)}, bf16[32,1024]{1,0:T(8,128)(2,1)S(1)}, u32[]{:S(2)}, u32[]{:S(2)}) collective-permute-start(bf16[32,1024]{1,0:T(8,128)(2,1)S(1)} %slice.29), channel_id=1, source_target_pairs={{0,1},{1,0},{2,3},{3,2},{4,5},{5,4},{6,7},{7,6},{8,9},{9,8},{10,11... | collective-permute-start | bytes 196616 | tf_op jit(solution)/shard_map/ppermute | solution.py:361
  57.9 0.0 collective-permute-done.2.refs_3_
  57.9 0.1 collective-permute-start.6
  58.0 0.6 pad_add_fusion.meta
  58.6 0.0 collective-permute-done.8.refs_2_
  58.6 0.0 collective-permute-start.9
  58.6 0.0 collective-permute-done.3.refs_4_
  58.6 0.8 collective-permute-done.4.refs_5_
  59.4 0.7 collective-permute-done.5.refs_6_
  60.1 0.9 collective-permute-done.6.refs_7_
  61.1 0.6 copy-done.12
  61.7 13.1 %forward.1 = (bf16[5,160,1024]{2,1,0:T(8,128)(2,1)}, bf16[6,128,1024]{2,1,0:T(8,128)(2,1)}, bf16[4,128,2048]{2,1,0:T(8,128)(2,1)}, bf16[4,128,1024]{2,1,0:T(8,128)(2,1)}, bf16[4,64,128]{2,1,0:T(8,128)(2,1)}) custom-call(s32[7]{0:T(128)} %pad_add_fusion.meta, bf16[128,1024]{1,0:T(8,128)(2,1)} %bitcast.33, bf16[128,1024]{1,0:T(8,128)(2,1)} %copy-done.3, ...), custom_call_target="tpu_custom_call" | custom-call | flops 10000000000 | bytes 8790016 | tf_op jit(solution)/shard_map/forward/pallas_call | solution.py:322
  74.8 0.0 collective-permute-done.9.refs_3_
  74.8 0.0 copy-start.8
  74.8 0.7 copy-done.8
  75.5 13.0 %long_backward.1 = (bf16[4,128,1024]{2,1,0:T(8,128)(2,1)}, bf16[4,128,1024]{2,1,0:T(8,128)(2,1)}, f32[128,1152]{1,0:T(8,128)}, bf16[128,1152]{1,0:T(8,128)(2,1)}) custom-call(s32[7]{0:T(128)} %pad_add_fusion.meta, bf16[128,1024]{1,0:T(8,128)(2,1)} %bitcast.39, bf16[128,1024]{1,0:T(8,128)(2,1)} %copy-done.6, bf16[128,1024]{1,0:T(8,128)(2,1)} %copy-done.7, ...), custom_call_target="tpu_custom_call" | custom-call | flops 10000000000 | bytes 13303808 | tf_op jit(solution)/shard_map/long_backward/pallas_call | solution.py:322
  88.5 0.6 collective-permute-start.13
  89.2 8.3 %own_backward.1 = (bf16[32,1024]{1,0:T(8,128)(2,1)}, f32[128,1024]{1,0:T(8,128)}) custom-call(s32[7]{0:T(128)} %pad_add_fusion.meta, bf16[5,160,1024]{2,1,0:T(8,128)(2,1)} %get-tuple-element.19.x_ref, bf16[4,128,1024]{2,1,0:T(8,128)(2,1)} %get-tuple-element.24.between_ref, bf16[2,8,384,256]{3,2,1,0:T(8,128)(2,1)} %weights.1.refs_9_.refs_8_, ...), custom_call_target="tpu_custom_call" | custom-call | flops 1000000000 | bytes 10027008 | tf_op jit(solution)/shard_map/own_backward/pallas_call | solution.py:322
  97.4 1.3 collective-permute-start.10
  98.7 1.0 slice.34
  99.8 0.0 copy-start
  99.8 7.8 %short_backward.1 = (f32[128,1152]{1,0:T(8,128)}, bf16[128,1152]{1,0:T(8,128)(2,1)}) custom-call(s32[7]{0:T(128)} %pad_add_fusion.meta, bf16[5,160,1024]{2,1,0:T(8,128)(2,1)} %get-tuple-element.19.x_ref, bf16[4,128,1024]{2,1,0:T(8,128)(2,1)} %get-tuple-element.24.between_ref, bf16[2,8,384,256]{3,2,1,0:T(8,128)(2,1)} %weights.1.refs_9_.refs_8_, ...), custom_call_target="tpu_custom_call" | custom-call | flops 1000000000 | bytes 10027008 | tf_op jit(solution)/shard_map/short_backward/pallas_call | solution.py:322
  107.6 2.1 %collective-permute-start.12 = (bf16[128,1152]{1,0:T(8,128)(2,1)}, bf16[128,1152]{1,0:T(8,128)(2,1)S(1)}, u32[]{:S(2)}, u32[]{:S(2)}) collective-permute-start(bf16[128,1152]{1,0:T(8,128)(2,1)} %get-tuple-element.30), channel_id=1, source_target_pairs={{0,1},{1,0},{2,3},{3,2},{4,5},{5,4},{6,7},{7,6},{8,9},{9,8},{10,11... | collective-permute-start | bytes 884744 | tf_op jit(solution)/shard_map/ppermute | solution.py:361
  109.7 12.3 %collective-permute-start.11 = (bf16[128,1024]{1,0:T(8,128)(2,1)S(1)}, bf16[128,1024]{1,0:T(8,128)(2,1)S(1)}, u32[]{:S(2)}, u32[]{:S(2)}) collective-permute-start(bf16[128,1024]{1,0:T(8,128)(2,1)S(1)} %pad_maximum_fusion.1), channel_id=1, source_target_pairs={{8,0},{16,8},{24,16},{9,1},{17,9},{25,17},{10,2},{18,10},{26,18},{... | collective-permute-start | bytes 786440 | tf_op jit(solution)/shard_map/ppermute | solution.py:439
  122.1 0.7 pad_maximum_fusion
  122.8 0.0 collective-permute-done.13.got1
  122.8 0.7 copy-done.1
  123.6 0.1 copy-done.2
  123.6 2.7 %finish.1 = (f32[128,2,1024]{2,1,0:T(2,128)}, f32[2,3,128,32]{3,2,1,0:T(8,128)}) custom-call(f32[128,1152]{1,0:T(8,128)} %get-tuple-element.28.own0, f32[128,1152]{1,0:T(8,128)} %get-tuple-element.29.own1, bf16[128,1152]{1,0:T(8,128)(2,1)} %copy-done.2, bf16[128,1152]{1,0:T(8,128)(2,1)} %copy-done.1), custom_call_target="tpu_custom_call" | custom-call | flops 100000000 | bytes 1769472 | tf_op jit(solution)/shard_map/finish/pallas_call | solution.py:322
  126.4 0.8 collective-permute-done.11
  127.2 1.7 %fusion = bf16[1,128,1024]{2,1,0:T(8,128)(2,1)} fusion(bf16[128,1024]{1,0:T(8,128)(2,1)S(1)} %collective-permute-done.11, bf16[4,128,1024]{2,1,0:T(8,128)(2,1)} %get-tuple-element.27, s32[]{:T(128)S(6)} %select_n.26, pred[]{:T(512)S(6)} %eq.5), kind=kLoop, calls=%fused_computation.4 | loop fusion | flops 131072 | bytes 786437 | tf_op jit(solution)/shard_map/broadcast_in_dim | solution.py:449
  (28 shorter events, 0.1 us)
Async XLA Ops:
  0.6 9.4 %collective-permute-start = (bf16[128,1024]{1,0:T(8,128)(2,1)}, bf16[128,1024]{1,0:T(8,128)(2,1)S(1)}, u32[]{:S(2)}, u32[]{:S(2)}) collective-permute-start(bf16[128,1024]{1,0:T(8,128)(2,1)} %bitcast.32), channel_id=1, source_target_pairs={{0,2},{1,3},{2,6},{3,7},{6,4},{7,5},{4,0},{5,1},{8,10},{9,11},{10,... | collective-permute-start | bytes 786440 | tf_op jit(solution)/shard_map/ppermute | solution.py:356
  10.1 46.2 %copy-start.3 = (bf16[128,1024]{1,0:T(8,128)(2,1)}, bf16[128,1024]{1,0:T(8,128)(2,1)S(1)}, u32[]{:S(2)}) copy-start(bf16[128,1024]{1,0:T(8,128)(2,1)S(1)} %collective-permute-done.refs_1_) | copy-start | bytes 786436
  10.1 7.5 %collective-permute-start.1 = (bf16[128,1024]{1,0:T(8,128)(2,1)S(1)}, bf16[128,1024]{1,0:T(8,128)(2,1)S(1)}, u32[]{:S(2)}, u32[]{:S(2)}) collective-permute-start(bf16[128,1024]{1,0:T(8,128)(2,1)S(1)} %collective-permute-done.refs_1_), channel_id=1, source_target_pairs={{0,2},{1,3},{2,6},{3,7},{6,4},{7,5},{4,0},{5,1},{8,10},{9,11},{10,... | collective-permute-start | bytes 786440 | tf_op jit(solution)/shard_map/ppermute | solution.py:356
  10.4 12.7 %collective-permute-start.7 = (bf16[128,1024]{1,0:T(8,128)(2,1)}, bf16[128,1024]{1,0:T(8,128)(2,1)S(1)}, u32[]{:S(2)}, u32[]{:S(2)}) collective-permute-start(bf16[128,1024]{1,0:T(8,128)(2,1)} %bitcast.38), channel_id=1, source_target_pairs={{0,2},{1,3},{2,6},{3,7},{6,4},{7,5},{4,0},{5,1},{8,10},{9,11},{10,... | collective-permute-start | bytes 786440 | tf_op jit(solution)/shard_map/ppermute | solution.py:356
  17.5 38.8 %copy-start.4 = (bf16[128,1024]{1,0:T(8,128)(2,1)}, bf16[128,1024]{1,0:T(8,128)(2,1)S(1)}, u32[]{:S(2)}) copy-start(bf16[128,1024]{1,0:T(8,128)(2,1)S(1)} %collective-permute-done.1.refs_2_) | copy-start | bytes 786436
  17.5 40.3 %collective-permute-start.2 = (bf16[128,1024]{1,0:T(8,128)(2,1)S(1)}, bf16[128,1024]{1,0:T(8,128)(2,1)S(1)}, u32[]{:S(2)}, u32[]{:S(2)}) collective-permute-start(bf16[128,1024]{1,0:T(8,128)(2,1)S(1)} %collective-permute-done.1.refs_2_), channel_id=1, source_target_pairs={{0,2},{1,3},{2,6},{3,7},{6,4},{7,5},{4,0},{5,1},{8,10},{9,11},{10,... | collective-permute-start | bytes 786440 | tf_op jit(solution)/shard_map/ppermute | solution.py:356
  18.4 40.1 %collective-permute-start.3 = (bf16[32,1024]{1,0:T(8,128)(2,1)S(1)}, bf16[32,1024]{1,0:T(8,128)(2,1)S(1)}, u32[]{:S(2)}, u32[]{:S(2)}) collective-permute-start(bf16[32,1024]{1,0:T(8,128)(2,1)S(1)} %slice_bitcast_fusion), channel_id=1, source_target_pairs={{0,1},{1,0},{2,3},{3,2},{4,5},{5,4},{6,7},{7,6},{8,9},{9,8},{10,11... | collective-permute-start | bytes 196616 | tf_op jit(solution)/shard_map/ppermute | solution.py:361
  23.2 32.4 %copy-start.6 = (bf16[128,1024]{1,0:T(8,128)(2,1)}, bf16[128,1024]{1,0:T(8,128)(2,1)S(1)}, u32[]{:S(2)}) copy-start(bf16[128,1024]{1,0:T(8,128)(2,1)S(1)} %collective-permute-done.7.refs_1_) | copy-start | bytes 786436
  23.2 35.4 %collective-permute-start.8 = (bf16[128,1024]{1,0:T(8,128)(2,1)S(1)}, bf16[128,1024]{1,0:T(8,128)(2,1)S(1)}, u32[]{:S(2)}, u32[]{:S(2)}) collective-permute-start(bf16[128,1024]{1,0:T(8,128)(2,1)S(1)} %collective-permute-done.7.refs_1_), channel_id=1, source_target_pairs={{0,2},{1,3},{2,6},{3,7},{6,4},{7,5},{4,0},{5,1},{8,10},{9,11},{10,... | collective-permute-start | bytes 786440 | tf_op jit(solution)/shard_map/ppermute | solution.py:356
  56.3 3.2 %collective-permute-start.4 = (bf16[32,1024]{1,0:T(8,128)(2,1)S(1)}, bf16[32,1024]{1,0:T(8,128)(2,1)S(1)}, u32[]{:S(2)}, u32[]{:S(2)}) collective-permute-start(bf16[32,1024]{1,0:T(8,128)(2,1)S(1)} %slice.28), channel_id=1, source_target_pairs={{0,1},{1,0},{2,3},{3,2},{4,5},{5,4},{6,7},{7,6},{8,9},{9,8},{10,11... | collective-permute-start | bytes 196616 | tf_op jit(solution)/shard_map/ppermute | solution.py:361
  56.4 3.8 %collective-permute-start.5 = (bf16[32,1024]{1,0:T(8,128)(2,1)S(1)}, bf16[32,1024]{1,0:T(8,128)(2,1)S(1)}, u32[]{:S(2)}, u32[]{:S(2)}) collective-permute-start(bf16[32,1024]{1,0:T(8,128)(2,1)S(1)} %slice.29), channel_id=1, source_target_pairs={{0,1},{1,0},{2,3},{3,2},{4,5},{5,4},{6,7},{7,6},{8,9},{9,8},{10,11... | collective-permute-start | bytes 196616 | tf_op jit(solution)/shard_map/ppermute | solution.py:361
  57.9 3.2 %copy-start.5 = (bf16[128,1024]{1,0:T(8,128)(2,1)}, bf16[128,1024]{1,0:T(8,128)(2,1)S(1)}, u32[]{:S(2)}) copy-start(bf16[128,1024]{1,0:T(8,128)(2,1)S(1)} %collective-permute-done.2.refs_3_) | copy-start | bytes 786436
  57.9 3.2 %collective-permute-start.6 = (bf16[32,1024]{1,0:T(8,128)(2,1)S(1)}, bf16[32,1024]{1,0:T(8,128)(2,1)S(1)}, u32[]{:S(2)}, u32[]{:S(2)}) collective-permute-start(bf16[32,1024]{1,0:T(8,128)(2,1)S(1)} %slice.30), channel_id=1, source_target_pairs={{0,1},{1,0},{2,3},{3,2},{4,5},{5,4},{6,7},{7,6},{8,9},{9,8},{10,11... | collective-permute-start | bytes 196616 | tf_op jit(solution)/shard_map/ppermute | solution.py:361
  58.6 16.2 %copy-start.7 = (bf16[128,1024]{1,0:T(8,128)(2,1)}, bf16[128,1024]{1,0:T(8,128)(2,1)S(1)}, u32[]{:S(2)}) copy-start(bf16[128,1024]{1,0:T(8,128)(2,1)S(1)} %collective-permute-done.8.refs_2_) | copy-start | bytes 786436
  58.6 16.2 %collective-permute-start.9 = (bf16[128,1024]{1,0:T(8,128)(2,1)S(1)}, bf16[128,1024]{1,0:T(8,128)(2,1)S(1)}, u32[]{:S(2)}, u32[]{:S(2)}) collective-permute-start(bf16[128,1024]{1,0:T(8,128)(2,1)S(1)} %collective-permute-done.8.refs_2_), channel_id=1, source_target_pairs={{0,2},{1,3},{2,6},{3,7},{6,4},{7,5},{4,0},{5,1},{8,10},{9,11},{10,... | collective-permute-start | bytes 786440 | tf_op jit(solution)/shard_map/ppermute | solution.py:356
  58.6 2.5 %copy-start.9 = (bf16[32,1024]{1,0:T(8,128)(2,1)}, bf16[32,1024]{1,0:T(8,128)(2,1)S(1)}, u32[]{:S(2)}) copy-start(bf16[32,1024]{1,0:T(8,128)(2,1)S(1)} %collective-permute-done.3.refs_4_) | copy-start | bytes 196612
  59.4 1.6 %copy-start.10 = (bf16[32,1024]{1,0:T(8,128)(2,1)}, bf16[32,1024]{1,0:T(8,128)(2,1)S(1)}, u32[]{:S(2)}) copy-start(bf16[32,1024]{1,0:T(8,128)(2,1)S(1)} %collective-permute-done.4.refs_5_) | copy-start | bytes 196612
  60.1 0.9 copy-start.11
  61.1 0.6 copy-start.12
  74.8 0.7 copy-start.8
  88.5 34.2 %collective-permute-start.13 = (bf16[128,1152]{1,0:T(8,128)(2,1)}, bf16[128,1152]{1,0:T(8,128)(2,1)S(1)}, u32[]{:S(2)}, u32[]{:S(2)}) collective-permute-start(bf16[128,1152]{1,0:T(8,128)(2,1)} %get-tuple-element.31), channel_id=1, source_target_pairs={{0,1},{1,0},{2,3},{3,2},{4,5},{5,4},{6,7},{7,6},{8,9},{9,8},{10,11... | collective-permute-start | bytes 884744 | tf_op jit(solution)/shard_map/ppermute | solution.py:361
  97.4 12.2 %collective-permute-start.10 = (bf16[32,1024]{1,0:T(8,128)(2,1)}, bf16[32,1024]{1,0:T(8,128)(2,1)S(1)}, u32[]{:S(2)}, u32[]{:S(2)}) collective-permute-start(bf16[32,1024]{1,0:T(8,128)(2,1)} %get-tuple-element.26), channel_id=1, source_target_pairs={{1,0},{2,1},{3,2},{4,3},{5,4},{6,5},{7,6},{9,8},{10,9},{11,10},{12... | collective-permute-start | bytes 196616 | tf_op jit(solution)/shard_map/ppermute | solution.py:424
  99.8 9.9 %copy-start = (f32[128,1024]{1,0:T(8,128)S(1)}, f32[128,1024]{1,0:T(8,128)}, u32[]{:S(2)}) copy-start(f32[128,1024]{1,0:T(8,128)} %get-tuple-element.25) | copy-start | bytes 1572868
  107.6 15.2 %collective-permute-start.12 = (bf16[128,1152]{1,0:T(8,128)(2,1)}, bf16[128,1152]{1,0:T(8,128)(2,1)S(1)}, u32[]{:S(2)}, u32[]{:S(2)}) collective-permute-start(bf16[128,1152]{1,0:T(8,128)(2,1)} %get-tuple-element.30), channel_id=1, source_target_pairs={{0,1},{1,0},{2,3},{3,2},{4,5},{5,4},{6,7},{7,6},{8,9},{9,8},{10,11... | collective-permute-start | bytes 884744 | tf_op jit(solution)/shard_map/ppermute | solution.py:361
  109.7 17.5 %collective-permute-start.11 = (bf16[128,1024]{1,0:T(8,128)(2,1)S(1)}, bf16[128,1024]{1,0:T(8,128)(2,1)S(1)}, u32[]{:S(2)}, u32[]{:S(2)}) collective-permute-start(bf16[128,1024]{1,0:T(8,128)(2,1)S(1)} %pad_maximum_fusion.1), channel_id=1, source_target_pairs={{8,0},{16,8},{24,16},{9,1},{17,9},{25,17},{10,2},{18,10},{26,18},{... | collective-permute-start | bytes 786440 | tf_op jit(solution)/shard_map/ppermute | solution.py:439
  122.8 0.8 copy-start.1
  122.8 0.8 copy-start.2

commit v2 on v1

v2 whole, which is shorter than its diff:
```python
import functools

import jax
import jax.numpy as jnp
from jax import lax
from jax.experimental import pallas as pl
from jax.experimental.pallas import tpu as pltpu
from jax.sharding import PartitionSpec as P

SPAN = 2
SLAB = 128
F32 = jnp.float32
BF16 = jnp.bfloat16
HALO = 32
REACH = 16


def nn(a, b):
    return lax.dot_general(a, b, (((1,), (0,)), ((), ())), preferred_element_type=F32)


def nt(a, b):
    return lax.dot_general(a, b, (((1,), (1,)), ((), ())), preferred_element_type=F32)


def tn(a, b, precision=None):
    return lax.dot_general(a, b, (((0,), (0,)), ((), ())), preferred_element_type=F32, precision=precision)


def sigmoid(x):
    return 0.5 * jnp.tanh(0.5 * x) + 0.5


def lanes(slab, width=SLAB):
    return pl.ds(pl.multiple_of(slab * width, width), width)


def same_group(group_size):
    rows = lax.broadcasted_iota(jnp.int32, (SLAB, 2 * SLAB), 0) // group_size
    columns = lax.broadcasted_iota(jnp.int32, (SLAB, 2 * SLAB), 1) % SLAB // group_size
    return rows == columns


def spread(group_size, shift, width):
    o = lax.broadcasted_iota(jnp.int32, (width, 2 * SLAB), 0) - shift
    column = lax.broadcasted_iota(jnp.int32, (width, 2 * SLAB), 1)
    return (o == column % group_size + jnp.where(column >= SLAB, group_size, 0)).astype(F32)


def conv(taps, weight):
    return nn(jnp.concatenate(taps, axis=1), weight).astype(BF16)


def gates(pre):
    pre = pre.astype(F32)
    return jnp.tanh(pre[:, :SLAB]), sigmoid(pre[:, SLAB:])


def gate_grad(tanh, sig, dgated):
    one = dgated * sig
    return jnp.concatenate(
        [(one * (1.0 - tanh * tanh)).astype(BF16), (one * tanh * (1.0 - sig)).astype(BF16)], axis=1
    )


def cut(slab, width=SLAB):
    return slice(slab * width, (slab + 1) * width)


def chunks(blocks, step):
    some = min(blocks, 4)
    if some == blocks:
        step(0, blocks)
    else:
        pl.loop(0, blocks // some)(lambda i: step(i * some, some))


def ring_place(index, blocks):
    return jnp.where(index <= blocks // 2, jnp.maximum(2 * index - 1, 0), 2 * (blocks - index))


def arrival(p, blocks):
    z = lax.axis_index("seq") // SPAN
    place = jnp.where(z % 2 == 1, (z + 1) // 2, jnp.where(z == 0, 0, blocks - z // 2))
    return ring_place(lax.rem(place - p + blocks, blocks), blocks)


def on_last_section():
    return lax.axis_index("section") == lax.axis_size("section") - 1


def start_copies(pairs, sems, first=0):
    copies = [pltpu.make_async_copy(source, target, sems.at[first + i]) for i, (source, target) in enumerate(pairs)]
    for copy in copies:
        copy.start()
    return copies


def finish_copies(copies):
    for copy in copies:
        copy.wait()


def weight_kernel(group_size, w_ref, out_ref, fold_ref):
    layers, slabs = out_ref.shape[:2]
    rows = slabs * SLAB
    one_hot = spread(group_size, 0, 2 * group_size).astype(BF16)
    keep = same_group(group_size)
    for layer in range(layers):
        for k in range(3):
            tiled = nn(w_ref[(layer * 3 + k) * rows : (layer * 3 + k + 1) * rows, :], one_hot)
            for slab in range(slabs):
                out_ref[layer, slab, cut(k), :] = jnp.where(keep, tiled[cut(slab)], 0.0).astype(BF16)
    for k in range(3):
        fold_ref[:, cut(k, 2 * SLAB)] = spread(group_size, 2 * group_size * k, SLAB).astype(BF16)


def tail_kernel(value, out_ref):
    out_ref[...] = value[value.shape[0] - HALO :, :]


def forward_kernel(blocks, *refs):
    inputs, tails, codes = refs[:blocks], refs[blocks : 2 * blocks], refs[2 * blocks : 3 * blocks]
    (far_weights, far_mixes, far_head, x_ref, mid_ref, pre_ref, dlogit_ref, weights, mixes, head,
     gated_ref, code_ref, sems) = refs[3 * blocks :]
    row_count, channels = inputs[0].shape
    slabs = channels // SLAB
    y = lax.axis_index("seq") % SPAN
    rows_in = []
    for p in range(blocks):
        z = arrival(p, blocks)
        rows_in.append((inputs[p], x_ref.at[z, pl.ds(HALO, row_count)]))
        rows_in.append((tails[p], x_ref.at[z + 1 - y, pl.ds(0, HALO)]))
    rows_in = start_copies(rows_in, sems)
    held = [(far_weights.at[0], weights.at[0]), (far_mixes.at[0], mixes.at[0]), (far_weights.at[1], weights.at[1])]
    held = start_copies(held + [(far_mixes.at[1], mixes.at[1]), (far_head, head)], sems, 2 * blocks)
    for p in range(blocks):
        code_ref[arrival(p, blocks)] = codes[p][...]
    mid_ref[0:SPAN] = jnp.zeros((SPAN, row_count, channels), BF16)

    @pl.when(y == 0)
    def _():
        x_ref[0, :HALO, :] = jnp.zeros((HALO, channels), BF16)

    finish_copies(rows_in + held[:1])

    def gate(first, count, layer, tap):
        for slab in range(slabs):
            for i in range(count):
                pre = conv([tap(first + i, k, cut(slab)) for k in range(3)], weights[layer, slab])
                if layer:
                    pre_ref[first + i, :, cut(slab, 2 * SLAB)] = pre
                tanh, sig = gates(pre)
                gated_ref[i * row_count : (i + 1) * row_count, cut(slab)] = (tanh * sig).astype(BF16)

    def short_tap(z, k, column):
        return x_ref[z, HALO - k * REACH : HALO - k * REACH + row_count, column]

    def short(first, count):
        gate(first, count, 0, short_tap)
        if count == blocks:
            finish_copies(held[1:2])
        mixed = nn(gated_ref[...], mixes[0]).reshape(count, row_count, channels)
        here = pl.ds(first, count)
        mid_ref[pl.ds(first + SPAN, count)] = (x_ref[here, HALO:, :].astype(F32) + mixed).astype(BF16)

    if blocks > 4:
        finish_copies(held[1:2])
    chunks(blocks, short)
    finish_copies(held[2:])

    def long_tap(z, k, column):
        return mid_ref[z + SPAN - k, :, column]

    def long(first, count):
        gate(first, count, 1, long_tap)

        @pl.when(on_last_section())
        def _():
            for i in range(count):
                z = first + i
                here = slice(i * row_count, (i + 1) * row_count)
                top = (mid_ref[z + SPAN].astype(F32) + nn(gated_ref[here, :], mixes[1])).astype(BF16)
                logits = nt(head[...], top)
                bins = lax.broadcasted_iota(jnp.int32, logits.shape, 0)
                label, event = code_ref[z, 0:1, :], code_ref[z, 1:2, :].astype(F32)
                dlogit = jnp.where(bins <= label, jax.nn.sigmoid(logits), 0.0) - jnp.where(bins == label, event, 0.0)
                dlogit_ref[z] = dlogit.astype(BF16)

    chunks(blocks, long)


def weight_sums(group_size, taps, dpre, fold):
    keep = same_group(group_size)
    product = jnp.concatenate([jnp.where(keep, tn(tap, dpre), 0.0) for tap in taps], axis=1)
    high = product.astype(BF16)
    low = (product - high.astype(F32)).astype(BF16)
    return nt(high, fold) + nt(low, fold)


def pair_slabs(channels, blocks):
    pair = channels // blocks
    return pair, max(pair, SLAB) // SLAB, lax.axis_index("seq") // SPAN * pair // SLAB


def split_pair(pair, total_ref, own_ref, send_ref):
    share = pair // SPAN
    place = lax.axis_index("seq")
    begin = place // SPAN * pair % SLAB if pair < SLAB else 0
    own = pl.multiple_of(begin + place % SPAN * share, share)
    other = pl.multiple_of(begin + (1 - place % SPAN) * share, share)
    own_ref[...] = total_ref[pl.ds(own, share), :]
    send_ref[...] = total_ref[pl.ds(other, share), :].astype(BF16)


def add_loss(z, dlogit_ref, head, g_ref):
    @pl.when(on_last_section())
    def _():
        g_ref[z] = (g_ref[z].astype(F32) + tn(dlogit_ref[z], head[...])).astype(BF16)


def gate_cotangent(z, g_ref, pre_ref, mixes, d_ref):
    for j in range(g_ref.shape[2] // SLAB // 2):
        dgated = nt(g_ref[z], mixes[1, cut(j, 2 * SLAB), :])
        for half in range(2):
            column = cut(j * 2 + half, 2 * SLAB)
            tanh, sig = gates(pre_ref[z, :, column])
            d_ref[z, :, column] = gate_grad(tanh, sig, dgated[:, cut(half)])


def mix_sums(z, g_ref, pre_ref, total_ref):
    channels = g_ref.shape[2]
    _, wide, first_slab = pair_slabs(channels, pre_ref.shape[0])
    for i in range(wide):
        tanh, sig = gates(pre_ref[z, :, lanes(first_slab + i, 2 * SLAB)])
        total_ref[cut(i), :] += tn((tanh * sig).astype(BF16), g_ref[z])


def some(first, end, blocks, step):
    if blocks <= 4:
        for p in range(first, end):
            step(arrival(p, blocks))
    else:
        pl.loop(first, end)(lambda p: step(arrival(p, blocks)))


def early_kernel(blocks, early, *refs):
    cots = refs[:early]
    pre_ref, dlogit_ref, head, mixes, g_ref, d_ref, total_ref, sems = refs[early:]
    copies = start_copies([(cots[p], g_ref.at[arrival(p, blocks)]) for p in range(early)], sems)
    total_ref[...] = jnp.zeros(total_ref.shape, F32)
    finish_copies(copies)

    def one(z):
        add_loss(z, dlogit_ref, head, g_ref)
        gate_cotangent(z, g_ref, pre_ref, mixes, d_ref)
        mix_sums(z, g_ref, pre_ref, total_ref)

    some(0, early, blocks, one)


def mix_kernel(blocks, early, *refs):
    cots, refs = refs[: blocks - early], refs[blocks - early :]
    pre_ref, dlogit_ref, head = refs[:3]
    g_ref, mine_ref, own_ref, send_ref, total_ref, sems = refs[-6:]
    copies = [(cot, g_ref.at[arrival(early + i, blocks)]) for i, cot in enumerate(cots)]
    copies = start_copies(copies, sems)
    total_ref[...] = refs[3][...] if early else jnp.zeros(total_ref.shape, F32)
    finish_copies(copies)

    def one(z):
        add_loss(z, dlogit_ref, head, g_ref)
        mix_sums(z, g_ref, pre_ref, total_ref)

    some(early, blocks, blocks, one)
    mine_ref[...] = g_ref[lax.axis_index("seq") // SPAN]
    split_pair(g_ref.shape[2] // blocks, total_ref, own_ref, send_ref)


def long_kernel(blocks, early, group_size, g_ref, mid_ref, pre_ref, weights, mixes, fold, *refs):
    between_ref, own_ref, send_ref, d_ref, total_ref = refs[-5:]
    row_count, channels = g_ref.shape[1:]
    slabs = channels // SLAB
    pair, wide, first_slab = pair_slabs(channels, blocks)
    d_ref[blocks:] = jnp.zeros((SPAN,) + d_ref.shape[1:], BF16)
    some(early, blocks, blocks, lambda z: gate_cotangent(z, g_ref, pre_ref, mixes, d_ref))

    def back(first, count):
        rows = count * row_count
        here = pl.ds(first, count)
        for slab in range(slabs):
            total = g_ref[here, :, cut(slab)].reshape(rows, SLAB).astype(F32)
            for k in range(3):
                later = d_ref[pl.ds(first + k, count), :, cut(slab, 2 * SLAB)].reshape(rows, 2 * SLAB)
                total = total + nt(later, weights[1, slab, cut(k), :])
            between_ref[here, :, cut(slab)] = total.astype(BF16).reshape(count, row_count, SLAB)

    chunks(blocks, back)
    rows = blocks * row_count
    for i in range(wide):
        slab = first_slab + i
        taps = [mid_ref[2 - k : 2 - k + blocks, :, lanes(slab)].reshape(rows, SLAB) for k in range(3)]
        dpre_part = d_ref[:blocks, :, lanes(slab, 2 * SLAB)].reshape(rows, 2 * SLAB)
        total_ref[cut(i), :] = weight_sums(group_size, taps, dpre_part, fold[...])
    split_pair(pair, total_ref, own_ref, send_ref)


def own_kernel(x_ref, between_ref, weights, mixes, push_ref, sum_ref):
    row_count, channels = sum_ref.shape
    slabs = channels // SLAB
    z = lax.axis_index("seq") // SPAN
    for j in range(slabs // 2):
        dgated = nt(between_ref[z], mixes[0, cut(j, 2 * SLAB), :])
        for half in range(2):
            slab = j * 2 + half
            taps = [x_ref[z, HALO - k * REACH : HALO - k * REACH + row_count, cut(slab)] for k in range(3)]
            tanh, sig = gates(conv(taps, weights[0, slab]))
            dpre = gate_grad(tanh, sig, dgated[:, cut(half)])
            moved = [nt(dpre, weights[0, slab, cut(k), :]) for k in range(3)]
            first = jnp.concatenate([jnp.zeros((REACH, SLAB), F32), moved[1]], axis=0)
            extended = jnp.concatenate([moved[2], jnp.zeros((HALO, SLAB), F32)], axis=0) + jnp.concatenate(
                [first, jnp.zeros((HALO - REACH, SLAB), F32)], axis=0
            )
            push_ref[:, cut(slab)] = extended[:HALO].astype(BF16)
            sum_ref[:, cut(slab)] = between_ref[z, :, cut(slab)].astype(F32) + moved[0] + extended[HALO:]


def short_kernel(blocks, group_size, x_ref, between_ref, weights, mixes, fold, own_ref, send_ref, total_ref):
    row_count, channels = between_ref.shape[1:]
    pair, wide, first_slab = pair_slabs(channels, blocks)
    rows = blocks * row_count
    between = between_ref[...].reshape(rows, channels)
    for i in range(wide):
        slab = first_slab + i
        taps = [
            x_ref[:blocks, HALO - k * REACH : HALO - k * REACH + row_count, lanes(slab)].reshape(rows, SLAB)
            for k in range(3)
        ]
        tanh, sig = gates(conv(taps, weights[0, slab]))
        dpre = gate_grad(tanh, sig, nt(between, mixes[0, lanes(slab), :]))
        total_ref[cut(i), :channels] = tn((tanh * sig).astype(BF16), between)
        total_ref[cut(i), channels:] = weight_sums(group_size, taps, dpre, fold[...])
    split_pair(pair, total_ref, own_ref, send_ref)


def finish_kernel(group_size, mix1, conv1, own0, got_mix1, got_conv1, got0, mix_ref, conv_ref):
    channels = mix_ref.shape[2]
    width = 2 * group_size
    total = own0[...] + got0[...].astype(F32)
    mix_ref[:, 0, :] = total[:, :channels]
    mix_ref[:, 1, :] = mix1[...] + got_mix1[...].astype(F32)
    convs = (total[:, channels:], conv1[...] + got_conv1[...].astype(F32))
    for layer in range(2):
        for k in range(3):
            conv_ref[layer, k] = convs[layer][:, width * k : width * (k + 1)]


VMEM = pl.BlockSpec(memory_space=pltpu.VMEM)
ANY = pl.BlockSpec(memory_space=pl.ANY)


def call(resident, kernel, outs, arrays, scratch=(), name=None, aliases={}, far=(), near=True, us=0.1):
    if resident and near:
        arrays = [a if i in far else pltpu.with_memory_space_constraint(a, pltpu.VMEM) for i, a in enumerate(arrays)]
    make = pltpu.VMEM if resident and near and name != "finish" else jax.ShapeDtypeStruct
    return pl.pallas_call(
        kernel,
        out_shape=[make(shape, kind) for shape, kind in outs],
        in_specs=[ANY if i in far else VMEM for i in range(len(arrays))],
        out_specs=[VMEM] * len(outs),
        scratch_shapes=[pltpu.VMEM(*s) if isinstance(s, tuple) else s for s in scratch],
        input_output_aliases=aliases,
        compiler_params=pltpu.CompilerParams(vmem_limit_bytes=(24 if resident else 56) * 1024 * 1024),
        cost_estimate=pl.CostEstimate(flops=int(us * 1.1e9), bytes_accessed=0, transcendentals=0),
        name=name,
    )(*arrays)


def body(saved_section_input, out_cot, kernel_weight, blend_weight, hazard_head, labels, events):
    first_input, cot = saved_section_input[0], out_cot[0]
    row_count, channels = first_input.shape
    seq = lax.axis_size("seq")
    blocks = seq // SPAN
    groups, group_size = kernel_weight.shape[3:5]
    slabs = channels // SLAB
    share = channels // seq

    ring = [0] + list(range(1, blocks, 2)) + [b for b in range(blocks - 1, 0, -1) if b % 2 == 0]
    hops = list(zip(ring, ring[1:] + ring[:1]))

    def step(value):
        return lax.ppermute(
            value, "seq", [(a * SPAN + y, b * SPAN + y) for a, b in hops for y in range(SPAN)]
        )

    def swap(value):
        return lax.ppermute(value, "seq", [(b, b + 1 - 2 * (b % 2)) for b in range(seq)])

    is_last = on_last_section()

    def direct(value, steps):
        pairs = [(source, source) for source in range(blocks)]
        for _ in range(steps):
            pairs = [(source, dict(hops)[target]) for source, target in pairs]
        return lax.ppermute(value, "seq", [(a * SPAN + y, b * SPAN + y) for a, b in pairs for y in range(SPAN)])

    resident = blocks <= 4
    run = functools.partial(call, resident)
    def tail(value):
        (out,) = run(tail_kernel, [((HALO, channels), BF16)], [value], name="tail", us=0.3)
        return out

    head = hazard_head.T
    tails = [swap(first_input[row_count - HALO :])]
    codes = [jnp.stack([labels, events])]
    weights, fold = run(
        functools.partial(weight_kernel, group_size),
        [((2, slabs, 3 * SLAB, 2 * SLAB), BF16), ((SLAB, 6 * SLAB), BF16)],
        [kernel_weight[0].reshape(-1, 2 * group_size)],
        name="weights",
        near=False,
        us=1.3,
    )
    inputs, cots = [first_input], [cot]
    for p in range(1, blocks):
        inputs.append(step(inputs[-1]))
        tails.append(swap(tail(inputs[-1])))
        codes.append(direct(codes[0], p))
        cots.append(step(cots[-1]))
    mixes = blend_weight[0]
    rows = min(blocks, 4) * row_count
    held = [(a.shape, BF16) for a in (weights, mixes, head)]
    x, mid, pre, dlogit, *kept = run(
        functools.partial(forward_kernel, blocks),
        [
            ((blocks + 1, HALO + row_count, channels), BF16),
            ((blocks + SPAN, row_count, channels), BF16),
            ((blocks, row_count, 2 * channels), BF16),
            ((blocks, head.shape[0], row_count), BF16),
        ]
        + held * resident,
        [*inputs, *tails, *codes, weights, mixes, head],
        held * (not resident)
        + [((rows, channels), BF16), ((blocks, 2, row_count), jnp.int32), pltpu.SemaphoreType.DMA((2 * blocks + 5,))],
        name="forward",
        far=[*range(2 * blocks), *range(3 * blocks, 3 * blocks + 3)],
        us=5,
    )
    if resident:
        weights, mixes, head = kept
    wide = max(channels // blocks, SLAB)
    block_rows = ((blocks, row_count, channels), BF16)
    early = blocks - 1 if resident else 0
    d_rows = ((blocks + SPAN, row_count, 2 * channels), BF16)
    if early:
        g, d, total = run(
            functools.partial(early_kernel, blocks, early),
            [block_rows, d_rows, ((wide, channels), F32)],
            [*cots[:early], pre, dlogit, head, mixes],
            [pltpu.SemaphoreType.DMA((early,))],
            name="early",
            far=range(early),
            us=4,
        )
    late = cots[early:]
    g, mine, mix1, send_mix1 = run(
        functools.partial(mix_kernel, blocks, early),
        [block_rows, ((row_count, channels), BF16), ((share, channels), F32), ((share, channels), BF16)],
        [*late, pre, dlogit, head] + ([total, g] if early else []),
        [((wide, channels), F32), pltpu.SemaphoreType.DMA((len(late),))],
        name="long_mix",
        aliases={len(late) + 4: 0} if early else {},
        far=range(len(late)),
        us=0.7,
    )
    got_mix1 = swap(send_mix1)
    between, conv1, send_conv1, *_ = run(
        functools.partial(long_kernel, blocks, early, group_size),
        [block_rows, ((share, SLAB), F32), ((share, SLAB), BF16)] + ([d_rows] if early else []),
        [g, mid, pre, weights, mixes, fold] + ([d] if early else []),
        ([] if early else [d_rows]) + [((wide, SLAB), F32)],
        name="long_backward",
        aliases={6: 3} if early else {},
        us=3.4,
    )
    got_conv1 = swap(send_conv1)
    push, own_sum = run(
        own_kernel,
        [((HALO, channels), BF16), ((row_count, channels), F32)],
        [x, between, weights, mixes],
        name="own_backward",
        us=2.7,
    )
    pushed = lax.ppermute(push, "seq", [(b, b - 1) for b in range(1, seq)])
    own0, send0 = run(
        functools.partial(short_kernel, blocks, group_size),
        [((share, channels + SLAB), F32), ((share, channels + SLAB), BF16)],
        [x, between, weights, mixes, fold],
        [((wide, channels + SLAB), F32)],
        name="short_backward",
        us=2.5,
    )
    got0 = swap(send0)
    input_gradient = jnp.concatenate(
        [own_sum[: row_count - HALO], own_sum[row_count - HALO :] + pushed.astype(F32)], axis=0
    ).astype(BF16)
    count = lax.axis_size("section")
    received = lax.ppermute(input_gradient, "section", [(s, s - 1) for s in range(1, count)])
    next_cot = jnp.where(is_last, mine, received)
    mix_share, conv_share = run(
        functools.partial(finish_kernel, group_size),
        [((share, 2, channels), F32), ((2, 3, share, 2 * group_size), F32)],
        [mix1, conv1, own0, got_mix1, got_conv1, got0],
        name="finish",
        us=1.4,
    )
    conv_share = conv_share.reshape(2, 3, share // group_size, group_size, 2 * group_size)
    return (input_gradient[None], next_cot[None], mix_share[None], conv_share[None])


def solution(mesh):
    return jax.shard_map(
        body,
        mesh=mesh,
        in_specs=(
            P("section", "seq", None),
            P("section", "seq", None),
            P("section", None, None, None, None, None),
            P("section", None, None, None),
            P(),
            P("seq"),
            P("seq"),
        ),
        out_specs=(
            P("section", "seq", None),
            P("section", "seq", None),
            P("section", "seq", None, None),
            P("section", None, None, "seq", None, None),
        ),
        check_vma=False,
    )
```

time: 130 us -> 85.9 us (0.66)
  the two profiles are of different devices: /device:TPU:1 before, /device:TPU:14 now
where the time goes in v2:
time: 85.9 us; the launch traced here: 85.6 us
  starting transfers between devices  28.6 us (33%)
  waiting for transfers between devices  22.7 us (26%)
  Pallas kernels  21.9 us (25%)
  local copies, waits for them, and re-layouts  9.48 us (11%)
  other arithmetic  2.17 us (3%)
    pallas_call x11, Pallas kernels, call(): pl.pallas_call(kernel, out_shape=[make(shape, kind) for shape, kind in ou...  21.9 us
    ppermute x6, starting transfers between devices, step(): lax.ppermute(value, 'seq', [(a * SPAN + y, b * SPAN + y) for a, b in hops...  15.8 us
    ppermute x6, waiting for transfers between devices, step(): lax.ppermute(value, 'seq', [(a * SPAN + y, b * SPAN + y) for a, b in hops...  10.6 us
    ppermute x7, waiting for transfers between devices, swap(): lax.ppermute(value, 'seq', [(b, b + 1 - 2 * (b % 2)) for b in range(seq)])  9.3 us
    unnamed x13, local copies, waits for them, and re-layouts  7.96 us
    ppermute x7, starting transfers between devices, swap(): lax.ppermute(value, 'seq', [(b, b + 1 - 2 * (b % 2)) for b in range(seq)])  6.22 us
    ppermute x1, waiting for transfers between devices, body(): pushed = lax.ppermute(push, 'seq', [(b, b - 1) for b in range(1, seq)])  2.74 us
    ppermute x1, starting transfers between devices, body(): pushed = lax.ppermute(push, 'seq', [(b, b - 1) for b in range(1, seq)])  2.39 us
  transfers between devices with their start and end apart: 18, of which 6 were waited for; matrix products, arithmetic and copies ran while one was open for 6% of the time, Pallas kernels for 15%

profile of v2, /device:TPU:14, one launch (start us, length us, event | category | flops | bytes accessed | tf_op | source)
XLA Modules:
  0.0 85.6 jit_solution(12419654244169971009)
XLA Ops:
  0.6 2.6 %collective-permute-start = (bf16[128,1024]{1,0:T(8,128)(2,1)}, bf16[128,1024]{1,0:T(8,128)(2,1)S(1)}, u32[]{:S(2)}, u32[]{:S(2)}) collective-permute-start(bf16[128,1024]{1,0:T(8,128)(2,1)} %bitcast.17), channel_id=1, source_target_pairs={{0,2},{1,3},{2,6},{3,7},{6,4},{7,5},{4,0},{5,1},{8,10},{9,11},{10,... | collective-permute-start | bytes 786440 | tf_op jit(solution)/shard_map/ppermute | solution.py:392
  3.3 0.4 collective-permute-start.10
  3.7 6.6 %collective-permute-done.value.refs_1_ = bf16[128,1024]{1,0:T(8,128)(2,1)S(1)} collective-permute-done((bf16[128,1024]{1,0:T(8,128)(2,1)}, bf16[128,1024]{1,0:T(8,128)(2,1)S(1)}, u32[]{:S(2)}, u32[]{:S(2)}) %collective-permute-start) | collective-permute-done | bytes 262176 | tf_op jit(solution)/shard_map/ppermute | solution.py:392
  10.3 3.3 %collective-permute-start.1 = (bf16[128,1024]{1,0:T(8,128)(2,1)S(1)}, bf16[128,1024]{1,0:T(8,128)(2,1)S(1)}, u32[]{:S(2)}, u32[]{:S(2)}) collective-permute-start(bf16[128,1024]{1,0:T(8,128)(2,1)S(1)} %collective-permute-done.value.refs_1_), channel_id=1, source_target_pairs={{0,2},{1,3},{2,6},{3,7},{6,4},{7,5},{4,0},{5,1},{8,10},{9,11},{10,... | collective-permute-start | bytes 786440 | tf_op jit(solution)/shard_map/ppermute | solution.py:392
  13.6 0.7 pad_add_fusion.refs_8_
  14.3 0.0 collective-permute-start.7
  14.3 0.2 collective-permute-start.8
  14.5 2.0 %collective-permute-start.9 = (s32[2,128]{1,0:T(2,128)S(1)}, s32[2,128]{1,0:T(2,128)S(1)}, u32[]{:S(2)}, u32[]{:S(2)}) collective-permute-start(s32[2,128]{1,0:T(2,128)S(1)} %pad_add_fusion.refs_8_), channel_id=1, source_target_pairs={{0,4},{1,5},{2,0},{3,1},{4,6},{5,7},{6,2},{7,3},{8,12},{9,13},{10,... | collective-permute-start | bytes 3080 | tf_op jit(solution)/shard_map/ppermute | solution.py:405
  16.5 0.0 collective-permute-done.10.refs_1_
  16.5 2.7 %collective-permute-start.11 = (bf16[128,1024]{1,0:T(8,128)(2,1)S(1)}, bf16[128,1024]{1,0:T(8,128)(2,1)S(1)}, u32[]{:S(2)}, u32[]{:S(2)}) collective-permute-start(bf16[128,1024]{1,0:T(8,128)(2,1)S(1)} %collective-permute-done.10.refs_1_), channel_id=1, source_target_pairs={{0,2},{1,3},{2,6},{3,7},{6,4},{7,5},{4,0},{5,1},{8,10},{9,11},{10,... | collective-permute-start | bytes 786440 | tf_op jit(solution)/shard_map/ppermute | solution.py:392
  19.2 2.3 %collective-permute-done.1.value.refs_2_ = bf16[128,1024]{1,0:T(8,128)(2,1)S(1)} collective-permute-done((bf16[128,1024]{1,0:T(8,128)(2,1)S(1)}, bf16[128,1024]{1,0:T(8,128)(2,1)S(1)}, u32[]{:S(2)}, u32[]{:S(2)}) %collective-permute-start.1) | collective-permute-done | bytes 262176 | tf_op jit(solution)/shard_map/ppermute | solution.py:392
  21.5 3.4 %collective-permute-start.2 = (bf16[128,1024]{1,0:T(8,128)(2,1)S(1)}, bf16[128,1024]{1,0:T(8,128)(2,1)S(1)}, u32[]{:S(2)}, u32[]{:S(2)}) collective-permute-start(bf16[128,1024]{1,0:T(8,128)(2,1)S(1)} %collective-permute-done.1.value.refs_2_), channel_id=1, source_target_pairs={{0,2},{1,3},{2,6},{3,7},{6,4},{7,5},{4,0},{5,1},{8,10},{9,11},{10,... | collective-permute-start | bytes 786440 | tf_op jit(solution)/shard_map/ppermute | solution.py:392
  24.9 1.5 %slice_bitcast_fusion = bf16[32,1024]{1,0:T(8,128)(2,1)} fusion(bf16[1,128,1024]{2,1,0:T(8,128)(2,1)} %param.7), kind=kLoop, calls=%fused_computation.5 | loop fusion | bytes 131072 | tf_op jit(solution)/shard_map/slice | solution.py:414
  26.3 2.2 %copy.13 = bf16[1,2,3,64,16,32]{5,4,3,2,1,0:T(8,128)(2,1)S(1)} copy(bf16[1,2,3,64,16,32]{3,5,4,2,1,0:T(8,128)(2,1)} %param.9) | data formatting | bytes 786432 | tf_op args[2]
  28.6 0.6 tail.3
  29.2 0.6 tail.4
  29.9 1.8 %collective-permute-done.2.value.refs_3_ = bf16[128,1024]{1,0:T(8,128)(2,1)S(1)} collective-permute-done((bf16[128,1024]{1,0:T(8,128)(2,1)S(1)}, bf16[128,1024]{1,0:T(8,128)(2,1)S(1)}, u32[]{:S(2)}, u32[]{:S(2)}) %collective-permute-start.2) | collective-permute-done | bytes 262176 | tf_op jit(solution)/shard_map/ppermute | solution.py:392
  31.6 0.5 collective-permute-start.3
  32.1 0.6 tail.5
  32.7 0.0 collective-permute-done.7.refs_9_
  32.8 1.5 %collective-permute-start.4 = (bf16[32,1024]{1,0:T(8,128)(2,1)}, bf16[32,1024]{1,0:T(8,128)(2,1)}, u32[]{:S(2)}, u32[]{:S(2)}) collective-permute-start(bf16[32,1024]{1,0:T(8,128)(2,1)} %tail.3), channel_id=1, source_target_pairs={{0,1},{1,0},{2,3},{3,2},{4,5},{5,4},{6,7},{7,6},{8,9},{9,8},{10,11... | collective-permute-start | bytes 196616 | tf_op jit(solution)/shard_map/ppermute | solution.py:397
  34.3 0.5 collective-permute-start.5
  34.8 1.5 %collective-permute-start.6 = (bf16[32,1024]{1,0:T(8,128)(2,1)}, bf16[32,1024]{1,0:T(8,128)(2,1)}, u32[]{:S(2)}, u32[]{:S(2)}) collective-permute-start(bf16[32,1024]{1,0:T(8,128)(2,1)} %tail.5), channel_id=1, source_target_pairs={{0,1},{1,0},{2,3},{3,2},{4,5},{5,4},{6,7},{7,6},{8,9},{9,8},{10,11... | collective-permute-start | bytes 196616 | tf_op jit(solution)/shard_map/ppermute | solution.py:397
  36.3 1.0 %weights.1 = (bf16[2,8,384,256]{3,2,1,0:T(8,128)(2,1)S(1)}, bf16[128,768]{1,0:T(8,128)(2,1)S(1)}) custom-call(bf16[6144,32]{1,0:T(8,128)(2,1)S(1)} %bitcast.16), custom_call_target="tpu_custom_call" | custom-call | flops 1430000000 | tf_op jit(solution)/shard_map/weights/pallas_call | solution.py:366
  37.3 1.6 %copy-done.4 = bf16[2,8,384,256]{3,2,1,0:T(8,128)(2,1)} copy-done((bf16[2,8,384,256]{3,2,1,0:T(8,128)(2,1)}, bf16[2,8,384,256]{3,2,1,0:T(8,128)(2,1)S(1)}, u32[]{:S(2)}) %copy-start.4) | copy-done | bytes 3145752
  38.9 0.0 collective-permute-done.11.refs_2_
  38.9 3.4 %collective-permute-start.12 = (bf16[128,1024]{1,0:T(8,128)(2,1)S(1)}, bf16[128,1024]{1,0:T(8,128)(2,1)S(1)}, u32[]{:S(2)}, u32[]{:S(2)}) collective-permute-start(bf16[128,1024]{1,0:T(8,128)(2,1)S(1)} %collective-permute-done.11.refs_2_), channel_id=1, source_target_pairs={{0,2},{1,3},{2,6},{3,7},{6,4},{7,5},{4,0},{5,1},{8,10},{9,11},{10,... | collective-permute-start | bytes 786440 | tf_op jit(solution)/shard_map/ppermute | solution.py:392
  42.3 0.0 collective-permute-done.6.refs_7_
  42.3 0.0 copy-start.1
  42.3 2.2 %copy-done.1 = bf16[1,2,1024,1024]{3,2,1,0:T(8,128)(2,1)S(1)} copy-done((bf16[1,2,1024,1024]{3,2,1,0:T(8,128)(2,1)S(1)}, bf16[1,2,1024,1024]{3,2,1,0:T(8,128)(2,1)}, u32[]{:S(2)}) %copy-start.1) | copy-done | bytes 4194328
  44.5 1.9 %copy-done.5 = bf16[2,8,384,256]{3,2,1,0:T(8,128)(2,1)S(1)} copy-done((bf16[2,8,384,256]{3,2,1,0:T(8,128)(2,1)S(1)}, bf16[2,8,384,256]{3,2,1,0:T(8,128)(2,1)}, u32[]{:S(2)}) %copy-start.5) | copy-done | bytes 3145752
  46.4 5.0 %forward.1 = (bf16[5,160,1024]{2,1,0:T(8,128)(2,1)S(1)}, bf16[6,128,1024]{2,1,0:T(8,128)(2,1)S(1)}, bf16[4,128,2048]{2,1,0:T(8,128)(2,1)S(1)}, bf16[4,64,128]{2,...) custom-call(bf16[128,1024]{1,0:T(8,128)(2,1)S(1)} %bitcast.18, ...), custom_call_target="tpu_custom_call" | custom-call | flops 5500000256 | tf_op jit(solution)/shard_map/forward/pallas_call | solution.py:366
  51.4 3.3 %early.1 = (bf16[4,128,1024]{2,1,0:T(8,128)(2,1)S(1)}, bf16[6,128,2048]{2,1,0:T(8,128)(2,1)S(1)}, f32[256,1024]{1,0:T(8,128)S(1)}) custom-call(bf16[128,1024]{1,0:T(8,128)(2,1)S(1)} %bitcast.21, bf16[128,1024]{1,0:T(8,128)(2,1)S(1)} %collective-permute-done.10.refs_1_, bf16[128,1024]{1,0:T(8,128)(2,1)S(1)} %collective-permute-done.11.refs_2_, ...), custom_call_target="tpu_custom_call" | custom-call | flops 4400000000 | tf_op jit(solution)/shard_map/early/pallas_call | solution.py:366
  54.7 0.8 long_mix.1
  55.5 3.4 %long_backward.1 = (bf16[4,128,1024]{2,1,0:T(8,128)(2,1)S(1)}, f32[128,128]{1,0:T(8,128)S(1)}, bf16[128,128]{1,0:T(8,128)(2,1)S(1)}, bf16[6,128,2048]{2,1,0:T(8,128)(2,1)S(1)}) custom-call(bf16[4,128,1024]{2,1,0:T(8,128)(2,1)S(1)} %get-tuple-element.37.g_ref, bf16[6,128,1024]{2,1,0:T(8,128)(2,1)S(1)} %get-tuple-element.38.mid_ref, ...), custom_call_target="tpu_custom_call", output_to_operand_aliasing={{3}: (6, {})} | custom-call | flops 3740000000 | tf_op jit(solution)/shard_map/long_backward/pallas_call | solution.py:366
  58.9 2.7 %own_backward.1 = (bf16[32,1024]{1,0:T(8,128)(2,1)S(1)}, f32[128,1024]{1,0:T(8,128)S(1)}) custom-call(bf16[5,160,1024]{2,1,0:T(8,128)(2,1)S(1)} %get-tuple-element.30.x_ref, bf16[4,128,1024]{2,1,0:T(8,128)(2,1)S(1)} %get-tuple-element.42.between_ref, bf16[2,8,384,256]{3,2,1,0:T(8,128)(2,1)S(1)} %get-tuple-element.39.weights, ...), custom_call_target="tpu_custom_call" | custom-call | flops 2969999872 | tf_op jit(solution)/shard_map/own_backward/pallas_call | solution.py:366
  61.6 2.5 %short_backward.1 = (f32[128,1152]{1,0:T(8,128)S(1)}, bf16[128,1152]{1,0:T(8,128)(2,1)S(1)}) custom-call(bf16[5,160,1024]{2,1,0:T(8,128)(2,1)S(1)} %get-tuple-element.30.x_ref, bf16[4,128,1024]{2,1,0:T(8,128)(2,1)S(1)} %get-tuple-element.42.between_ref, bf16[2,8,384,256]{3,2,1,0:T(8,128)(2,1)S(1)} %get-tuple-element.39.weights, ...), custom_call_target="tpu_custom_call" | custom-call | flops 2750000128 | tf_op jit(solution)/shard_map/short_backward/pallas_call | solution.py:366
  64.1 2.4 %collective-permute-start.13 = (bf16[32,1024]{1,0:T(8,128)(2,1)S(1)}, bf16[32,1024]{1,0:T(8,128)(2,1)S(1)}, u32[]{:S(2)}, u32[]{:S(2)}) collective-permute-start(bf16[32,1024]{1,0:T(8,128)(2,1)S(1)} %get-tuple-element.44), channel_id=1, source_target_pairs={{1,0},{2,1},{3,2},{4,3},{5,4},{6,5},{7,6},{9,8},{10,9},{11,10},{12... | collective-permute-start | bytes 196616 | tf_op jit(solution)/shard_map/ppermute | solution.py:494
  66.6 0.1 collective-permute-start.15
  66.6 2.0 %collective-permute-start.16 = (bf16[128,128]{1,0:T(8,128)(2,1)S(1)}, bf16[128,128]{1,0:T(8,128)(2,1)S(1)}, u32[]{:S(2)}, u32[]{:S(2)}) collective-permute-start(bf16[128,128]{1,0:T(8,128)(2,1)S(1)} %get-tuple-element.50), channel_id=1, source_target_pairs={{0,1},{1,0},{2,3},{3,2},{4,5},{5,4},{6,7},{7,6},{8,9},{9,8},{10,11... | collective-permute-start | bytes 98312 | tf_op jit(solution)/shard_map/ppermute | solution.py:397
  68.7 0.1 collective-permute-start.17
  68.7 2.7 %collective-permute-done.13 = bf16[32,1024]{1,0:T(8,128)(2,1)S(1)} collective-permute-done((bf16[32,1024]{1,0:T(8,128)(2,1)S(1)}, bf16[32,1024]{1,0:T(8,128)(2,1)S(1)}, u32[]{:S(2)}, u32[]{:S(2)}) %collective-permute-start.13) | collective-permute-done | bytes 65568 | tf_op jit(solution)/shard_map/ppermute | solution.py:494
  71.5 1.9 %collective-permute-start.14 = (bf16[128,1024]{1,0:T(8,128)(2,1)S(1)}, bf16[128,1024]{1,0:T(8,128)(2,1)S(1)}, u32[]{:S(2)}, u32[]{:S(2)}) collective-permute-start(bf16[128,1024]{1,0:T(8,128)(2,1)S(1)} %pad_maximum_fusion.1), channel_id=1, source_target_pairs={{8,0},{16,8},{24,16},{9,1},{17,9},{25,17},{10,2},{18,10},{26,18},{... | collective-permute-start | bytes 786440 | tf_op jit(solution)/shard_map/ppermute | solution.py:508
  73.5 0.7 pad_maximum_fusion
  74.2 3.6 %collective-permute-done.16.got_conv1 = bf16[128,128]{1,0:T(8,128)(2,1)S(1)} collective-permute-done((bf16[128,128]{1,0:T(8,128)(2,1)S(1)}, bf16[128,128]{1,0:T(8,128)(2,1)S(1)}, u32[]{:S(2)}, u32[]{:S(2)}) %collective-permute-start.16) | collective-permute-done | bytes 32800 | tf_op jit(solution)/shard_map/ppermute | solution.py:397
  77.8 5.7 %collective-permute-done.17.got0 = bf16[128,1152]{1,0:T(8,128)(2,1)S(1)} collective-permute-done((bf16[128,1152]{1,0:T(8,128)(2,1)S(1)}, bf16[128,1152]{1,0:T(8,128)(2,1)S(1)}, u32[]{:S(2)}, u32[]{:S(2)}) %collective-permute-start.17) | collective-permute-done | bytes 294944 | tf_op jit(solution)/shard_map/ppermute | solution.py:397
  83.5 1.4 %finish.1 = (f32[128,2,1024]{2,1,0:T(2,128)}, f32[2,3,128,32]{3,2,1,0:T(8,128)}) custom-call(f32[128,1024]{1,0:T(8,128)S(1)} %get-tuple-element.46.mix1, f32[128,128]{1,0:T(8,128)S(1)} %get-tuple-element.47.conv1, f32[128,1152]{1,0:T(8,128)S(1)} %get-tuple-element.48.own0, bf16[128,1024]{1,0:T(8,128)(2,1)S(1)} %collective-permute-done.15.got_mix1, ...), custom_call_target="tpu_custom_call" | custom-call | flops 1540000000 | tf_op jit(solution)/shard_map/finish/pallas_call | solution.py:366
  84.8 0.7 select_bitcast_fusion
  (20 shorter events, 0.1 us)
Async XLA Ops:
  0.6 9.7 %collective-permute-start = (bf16[128,1024]{1,0:T(8,128)(2,1)}, bf16[128,1024]{1,0:T(8,128)(2,1)S(1)}, u32[]{:S(2)}, u32[]{:S(2)}) collective-permute-start(bf16[128,1024]{1,0:T(8,128)(2,1)} %bitcast.17), channel_id=1, source_target_pairs={{0,2},{1,3},{2,6},{3,7},{6,4},{7,5},{4,0},{5,1},{8,10},{9,11},{10,... | collective-permute-start | bytes 786440 | tf_op jit(solution)/shard_map/ppermute | solution.py:392
  3.3 13.2 %collective-permute-start.10 = (bf16[128,1024]{1,0:T(8,128)(2,1)}, bf16[128,1024]{1,0:T(8,128)(2,1)S(1)}, u32[]{:S(2)}, u32[]{:S(2)}) collective-permute-start(bf16[128,1024]{1,0:T(8,128)(2,1)} %bitcast.20), channel_id=1, source_target_pairs={{0,2},{1,3},{2,6},{3,7},{6,4},{7,5},{4,0},{5,1},{8,10},{9,11},{10,... | collective-permute-start | bytes 786440 | tf_op jit(solution)/shard_map/ppermute | solution.py:392
  10.3 11.2 %collective-permute-start.1 = (bf16[128,1024]{1,0:T(8,128)(2,1)S(1)}, bf16[128,1024]{1,0:T(8,128)(2,1)S(1)}, u32[]{:S(2)}, u32[]{:S(2)}) collective-permute-start(bf16[128,1024]{1,0:T(8,128)(2,1)S(1)} %collective-permute-done.value.refs_1_), channel_id=1, source_target_pairs={{0,2},{1,3},{2,6},{3,7},{6,4},{7,5},{4,0},{5,1},{8,10},{9,11},{10,... | collective-permute-start | bytes 786440 | tf_op jit(solution)/shard_map/ppermute | solution.py:392
  14.3 18.5 %collective-permute-start.7 = (s32[2,128]{1,0:T(2,128)S(1)}, s32[2,128]{1,0:T(2,128)S(1)}, u32[]{:S(2)}, u32[]{:S(2)}) collective-permute-start(s32[2,128]{1,0:T(2,128)S(1)} %pad_add_fusion.refs_8_), channel_id=1, source_target_pairs={{0,2},{1,3},{2,6},{3,7},{4,0},{5,1},{6,4},{7,5},{8,10},{9,11},{10,... | collective-permute-start | bytes 3080 | tf_op jit(solution)/shard_map/ppermute | solution.py:405
  14.3 20.0 %collective-permute-start.8 = (s32[2,128]{1,0:T(2,128)S(1)}, s32[2,128]{1,0:T(2,128)S(1)}, u32[]{:S(2)}, u32[]{:S(2)}) collective-permute-start(s32[2,128]{1,0:T(2,128)S(1)} %pad_add_fusion.refs_8_), channel_id=1, source_target_pairs={{0,6},{1,7},{2,4},{3,5},{4,2},{5,3},{6,0},{7,1},{8,14},{9,15},{10,... | collective-permute-start | bytes 3080 | tf_op jit(solution)/shard_map/ppermute | solution.py:405
  14.5 20.3 %collective-permute-start.9 = (s32[2,128]{1,0:T(2,128)S(1)}, s32[2,128]{1,0:T(2,128)S(1)}, u32[]{:S(2)}, u32[]{:S(2)}) collective-permute-start(s32[2,128]{1,0:T(2,128)S(1)} %pad_add_fusion.refs_8_), channel_id=1, source_target_pairs={{0,4},{1,5},{2,0},{3,1},{4,6},{5,7},{6,2},{7,3},{8,12},{9,13},{10,... | collective-permute-start | bytes 3080 | tf_op jit(solution)/shard_map/ppermute | solution.py:405
  16.5 22.4 %collective-permute-start.11 = (bf16[128,1024]{1,0:T(8,128)(2,1)S(1)}, bf16[128,1024]{1,0:T(8,128)(2,1)S(1)}, u32[]{:S(2)}, u32[]{:S(2)}) collective-permute-start(bf16[128,1024]{1,0:T(8,128)(2,1)S(1)} %collective-permute-done.10.refs_1_), channel_id=1, source_target_pairs={{0,2},{1,3},{2,6},{3,7},{6,4},{7,5},{4,0},{5,1},{8,10},{9,11},{10,... | collective-permute-start | bytes 786440 | tf_op jit(solution)/shard_map/ppermute | solution.py:392
  21.5 10.1 %collective-permute-start.2 = (bf16[128,1024]{1,0:T(8,128)(2,1)S(1)}, bf16[128,1024]{1,0:T(8,128)(2,1)S(1)}, u32[]{:S(2)}, u32[]{:S(2)}) collective-permute-start(bf16[128,1024]{1,0:T(8,128)(2,1)S(1)} %collective-permute-done.1.value.refs_2_), channel_id=1, source_target_pairs={{0,2},{1,3},{2,6},{3,7},{6,4},{7,5},{4,0},{5,1},{8,10},{9,11},{10,... | collective-permute-start | bytes 786440 | tf_op jit(solution)/shard_map/ppermute | solution.py:392
  29.9 12.5 %copy-start = (bf16[1,128,1024]{2,1,0:T(8,128)(2,1)S(1)}, bf16[1,128,1024]{2,1,0:T(8,128)(2,1)}, u32[]{:S(2)}) copy-start(bf16[1,128,1024]{2,1,0:T(8,128)(2,1)} %param.7) | copy-start | bytes 786436
  29.9 12.5 %copy-start.3 = (bf16[1024,64]{0,1:T(8,128)(2,1)S(1)}, bf16[1024,64]{0,1:T(8,128)(2,1)}, u32[]{:S(2)}) copy-start(bf16[1024,64]{0,1:T(8,128)(2,1)} %param.11) | copy-start | bytes 393220
  31.6 10.7 %collective-permute-start.3 = (bf16[32,1024]{1,0:T(8,128)(2,1)}, bf16[32,1024]{1,0:T(8,128)(2,1)S(1)}, u32[]{:S(2)}, u32[]{:S(2)}) collective-permute-start(bf16[32,1024]{1,0:T(8,128)(2,1)} %slice_bitcast_fusion), channel_id=1, source_target_pairs={{0,1},{1,0},{2,3},{3,2},{4,5},{5,4},{6,7},{7,6},{8,9},{9,8},{10,11... | collective-permute-start | bytes 196616 | tf_op jit(solution)/shard_map/ppermute | solution.py:397
  32.8 9.6 %collective-permute-start.4 = (bf16[32,1024]{1,0:T(8,128)(2,1)}, bf16[32,1024]{1,0:T(8,128)(2,1)}, u32[]{:S(2)}, u32[]{:S(2)}) collective-permute-start(bf16[32,1024]{1,0:T(8,128)(2,1)} %tail.3), channel_id=1, source_target_pairs={{0,1},{1,0},{2,3},{3,2},{4,5},{5,4},{6,7},{7,6},{8,9},{9,8},{10,11... | collective-permute-start | bytes 196616 | tf_op jit(solution)/shard_map/ppermute | solution.py:397
  34.3 8.0 %collective-permute-start.5 = (bf16[32,1024]{1,0:T(8,128)(2,1)}, bf16[32,1024]{1,0:T(8,128)(2,1)}, u32[]{:S(2)}, u32[]{:S(2)}) collective-permute-start(bf16[32,1024]{1,0:T(8,128)(2,1)} %tail.4), channel_id=1, source_target_pairs={{0,1},{1,0},{2,3},{3,2},{4,5},{5,4},{6,7},{7,6},{8,9},{9,8},{10,11... | collective-permute-start | bytes 196616 | tf_op jit(solution)/shard_map/ppermute | solution.py:397
  34.8 7.5 %collective-permute-start.6 = (bf16[32,1024]{1,0:T(8,128)(2,1)}, bf16[32,1024]{1,0:T(8,128)(2,1)}, u32[]{:S(2)}, u32[]{:S(2)}) collective-permute-start(bf16[32,1024]{1,0:T(8,128)(2,1)} %tail.5), channel_id=1, source_target_pairs={{0,1},{1,0},{2,3},{3,2},{4,5},{5,4},{6,7},{7,6},{8,9},{9,8},{10,11... | collective-permute-start | bytes 196616 | tf_op jit(solution)/shard_map/ppermute | solution.py:397
  37.3 1.6 %copy-start.4 = (bf16[2,8,384,256]{3,2,1,0:T(8,128)(2,1)}, bf16[2,8,384,256]{3,2,1,0:T(8,128)(2,1)S(1)}, u32[]{:S(2)}) copy-start(bf16[2,8,384,256]{3,2,1,0:T(8,128)(2,1)S(1)} %get-tuple-element.29.refs_12_) | copy-start | bytes 9437188
  38.9 15.8 %collective-permute-start.12 = (bf16[128,1024]{1,0:T(8,128)(2,1)S(1)}, bf16[128,1024]{1,0:T(8,128)(2,1)S(1)}, u32[]{:S(2)}, u32[]{:S(2)}) collective-permute-start(bf16[128,1024]{1,0:T(8,128)(2,1)S(1)} %collective-permute-done.11.refs_2_), channel_id=1, source_target_pairs={{0,2},{1,3},{2,6},{3,7},{6,4},{7,5},{4,0},{5,1},{8,10},{9,11},{10,... | collective-permute-start | bytes 786440 | tf_op jit(solution)/shard_map/ppermute | solution.py:392
  42.3 2.2 %copy-start.1 = (bf16[1,2,1024,1024]{3,2,1,0:T(8,128)(2,1)S(1)}, bf16[1,2,1024,1024]{3,2,1,0:T(8,128)(2,1)}, u32[]{:S(2)}) copy-start(bf16[1,2,1024,1024]{3,2,1,0:T(8,128)(2,1)} %param.10) | copy-start | bytes 12582916
  44.5 1.9 %copy-start.5 = (bf16[2,8,384,256]{3,2,1,0:T(8,128)(2,1)S(1)}, bf16[2,8,384,256]{3,2,1,0:T(8,128)(2,1)}, u32[]{:S(2)}) copy-start(bf16[2,8,384,256]{3,2,1,0:T(8,128)(2,1)} %copy-done.4) | copy-start | bytes 9437188
  46.4 5.0 %copy-start.2 = (bf16[1,128,1024]{2,1,0:T(8,128)(2,1)S(1)}, bf16[1,128,1024]{2,1,0:T(8,128)(2,1)}, u32[]{:S(2)}) copy-start(bf16[1,128,1024]{2,1,0:T(8,128)(2,1)} %param.8) | copy-start | bytes 786436
  64.1 7.4 %collective-permute-start.13 = (bf16[32,1024]{1,0:T(8,128)(2,1)S(1)}, bf16[32,1024]{1,0:T(8,128)(2,1)S(1)}, u32[]{:S(2)}, u32[]{:S(2)}) collective-permute-start(bf16[32,1024]{1,0:T(8,128)(2,1)S(1)} %get-tuple-element.44), channel_id=1, source_target_pairs={{1,0},{2,1},{3,2},{4,3},{5,4},{6,5},{7,6},{9,8},{10,9},{11,10},{12... | collective-permute-start | bytes 196616 | tf_op jit(solution)/shard_map/ppermute | solution.py:494
  66.6 11.2 %collective-permute-start.15 = (bf16[128,1024]{1,0:T(8,128)(2,1)S(1)}, bf16[128,1024]{1,0:T(8,128)(2,1)S(1)}, u32[]{:S(2)}, u32[]{:S(2)}) collective-permute-start(bf16[128,1024]{1,0:T(8,128)(2,1)S(1)} %get-tuple-element.49), channel_id=1, source_target_pairs={{0,1},{1,0},{2,3},{3,2},{4,5},{5,4},{6,7},{7,6},{8,9},{9,8},{10,11... | collective-permute-start | bytes 786440 | tf_op jit(solution)/shard_map/ppermute | solution.py:397
  66.6 11.1 %collective-permute-start.16 = (bf16[128,128]{1,0:T(8,128)(2,1)S(1)}, bf16[128,128]{1,0:T(8,128)(2,1)S(1)}, u32[]{:S(2)}, u32[]{:S(2)}) collective-permute-start(bf16[128,128]{1,0:T(8,128)(2,1)S(1)} %get-tuple-element.50), channel_id=1, source_target_pairs={{0,1},{1,0},{2,3},{3,2},{4,5},{5,4},{6,7},{7,6},{8,9},{9,8},{10,11... | collective-permute-start | bytes 98312 | tf_op jit(solution)/shard_map/ppermute | solution.py:397
  68.7 14.8 %collective-permute-start.17 = (bf16[128,1152]{1,0:T(8,128)(2,1)S(1)}, bf16[128,1152]{1,0:T(8,128)(2,1)S(1)}, u32[]{:S(2)}, u32[]{:S(2)}) collective-permute-start(bf16[128,1152]{1,0:T(8,128)(2,1)S(1)} %get-tuple-element.51), channel_id=1, source_target_pairs={{0,1},{1,0},{2,3},{3,2},{4,5},{5,4},{6,7},{7,6},{8,9},{9,8},{10,11... | collective-permute-start | bytes 884744 | tf_op jit(solution)/shard_map/ppermute | solution.py:397
  71.5 13.3 %collective-permute-start.14 = (bf16[128,1024]{1,0:T(8,128)(2,1)S(1)}, bf16[128,1024]{1,0:T(8,128)(2,1)S(1)}, u32[]{:S(2)}, u32[]{:S(2)}) collective-permute-start(bf16[128,1024]{1,0:T(8,128)(2,1)S(1)} %pad_maximum_fusion.1), channel_id=1, source_target_pairs={{8,0},{16,8},{24,16},{9,1},{17,9},{25,17},{10,2},{18,10},{26,18},{... | collective-permute-start | bytes 786440 | tf_op jit(solution)/shard_map/ppermute | solution.py:508

commit v3 on v2

--- a/solution.py
+++ b/solution.py
@@ -12,6 +12,7 @@
 F32 = jnp.float32
 BF16 = jnp.bfloat16
 HALO = 32
+SCALE = 0.5
 REACH = 16
 
 
@@ -101,28 +102,43 @@
         copy.wait()
 
 
-def weight_kernel(group_size, w_ref, out_ref, fold_ref):
+def weight_kernel(group_size, far_w, far_mixes, far_head, far_cot, out_ref, fold_ref, mixes_ref, head_ref, cot_ref,
+                  w_ref, sems):
+    copies = start_copies([(far_w, w_ref), (far_cot, cot_ref), (far_mixes, mixes_ref), (far_head, head_ref)], sems)
     layers, slabs = out_ref.shape[:2]
+    width, groups = w_ref.shape[2:]
     rows = slabs * SLAB
-    one_hot = spread(group_size, 0, 2 * group_size).astype(BF16)
+    outputs = 2 * group_size
+    row = lax.broadcasted_iota(jnp.int32, (rows, groups), 0)
+    pick = (row // group_size == lax.broadcasted_iota(jnp.int32, (rows, groups), 1)).astype(F32).astype(BF16)
+    row = lax.broadcasted_iota(jnp.int32, (SLAB, width), 0)
+    own = lax.broadcasted_iota(jnp.int32, (SLAB, width), 1) // outputs == row % group_size
+    o = lax.broadcasted_iota(jnp.int32, (width, 2 * SLAB), 0) % outputs
+    column = lax.broadcasted_iota(jnp.int32, (width, 2 * SLAB), 1)
+    one_hot = (o == column % group_size + jnp.where(column >= SLAB, group_size, 0)).astype(F32).astype(BF16)
     keep = same_group(group_size)
+    finish_copies(copies[:1])
     for layer in range(layers):
         for k in range(3):
-            tiled = nn(w_ref[(layer * 3 + k) * rows : (layer * 3 + k + 1) * rows, :], one_hot)
             for slab in range(slabs):
-                out_ref[layer, slab, cut(k), :] = jnp.where(keep, tiled[cut(slab)], 0.0).astype(BF16)
+                picked = nt(pick[cut(slab)], w_ref[layer, k])
+                tiled = nn(jnp.where(own, picked, 0.0).astype(BF16), one_hot)
+                out_ref[layer, slab, cut(k), :] = jnp.where(keep, tiled, 0.0).astype(BF16)
     for k in range(3):
-        fold_ref[:, cut(k, 2 * SLAB)] = spread(group_size, 2 * group_size * k, SLAB).astype(BF16)
-
-
-def tail_kernel(value, out_ref):
-    out_ref[...] = value[value.shape[0] - HALO :, :]
+        fold_ref[:, cut(k, 2 * SLAB)] = spread(group_size, outputs * k, SLAB).astype(BF16)
+    finish_copies(copies[1:])
+
+
+def relay_kernel(value, *refs):
+    tail_ref, copy_ref, sems = refs[-3:]
+    copies = start_copies([(value, copy_ref)], sems)
+    tail_ref[...] = value[value.shape[0] - HALO :, :]
+    finish_copies(copies)
 
 
 def forward_kernel(blocks, *refs):
     inputs, tails, codes = refs[:blocks], refs[blocks : 2 * blocks], refs[2 * blocks : 3 * blocks]
-    (far_weights, far_mixes, far_head, x_ref, mid_ref, pre_ref, dlogit_ref, weights, mixes, head,
-     gated_ref, code_ref, sems) = refs[3 * blocks :]
+    weights, mixes, head, x_ref, mid_ref, pre_ref, dlogit_ref, gated_ref, code_ref, sems = refs[3 * blocks :]
     row_count, channels = inputs[0].shape
     slabs = channels // SLAB
     y = lax.axis_index("seq") % SPAN
@@ -132,8 +148,6 @@
         rows_in.append((inputs[p], x_ref.at[z, pl.ds(HALO, row_count)]))
         rows_in.append((tails[p], x_ref.at[z + 1 - y, pl.ds(0, HALO)]))
     rows_in = start_copies(rows_in, sems)
-    held = [(far_weights.at[0], weights.at[0]), (far_mixes.at[0], mixes.at[0]), (far_weights.at[1], weights.at[1])]
-    held = start_copies(held + [(far_mixes.at[1], mixes.at[1]), (far_head, head)], sems, 2 * blocks)
     for p in range(blocks):
         code_ref[arrival(p, blocks)] = codes[p][...]
     mid_ref[0:SPAN] = jnp.zeros((SPAN, row_count, channels), BF16)
@@ -142,7 +156,7 @@
     def _():
         x_ref[0, :HALO, :] = jnp.zeros((HALO, channels), BF16)
 
-    finish_copies(rows_in + held[:1])
+    finish_copies(rows_in)
 
     def gate(first, count, layer, tap):
         for slab in range(slabs):
@@ -158,16 +172,11 @@
 
     def short(first, count):
         gate(first, count, 0, short_tap)
-        if count == blocks:
-            finish_copies(held[1:2])
         mixed = nn(gated_ref[...], mixes[0]).reshape(count, row_count, channels)
         here = pl.ds(first, count)
         mid_ref[pl.ds(first + SPAN, count)] = (x_ref[here, HALO:, :].astype(F32) + mixed).astype(BF16)
 
-    if blocks > 4:
-        finish_copies(held[1:2])
     chunks(blocks, short)
-    finish_copies(held[2:])
 
     def long_tap(z, k, column):
         return mid_ref[z + SPAN - k, :, column]
@@ -219,29 +228,35 @@
         g_ref[z] = (g_ref[z].astype(F32) + tn(dlogit_ref[z], head[...])).astype(BF16)
 
 
-def gate_cotangent(z, g_ref, pre_ref, mixes, d_ref):
+def gate_cotangent(places, g_ref, pre_ref, mixes, d_ref):
+    rows = g_ref.shape[1]
+    g = jnp.concatenate([g_ref[z] for z in places], axis=0)
     for j in range(g_ref.shape[2] // SLAB // 2):
-        dgated = nt(g_ref[z], mixes[1, cut(j, 2 * SLAB), :])
+        dgated = nt(g, mixes[1, cut(j, 2 * SLAB), :])
         for half in range(2):
             column = cut(j * 2 + half, 2 * SLAB)
-            tanh, sig = gates(pre_ref[z, :, column])
-            d_ref[z, :, column] = gate_grad(tanh, sig, dgated[:, cut(half)])
-
-
-def mix_sums(z, g_ref, pre_ref, total_ref):
+            for i, z in enumerate(places):
+                tanh, sig = gates(pre_ref[z, :, column])
+                d_ref[z, :, column] = gate_grad(tanh, sig, dgated[cut(i, rows), cut(half)])
+
+
+def mix_sums(places, g_ref, pre_ref, total_ref):
     channels = g_ref.shape[2]
     _, wide, first_slab = pair_slabs(channels, pre_ref.shape[0])
+    g = jnp.concatenate([g_ref[z] for z in places], axis=0)
     for i in range(wide):
-        tanh, sig = gates(pre_ref[z, :, lanes(first_slab + i, 2 * SLAB)])
-        total_ref[cut(i), :] += tn((tanh * sig).astype(BF16), g_ref[z])
+        gated = []
+        for z in places:
+            tanh, sig = gates(pre_ref[z, :, lanes(first_slab + i, 2 * SLAB)])
+            gated.append((tanh * sig).astype(BF16))
+        total_ref[cut(i), :] += tn(jnp.concatenate(gated, axis=0), g)
 
 
 def some(first, end, blocks, step):
     if blocks <= 4:
-        for p in range(first, end):
-            step(arrival(p, blocks))
+        step([arrival(p, blocks) for p in range(first, end)])
     else:
-        pl.loop(first, end)(lambda p: step(arrival(p, blocks)))
+        pl.loop(first, end)(lambda p: step([arrival(p, blocks)]))
 
 
 def early_kernel(blocks, early, *refs):
@@ -251,10 +266,11 @@
     total_ref[...] = jnp.zeros(total_ref.shape, F32)
     finish_copies(copies)
 
-    def one(z):
-        add_loss(z, dlogit_ref, head, g_ref)
-        gate_cotangent(z, g_ref, pre_ref, mixes, d_ref)
-        mix_sums(z, g_ref, pre_ref, total_ref)
+    def one(places):
+        for z in places:
+            add_loss(z, dlogit_ref, head, g_ref)
+        gate_cotangent(places, g_ref, pre_ref, mixes, d_ref)
+        mix_sums(places, g_ref, pre_ref, total_ref)
 
     some(0, early, blocks, one)
 
@@ -268,22 +284,34 @@
     total_ref[...] = refs[3][...] if early else jnp.zeros(total_ref.shape, F32)
     finish_copies(copies)
 
-    def one(z):
-        add_loss(z, dlogit_ref, head, g_ref)
-        mix_sums(z, g_ref, pre_ref, total_ref)
+    def one(places):
+        for z in places:
+            add_loss(z, dlogit_ref, head, g_ref)
+        mix_sums(places, g_ref, pre_ref, total_ref)
 
     some(early, blocks, blocks, one)
     mine_ref[...] = g_ref[lax.axis_index("seq") // SPAN]
     split_pair(g_ref.shape[2] // blocks, total_ref, own_ref, send_ref)
 
 
+def long_conv_sums(blocks, group_size, mid_ref, d_ref, fold, total_ref, columns):
+    row_count, channels = mid_ref.shape[1:]
+    rows = blocks * row_count
+    _, wide, first_slab = pair_slabs(channels, blocks)
+    for i in range(wide):
+        slab = first_slab + i
+        taps = [mid_ref[2 - k : 2 - k + blocks, :, lanes(slab)].reshape(rows, SLAB) for k in range(3)]
+        dpre_part = d_ref[:blocks, :, lanes(slab, 2 * SLAB)].reshape(rows, 2 * SLAB)
+        total_ref[cut(i), columns] = weight_sums(group_size, taps, dpre_part, fold[...])
+
+
 def long_kernel(blocks, early, group_size, g_ref, mid_ref, pre_ref, weights, mixes, fold, *refs):
-    between_ref, own_ref, send_ref, d_ref, total_ref = refs[-5:]
+    between_ref, last_ref = refs[-3:-1] if early else refs[:2]
+    d_ref = last_ref if early else refs[2]
     row_count, channels = g_ref.shape[1:]
     slabs = channels // SLAB
-    pair, wide, first_slab = pair_slabs(channels, blocks)
     d_ref[blocks:] = jnp.zeros((SPAN,) + d_ref.shape[1:], BF16)
-    some(early, blocks, blocks, lambda z: gate_cotangent(z, g_ref, pre_ref, mixes, d_ref))
+    some(early, blocks, blocks, lambda places: gate_cotangent(places, g_ref, pre_ref, mixes, d_ref))
 
     def back(first, count):
         rows = count * row_count
@@ -296,13 +324,8 @@
             between_ref[here, :, cut(slab)] = total.astype(BF16).reshape(count, row_count, SLAB)
 
     chunks(blocks, back)
-    rows = blocks * row_count
-    for i in range(wide):
-        slab = first_slab + i
-        taps = [mid_ref[2 - k : 2 - k + blocks, :, lanes(slab)].reshape(rows, SLAB) for k in range(3)]
-        dpre_part = d_ref[:blocks, :, lanes(slab, 2 * SLAB)].reshape(rows, 2 * SLAB)
-        total_ref[cut(i), :] = weight_sums(group_size, taps, dpre_part, fold[...])
-    split_pair(pair, total_ref, own_ref, send_ref)
+    if not early:
+        long_conv_sums(blocks, group_size, mid_ref, d_ref, fold, last_ref, slice(0, SLAB))
 
 
 def own_kernel(x_ref, between_ref, weights, mixes, push_ref, sum_ref):
@@ -325,7 +348,8 @@
             sum_ref[:, cut(slab)] = between_ref[z, :, cut(slab)].astype(F32) + moved[0] + extended[HALO:]
 
 
-def short_kernel(blocks, group_size, x_ref, between_ref, weights, mixes, fold, own_ref, send_ref, total_ref):
+def short_kernel(blocks, group_size, x_ref, between_ref, weights, mixes, fold, *refs):
+    *long_refs, _, _, own_ref, send_ref, total_ref = refs
     row_count, channels = between_ref.shape[1:]
     pair, wide, first_slab = pair_slabs(channels, blocks)
     rows = blocks * row_count
@@ -339,30 +363,45 @@
         tanh, sig = gates(conv(taps, weights[0, slab]))
         dpre = gate_grad(tanh, sig, nt(between, mixes[0, lanes(slab), :]))
         total_ref[cut(i), :channels] = tn((tanh * sig).astype(BF16), between)
-        total_ref[cut(i), channels:] = weight_sums(group_size, taps, dpre, fold[...])
+        total_ref[cut(i), channels : channels + SLAB] = weight_sums(group_size, taps, dpre, fold[...])
+    last = slice(channels + SLAB, channels + 2 * SLAB)
+    if len(long_refs) > 1:
+        long_conv_sums(blocks, group_size, *long_refs, fold, total_ref, last)
+    else:
+        total_ref[:, last] = long_refs[0][...]
     split_pair(pair, total_ref, own_ref, send_ref)
 
 
-def finish_kernel(group_size, mix1, conv1, own0, got_mix1, got_conv1, got0, mix_ref, conv_ref):
+def finish_kernel(group_size, mix1, own0, got_mix1, got0, mix_ref, conv_ref):
     channels = mix_ref.shape[2]
     width = 2 * group_size
     total = own0[...] + got0[...].astype(F32)
     mix_ref[:, 0, :] = total[:, :channels]
     mix_ref[:, 1, :] = mix1[...] + got_mix1[...].astype(F32)
-    convs = (total[:, channels:], conv1[...] + got_conv1[...].astype(F32))
     for layer in range(2):
         for k in range(3):
-            conv_ref[layer, k] = convs[layer][:, width * k : width * (k + 1)]
+            begin = channels + SLAB * layer + width * k
+            conv_ref[layer, k] = total[:, begin : begin + width]
+
+
+def add_kernel(own_ref, pushed_ref, out_ref):
+    rest = out_ref.shape[0] - HALO
+    out_ref[:rest, :] = own_ref[:rest, :].astype(BF16)
+    out_ref[rest:, :] = (own_ref[rest:, :] + pushed_ref[...].astype(F32)).astype(BF16)
+
+
+def choose_kernel(last_ref, other_ref, out_ref):
+    out_ref[...] = jnp.where(on_last_section(), last_ref[...].astype(F32), other_ref[...].astype(F32)).astype(BF16)
 
 
 VMEM = pl.BlockSpec(memory_space=pltpu.VMEM)
 ANY = pl.BlockSpec(memory_space=pl.ANY)
 
 
-def call(resident, kernel, outs, arrays, scratch=(), name=None, aliases={}, far=(), near=True, us=0.1):
+def call(resident, kernel, outs, arrays, scratch=(), name=None, aliases={}, far=(), near=True, final=False, us=0.1):
     if resident and near:
         arrays = [a if i in far else pltpu.with_memory_space_constraint(a, pltpu.VMEM) for i, a in enumerate(arrays)]
-    make = pltpu.VMEM if resident and near and name != "finish" else jax.ShapeDtypeStruct
+    make = pltpu.VMEM if resident and near and not final else jax.ShapeDtypeStruct
     return pl.pallas_call(
         kernel,
         out_shape=[make(shape, kind) for shape, kind in outs],
@@ -371,7 +410,7 @@
         scratch_shapes=[pltpu.VMEM(*s) if isinstance(s, tuple) else s for s in scratch],
         input_output_aliases=aliases,
         compiler_params=pltpu.CompilerParams(vmem_limit_bytes=(24 if resident else 56) * 1024 * 1024),
-        cost_estimate=pl.CostEstimate(flops=int(us * 1.1e9), bytes_accessed=0, transcendentals=0),
+        cost_estimate=pl.CostEstimate(flops=int(us * SCALE * 1.1e9), bytes_accessed=0, transcendentals=0),
         name=name,
     )(*arrays)
 
@@ -396,8 +435,6 @@
     def swap(value):
         return lax.ppermute(value, "seq", [(b, b + 1 - 2 * (b % 2)) for b in range(seq)])
 
-    is_last = on_last_section()
-
     def direct(value, steps):
         pairs = [(source, source) for source in range(blocks)]
         for _ in range(steps):
@@ -406,48 +443,60 @@
 
     resident = blocks <= 4
     run = functools.partial(call, resident)
-    def tail(value):
-        (out,) = run(tail_kernel, [((HALO, channels), BF16)], [value], name="tail", us=0.3)
-        return out
-
-    head = hazard_head.T
+    def relay(value, *others):
+        return run(
+            relay_kernel,
+            [((HALO, channels), BF16), ((row_count, channels), BF16)],
+            [value, *others],
+            [pltpu.SemaphoreType.DMA((1,))],
+            name="relay",
+            far=range(1, 1 + len(others)),
+            us=0.3,
+        )
+
+    def far(value):
+        return pltpu.with_memory_space_constraint(value, pltpu.HBM) if resident else value
+
+    head = far(hazard_head.T)
     tails = [swap(first_input[row_count - HALO :])]
     codes = [jnp.stack([labels, events])]
-    weights, fold = run(
+    taps = far(kernel_weight[0].transpose(0, 1, 3, 4, 2).reshape(2, 3, -1, groups))
+    mixes, far_cot = far(blend_weight[0]), far(cot)
+    weights, fold, mixes, head, own_cot = run(
         functools.partial(weight_kernel, group_size),
-        [((2, slabs, 3 * SLAB, 2 * SLAB), BF16), ((SLAB, 6 * SLAB), BF16)],
-        [kernel_weight[0].reshape(-1, 2 * group_size)],
+        [((2, slabs, 3 * SLAB, 2 * SLAB), BF16), ((SLAB, 6 * SLAB), BF16), (mixes.shape, BF16), (head.shape, BF16), (cot.shape, BF16)],
+        [taps, mixes, head, far_cot],
+        [(taps.shape, BF16), pltpu.SemaphoreType.DMA((4,))],
         name="weights",
-        near=False,
-        us=1.3,
+        far=(0, 1, 2, 3),
+        us=3.5,
     )
     inputs, cots = [first_input], [cot]
+    codes += [direct(codes[0], p) for p in range(1, blocks)]
+    before = {1: [tails[0], fold], 2: codes[1:]}
+    sent_input = first_input
+    cots.append(step(own_cot))
     for p in range(1, blocks):
-        inputs.append(step(inputs[-1]))
-        tails.append(swap(tail(inputs[-1])))
-        codes.append(direct(codes[0], p))
-        cots.append(step(cots[-1]))
-    mixes = blend_weight[0]
+        inputs.append(step(sent_input))
+        if p > 1:
+            cots.append(step(cots[-1]))
+        tail, sent_input = relay(inputs[-1], *before.get(p, []))
+        tails.append(swap(tail))
     rows = min(blocks, 4) * row_count
-    held = [(a.shape, BF16) for a in (weights, mixes, head)]
-    x, mid, pre, dlogit, *kept = run(
+    x, mid, pre, dlogit = run(
         functools.partial(forward_kernel, blocks),
         [
             ((blocks + 1, HALO + row_count, channels), BF16),
             ((blocks + SPAN, row_count, channels), BF16),
             ((blocks, row_count, 2 * channels), BF16),
             ((blocks, head.shape[0], row_count), BF16),
-        ]
-        + held * resident,
-        [*inputs, *tails, *codes, weights, mixes, head],
-        held * (not resident)
-        + [((rows, channels), BF16), ((blocks, 2, row_count), jnp.int32), pltpu.SemaphoreType.DMA((2 * blocks + 5,))],
+        ],
+        [far(first_input), *inputs[1:], *tails, *codes, weights, mixes, head],
+        [((rows, channels), BF16), ((blocks, 2, row_count), jnp.int32), pltpu.SemaphoreType.DMA((2 * blocks,))],
         name="forward",
-        far=[*range(2 * blocks), *range(3 * blocks, 3 * blocks + 3)],
+        far=range(2 * blocks),
         us=5,
     )
-    if resident:
-        weights, mixes, head = kept
     wide = max(channels // blocks, SLAB)
     block_rows = ((blocks, row_count, channels), BF16)
     early = blocks - 1 if resident else 0
@@ -456,7 +505,7 @@
         g, d, total = run(
             functools.partial(early_kernel, blocks, early),
             [block_rows, d_rows, ((wide, channels), F32)],
-            [*cots[:early], pre, dlogit, head, mixes],
+            [far_cot, *cots[1:early], pre, dlogit, head, mixes],
             [pltpu.SemaphoreType.DMA((early,))],
             name="early",
             far=range(early),
@@ -474,16 +523,15 @@
         us=0.7,
     )
     got_mix1 = swap(send_mix1)
-    between, conv1, send_conv1, *_ = run(
+    between, last = run(
         functools.partial(long_kernel, blocks, early, group_size),
-        [block_rows, ((share, SLAB), F32), ((share, SLAB), BF16)] + ([d_rows] if early else []),
+        [block_rows, d_rows if early else ((wide, SLAB), F32)],
         [g, mid, pre, weights, mixes, fold] + ([d] if early else []),
-        ([] if early else [d_rows]) + [((wide, SLAB), F32)],
+        [((8, SLAB), F32) if early else d_rows],
         name="long_backward",
-        aliases={6: 3} if early else {},
+        aliases={6: 1} if early else {},
         us=3.4,
     )
-    got_conv1 = swap(send_conv1)
     push, own_sum = run(
         own_kernel,
         [((HALO, channels), BF16), ((row_count, channels), F32)],
@@ -492,26 +540,28 @@
         us=2.7,
     )
     pushed = lax.ppermute(push, "seq", [(b, b - 1) for b in range(1, seq)])
+    sums = channels + 2 * SLAB
     own0, send0 = run(
         functools.partial(short_kernel, blocks, group_size),
-        [((share, channels + SLAB), F32), ((share, channels + SLAB), BF16)],
-        [x, between, weights, mixes, fold],
-        [((wide, channels + SLAB), F32)],
+        [((share, sums), F32), ((share, sums), BF16)],
+        [x, between, weights, mixes, fold] + ([mid, last] if early else [last]) + [push, got_mix1],
+        [((wide, sums), F32)],
         name="short_backward",
+        far=(7, 8) if early else (6, 7),
         us=2.5,
     )
     got0 = swap(send0)
-    input_gradient = jnp.concatenate(
-        [own_sum[: row_count - HALO], own_sum[row_count - HALO :] + pushed.astype(F32)], axis=0
-    ).astype(BF16)
+    rows_out = ((row_count, channels), BF16)
+    (input_gradient,) = run(add_kernel, [rows_out], [own_sum, pushed], name="add", final=True, us=0.4)
     count = lax.axis_size("section")
     received = lax.ppermute(input_gradient, "section", [(s, s - 1) for s in range(1, count)])
-    next_cot = jnp.where(is_last, mine, received)
+    (next_cot,) = run(choose_kernel, [rows_out], [mine, received], name="choose", final=True, us=0.4)
     mix_share, conv_share = run(
         functools.partial(finish_kernel, group_size),
         [((share, 2, channels), F32), ((2, 3, share, 2 * group_size), F32)],
-        [mix1, conv1, own0, got_mix1, got_conv1, got0],
+        [mix1, own0, got_mix1, got0],
         name="finish",
+        final=True,
         us=1.4,
     )
     conv_share = conv_share.reshape(2, 3, share // group_size, group_size, 2 * group_size)

time: 85.9 us -> 73.8 us (0.86)
  the two profiles are of different devices: /device:TPU:14 before, /device:TPU:1 now
where the time goes in v3:
time: 73.8 us; the launch traced here: 73.6 us
  starting transfers between devices  27.6 us (37%)
  Pallas kernels  25 us (34%)
  waiting for transfers between devices  19.3 us (26%)
  local copies, waits for them, and re-layouts  0.88 us (1%)
  between operations  0.77 us (1%)
    pallas_call x13, Pallas kernels, call(): pl.pallas_call(kernel, out_shape=[make(shape, kind) for shape, kind in ou...  25 us
    ppermute x6, starting transfers between devices, step(): lax.ppermute(value, 'seq', [(a * SPAN + y, b * SPAN + y) for a, b in hops...  8.37 us
    ppermute x1, starting transfers between devices, body(): lax.ppermute(input_gradient, 'section', [(s, s - 1) for s in range(1, cou...  8.35 us
    ppermute x3, waiting for transfers between devices, direct(): lax.ppermute(value, 'seq', [(a * SPAN + y, b * SPAN + y) for a, b in pair...  7.94 us
    ppermute x6, starting transfers between devices, swap(): lax.ppermute(value, 'seq', [(b, b + 1 - 2 * (b % 2)) for b in range(seq)])  7.36 us
    ppermute x6, waiting for transfers between devices, step(): lax.ppermute(value, 'seq', [(a * SPAN + y, b * SPAN + y) for a, b in hops...  6.02 us
    ppermute x1, waiting for transfers between devices, body(): lax.ppermute(input_gradient, 'section', [(s, s - 1) for s in range(1, cou...  5.35 us
    ppermute x3, starting transfers between devices, direct(): lax.ppermute(value, 'seq', [(a * SPAN + y, b * SPAN + y) for a, b in pair...  2.2 us
  transfers between devices with their start and end apart: 17, of which 6 were waited for; matrix products, arithmetic and copies ran while one was open for 1% of the time, Pallas kernels for 31%

profile of v3, /device:TPU:1, one launch (start us, length us, event | category | flops | bytes accessed | tf_op | source)
XLA Modules:
  0.0 73.6 jit_solution(8243296041738075256)
XLA Ops:
  0.6 2.2 %collective-permute-start = (bf16[128,1024]{1,0:T(8,128)(2,1)}, bf16[128,1024]{1,0:T(8,128)(2,1)S(1)}, u32[]{:S(2)}, u32[]{:S(2)}) collective-permute-start(bf16[128,1024]{1,0:T(8,128)(2,1)} %bitcast.18), channel_id=1, source_target_pairs={{0,2},{1,3},{2,6},{3,7},{6,4},{7,5},{4,0},{5,1},{8,10},{9,11},{10,... | collective-permute-start | bytes 786440 | tf_op jit(solution)/shard_map/ppermute | solution.py:431
  2.8 0.9 %slice_bitcast_fusion = bf16[32,1024]{1,0:T(8,128)(2,1)S(1)} fusion(bf16[1,128,1024]{2,1,0:T(8,128)(2,1)} %param.7), kind=kLoop, calls=%fused_computation | loop fusion | bytes 131072 | tf_op jit(solution)/shard_map/slice | solution.py:461
  3.7 1.2 %collective-permute-start.1 = (bf16[32,1024]{1,0:T(8,128)(2,1)S(1)}, bf16[32,1024]{1,0:T(8,128)(2,1)S(1)}, u32[]{:S(2)}, u32[]{:S(2)}) collective-permute-start(bf16[32,1024]{1,0:T(8,128)(2,1)S(1)} %slice_bitcast_fusion), channel_id=1, source_target_pairs={{0,1},{1,0},{2,3},{3,2},{4,5},{5,4},{6,7},{7,6},{8,9},{9,8},{10,11... | collective-permute-start | bytes 196616 | tf_op jit(solution)/shard_map/ppermute | solution.py:436
  4.9 4.8 %weights.1 = (bf16[2,8,384,256]{3,2,1,0:T(8,128)(2,1)S(1)}, bf16[128,768]{1,0:T(8,128)(2,1)S(1)}, bf16[2,1024,1024]{2,1,0:T(8,128)(2,1)S(1)}, bf16[64,1024]{1,0:T(8,128)(2,1)S(1)}, bf16[128,1024]{1,0:T(8,128)(2,1)S(1)}) custom-call(bf16[2,3,512,64]{3,2,1,0:T(8,128)(2,1)} %bitcast.23, bf16[2,1024,1024]{2,1,0:T(8,128)(2,1)} %bitcast.22, ...), custom_call_target="tpu_custom_call" | custom-call | flops 1924999936 | tf_op jit(solution)/shard_map/weights/pallas_call | solution.py:405
  9.7 0.0 collective-permute-done.1.refs_0_.refs_4_
  9.7 0.4 collective-permute-done.value.refs_1_
  10.1 2.0 %collective-permute-start.2 = (bf16[128,1024]{1,0:T(8,128)(2,1)S(1)}, bf16[128,1024]{1,0:T(8,128)(2,1)S(1)}, u32[]{:S(2)}, u32[]{:S(2)}) collective-permute-start(bf16[128,1024]{1,0:T(8,128)(2,1)S(1)} %get-tuple-element.34), channel_id=1, source_target_pairs={{0,2},{1,3},{2,6},{3,7},{6,4},{7,5},{4,0},{5,1},{8,10},{9,11},{10,... | collective-permute-start | bytes 786440 | tf_op jit(solution)/shard_map/ppermute | solution.py:431
  12.1 1.4 %collective-permute-start.10 = (bf16[128,1024]{1,0:T(8,128)(2,1)S(1)}, bf16[128,1024]{1,0:T(8,128)(2,1)S(1)}, u32[]{:S(2)}, u32[]{:S(2)}) collective-permute-start(bf16[128,1024]{1,0:T(8,128)(2,1)S(1)} %get-tuple-element.43), channel_id=1, source_target_pairs={{0,2},{1,3},{2,6},{3,7},{6,4},{7,5},{4,0},{5,1},{8,10},{9,11},{10,... | collective-permute-start | bytes 786440 | tf_op jit(solution)/shard_map/ppermute | solution.py:431
  13.5 0.0 copy-done
  13.5 0.0 copy-done.1
  13.5 1.0 %collective-permute-start.5 = (s32[2,128]{1,0:T(2,128)S(1)}, s32[2,128]{1,0:T(2,128)S(1)}, u32[]{:S(2)}, u32[]{:S(2)}) collective-permute-start(s32[2,128]{1,0:T(2,128)S(1)} %pad_add_fusion.refs_8_), channel_id=1, source_target_pairs={{0,4},{1,5},{2,0},{3,1},{4,6},{5,7},{6,2},{7,3},{8,12},{9,13},{10,... | collective-permute-start | bytes 3080 | tf_op jit(solution)/shard_map/ppermute | solution.py:442
  14.6 1.2 %collective-permute-start.4 = (s32[2,128]{1,0:T(2,128)S(1)}, s32[2,128]{1,0:T(2,128)S(1)}, u32[]{:S(2)}, u32[]{:S(2)}) collective-permute-start(s32[2,128]{1,0:T(2,128)S(1)} %pad_add_fusion.refs_8_), channel_id=1, source_target_pairs={{0,6},{1,7},{2,4},{3,5},{4,2},{5,3},{6,0},{7,1},{8,14},{9,15},{10,... | collective-permute-start | bytes 3080 | tf_op jit(solution)/shard_map/ppermute | solution.py:442
  15.7 0.0 collective-permute-start.3
  15.7 6.4 %collective-permute-done.5.refs_2_.refs_11_ = s32[2,128]{1,0:T(2,128)S(1)} collective-permute-done((s32[2,128]{1,0:T(2,128)S(1)}, s32[2,128]{1,0:T(2,128)S(1)}, u32[]{:S(2)}, u32[]{:S(2)}) %collective-permute-start.5) | collective-permute-done | bytes 1056 | tf_op jit(solution)/shard_map/ppermute | solution.py:442
  22.1 1.5 %collective-permute-done.4.refs_1_.refs_10_ = s32[2,128]{1,0:T(2,128)S(1)} collective-permute-done((s32[2,128]{1,0:T(2,128)S(1)}, s32[2,128]{1,0:T(2,128)S(1)}, u32[]{:S(2)}, u32[]{:S(2)}) %collective-permute-start.4) | collective-permute-done | bytes 1056 | tf_op jit(solution)/shard_map/ppermute | solution.py:442
  23.6 0.0 collective-permute-done.3.refs_0_.refs_9_
  23.7 0.0 collective-permute-done.2.value.refs_2_
  23.7 0.8 %collective-permute-start.6 = (bf16[128,1024]{1,0:T(8,128)(2,1)S(1)}, bf16[128,1024]{1,0:T(8,128)(2,1)S(1)}, u32[]{:S(2)}, u32[]{:S(2)}) collective-permute-start(bf16[128,1024]{1,0:T(8,128)(2,1)S(1)} %get-tuple-element.35), channel_id=1, source_target_pairs={{0,2},{1,3},{2,6},{3,7},{6,4},{7,5},{4,0},{5,1},{8,10},{9,11},{10,... | collective-permute-start | bytes 786440 | tf_op jit(solution)/shard_map/ppermute | solution.py:431
  24.5 0.0 collective-permute-done.10.refs_1_
  24.5 1.9 %collective-permute-start.11 = (bf16[128,1024]{1,0:T(8,128)(2,1)S(1)}, bf16[128,1024]{1,0:T(8,128)(2,1)S(1)}, u32[]{:S(2)}, u32[]{:S(2)}) collective-permute-start(bf16[128,1024]{1,0:T(8,128)(2,1)S(1)} %collective-permute-done.10.refs_1_), channel_id=1, source_target_pairs={{0,2},{1,3},{2,6},{3,7},{6,4},{7,5},{4,0},{5,1},{8,10},{9,11},{10,... | collective-permute-start | bytes 786440 | tf_op jit(solution)/shard_map/ppermute | solution.py:431
  26.4 1.3 %collective-permute-start.7 = (bf16[32,1024]{1,0:T(8,128)(2,1)S(1)}, bf16[32,1024]{1,0:T(8,128)(2,1)S(1)}, u32[]{:S(2)}, u32[]{:S(2)}) collective-permute-start(bf16[32,1024]{1,0:T(8,128)(2,1)S(1)} %get-tuple-element.36), channel_id=1, source_target_pairs={{0,1},{1,0},{2,3},{3,2},{4,5},{5,4},{6,7},{7,6},{8,9},{9,8},{10,11... | collective-permute-start | bytes 196616 | tf_op jit(solution)/shard_map/ppermute | solution.py:436
  27.7 0.2 collective-permute-start.8
  27.9 2.0 %collective-permute-done.6.value.refs_3_ = bf16[128,1024]{1,0:T(8,128)(2,1)S(1)} collective-permute-done((bf16[128,1024]{1,0:T(8,128)(2,1)S(1)}, bf16[128,1024]{1,0:T(8,128)(2,1)S(1)}, u32[]{:S(2)}, u32[]{:S(2)}) %collective-permute-start.6) | collective-permute-done | bytes 262176 | tf_op jit(solution)/shard_map/ppermute | solution.py:431
  29.9 0.7 relay.5
  30.6 1.3 %collective-permute-start.9 = (bf16[32,1024]{1,0:T(8,128)(2,1)S(1)}, bf16[32,1024]{1,0:T(8,128)(2,1)S(1)}, u32[]{:S(2)}, u32[]{:S(2)}) collective-permute-start(bf16[32,1024]{1,0:T(8,128)(2,1)S(1)} %get-tuple-element.38), channel_id=1, source_target_pairs={{0,1},{1,0},{2,3},{3,2},{4,5},{5,4},{6,7},{7,6},{8,9},{9,8},{10,11... | collective-permute-start | bytes 196616 | tf_op jit(solution)/shard_map/ppermute | solution.py:436
  31.9 3.7 %collective-permute-done.11.refs_2_ = bf16[128,1024]{1,0:T(8,128)(2,1)S(1)} collective-permute-done((bf16[128,1024]{1,0:T(8,128)(2,1)S(1)}, bf16[128,1024]{1,0:T(8,128)(2,1)S(1)}, u32[]{:S(2)}, u32[]{:S(2)}) %collective-permute-start.11) | collective-permute-done | bytes 262176 | tf_op jit(solution)/shard_map/ppermute | solution.py:431
  35.6 0.1 collective-permute-start.12
  35.7 0.0 collective-permute-done.7.refs_5_
  35.7 0.0 collective-permute-done.8.refs_6_
  35.7 0.0 collective-permute-done.9.refs_7_
  35.7 4.6 %forward.1 = (bf16[5,160,1024]{2,1,0:T(8,128)(2,1)S(1)}, bf16[6,128,1024]{2,1,0:T(8,128)(2,1)S(1)}, bf16[4,128,2048]{2,1,0:T(8,128)(2,1)S(1)}, bf16[4,64,128]{2,1,0:T(8,128)(2,1)S(1)}) custom-call(bf16[128,1024]{1,0:T(8,128)(2,1)} %bitcast.19, bf16[128,1024]{1,0:T(8,128)(2,1)S(1)} %collective-permute-done.value.refs_1_, ...), custom_call_target="tpu_custom_call" | custom-call | flops 2750000128 | tf_op jit(solution)/shard_map/forward/pallas_call | solution.py:405
  40.3 3.0 %early.1 = (bf16[4,128,1024]{2,1,0:T(8,128)(2,1)S(1)}, bf16[6,128,2048]{2,1,0:T(8,128)(2,1)S(1)}, f32[256,1024]{1,0:T(8,128)S(1)}) custom-call(bf16[128,1024]{1,0:T(8,128)(2,1)} %bitcast.25, bf16[128,1024]{1,0:T(8,128)(2,1)S(1)} %collective-permute-done.10.refs_1_, bf16[128,1024]{1,0:T(8,128)(2,1)S(1)} %collective-permute-done.11.refs_2_, ...), custom_call_target="tpu_custom_call" | custom-call | flops 2200000000 | tf_op jit(solution)/shard_map/early/pallas_call | solution.py:405
  43.3 0.0 collective-permute-done.12.refs_0_
  43.3 0.6 long_mix.1
  43.9 1.2 %collective-permute-start.15 = (bf16[128,1024]{1,0:T(8,128)(2,1)S(1)}, bf16[128,1024]{1,0:T(8,128)(2,1)S(1)}, u32[]{:S(2)}, u32[]{:S(2)}) collective-permute-start(bf16[128,1024]{1,0:T(8,128)(2,1)S(1)} %get-tuple-element.57), channel_id=1, source_target_pairs={{0,1},{1,0},{2,3},{3,2},{4,5},{5,4},{6,7},{7,6},{8,9},{9,8},{10,11... | collective-permute-start | bytes 786440 | tf_op jit(solution)/shard_map/ppermute | solution.py:436
  45.1 2.7 %long_backward.1 = (bf16[4,128,1024]{2,1,0:T(8,128)(2,1)S(1)}, bf16[6,128,2048]{2,1,0:T(8,128)(2,1)S(1)}) custom-call(bf16[4,128,1024]{2,1,0:T(8,128)(2,1)S(1)} %get-tuple-element.48.g_ref, bf16[6,128,1024]{2,1,0:T(8,128)(2,1)S(1)} %get-tuple-element.49.mid_ref.refs_0_, ...), custom_call_target="tpu_custom_call", output_to_operand_aliasing={{1}: (6, {})} | custom-call | flops 1870000000 | tf_op jit(solution)/shard_map/long_backward/pallas_call | solution.py:405
  47.9 2.7 %own_backward.1 = (bf16[32,1024]{1,0:T(8,128)(2,1)S(1)}, f32[128,1024]{1,0:T(8,128)S(1)}) custom-call(bf16[5,160,1024]{2,1,0:T(8,128)(2,1)S(1)} %get-tuple-element.42.x_ref, bf16[4,128,1024]{2,1,0:T(8,128)(2,1)S(1)} %get-tuple-element.51.between_ref, bf16[2,8,384,256]{3,2,1,0:T(8,128)(2,1)S(1)} %get-tuple-element.39.refs_12_.weights, ...), custom_call_target="tpu_custom_call" | custom-call | flops 1484999936 | tf_op jit(solution)/shard_map/own_backward/pallas_call | solution.py:405
  50.6 1.3 %collective-permute-start.13 = (bf16[32,1024]{1,0:T(8,128)(2,1)S(1)}, bf16[32,1024]{1,0:T(8,128)(2,1)S(1)}, u32[]{:S(2)}, u32[]{:S(2)}) collective-permute-start(bf16[32,1024]{1,0:T(8,128)(2,1)S(1)} %get-tuple-element.53.refs_2_), channel_id=1, source_target_pairs={{1,0},{2,1},{3,2},{4,3},{5,4},{6,5},{7,6},{9,8},{10,9},{11,10},{12... | collective-permute-start | bytes 196616 | tf_op jit(solution)/shard_map/ppermute | solution.py:542
  51.9 0.0 collective-permute-done.15.refs_3_.got_mix1
  51.9 2.9 %short_backward.1 = (f32[128,1280]{1,0:T(8,128)S(1)}, bf16[128,1280]{1,0:T(8,128)(2,1)S(1)}) custom-call(bf16[5,160,1024]{2,1,0:T(8,128)(2,1)S(1)} %get-tuple-element.42.x_ref, bf16[4,128,1024]{2,1,0:T(8,128)(2,1)S(1)} %get-tuple-element.51.between_ref, bf16[2,8,384,256]{3,2,1,0:T(8,128)(2,1)S(1)} %get-tuple-element.39.refs_12_.weights, ...), custom_call_target="tpu_custom_call" | custom-call | flops 1375000064 | tf_op jit(solution)/shard_map/short_backward/pallas_call | solution.py:405
  54.8 2.2 %collective-permute-start.16 = (bf16[128,1280]{1,0:T(8,128)(2,1)S(1)}, bf16[128,1280]{1,0:T(8,128)(2,1)S(1)}, u32[]{:S(2)}, u32[]{:S(2)}) collective-permute-start(bf16[128,1280]{1,0:T(8,128)(2,1)S(1)} %get-tuple-element.59), channel_id=1, source_target_pairs={{0,1},{1,0},{2,3},{3,2},{4,5},{5,4},{6,7},{7,6},{8,9},{9,8},{10,11... | collective-permute-start | bytes 983048 | tf_op jit(solution)/shard_map/ppermute | solution.py:436
  57.0 0.0 collective-permute-done.13.pushed_ref
  57.0 0.7 add.3
  57.7 8.3 %collective-permute-start.14 = (bf16[128,1024]{1,0:T(8,128)(2,1)}, bf16[128,1024]{1,0:T(8,128)(2,1)S(1)}, u32[]{:S(2)}, u32[]{:S(2)}) collective-permute-start(bf16[128,1024]{1,0:T(8,128)(2,1)} %add.3), channel_id=1, source_target_pairs={{8,0},{16,8},{24,16},{9,1},{17,9},{25,17},{10,2},{18,10},{26,18},{... | collective-permute-start | bytes 786440 | tf_op jit(solution)/shard_map/ppermute | solution.py:557
  66.1 5.3 %collective-permute-done.14.other_ref = bf16[128,1024]{1,0:T(8,128)(2,1)S(1)} collective-permute-done((bf16[128,1024]{1,0:T(8,128)(2,1)}, bf16[128,1024]{1,0:T(8,128)(2,1)S(1)}, u32[]{:S(2)}, u32[]{:S(2)}) %collective-permute-start.14) | collective-permute-done | bytes 262176 | tf_op jit(solution)/shard_map/ppermute | solution.py:557
  71.4 0.8 %choose.1 = bf16[128,1024]{1,0:T(8,128)(2,1)} custom-call(bf16[128,1024]{1,0:T(8,128)(2,1)S(1)} %get-tuple-element.54.last_ref, bf16[128,1024]{1,0:T(8,128)(2,1)S(1)} %collective-permute-done.14.other_ref), custom_call_target="tpu_custom_call" | custom-call | flops 220000000 | tf_op jit(solution)/shard_map/choose/pallas_call | solution.py:405
  72.2 0.0 collective-permute-done.16.got0
  72.2 1.4 %finish.1 = (f32[128,2,1024]{2,1,0:T(2,128)}, f32[2,3,128,32]{3,2,1,0:T(8,128)}) custom-call(f32[128,1024]{1,0:T(8,128)S(1)} %get-tuple-element.55.mix1, f32[128,1280]{1,0:T(8,128)S(1)} %get-tuple-element.58.own0, bf16[128,1024]{1,0:T(8,128)(2,1)S(1)} %collective-permute-done.15.refs_3_.got_mix1, bf16[128,1280]{1,0:T(8,128)(2,1)S(1)} %collective-permute-done.16.got0), custom_call_target="tpu_custom_call" | custom-call | flops 770000000 | tf_op jit(solution)/shard_map/finish/pallas_call | solution.py:405
  (5 shorter events, 0.1 us)
Async XLA Ops:
  0.6 9.4 %collective-permute-start = (bf16[128,1024]{1,0:T(8,128)(2,1)}, bf16[128,1024]{1,0:T(8,128)(2,1)S(1)}, u32[]{:S(2)}, u32[]{:S(2)}) collective-permute-start(bf16[128,1024]{1,0:T(8,128)(2,1)} %bitcast.18), channel_id=1, source_target_pairs={{0,2},{1,3},{2,6},{3,7},{6,4},{7,5},{4,0},{5,1},{8,10},{9,11},{10,... | collective-permute-start | bytes 786440 | tf_op jit(solution)/shard_map/ppermute | solution.py:431
  3.7 6.0 %collective-permute-start.1 = (bf16[32,1024]{1,0:T(8,128)(2,1)S(1)}, bf16[32,1024]{1,0:T(8,128)(2,1)S(1)}, u32[]{:S(2)}, u32[]{:S(2)}) collective-permute-start(bf16[32,1024]{1,0:T(8,128)(2,1)S(1)} %slice_bitcast_fusion), channel_id=1, source_target_pairs={{0,1},{1,0},{2,3},{3,2},{4,5},{5,4},{6,7},{7,6},{8,9},{9,8},{10,11... | collective-permute-start | bytes 196616 | tf_op jit(solution)/shard_map/ppermute | solution.py:436
  4.9 8.6 %copy-start = (s32[128]{0:T(128)S(1)}, s32[128]{0:T(128)}, u32[]{:S(2)}) copy-start(s32[128]{0:T(128)} %param.13) | copy-start | bytes 1540
  4.9 8.6 %copy-start.1 = (s32[128]{0:T(128)S(1)}, s32[128]{0:T(128)}, u32[]{:S(2)}) copy-start(s32[128]{0:T(128)} %param.12) | copy-start | bytes 1540
  10.1 13.5 %collective-permute-start.2 = (bf16[128,1024]{1,0:T(8,128)(2,1)S(1)}, bf16[128,1024]{1,0:T(8,128)(2,1)S(1)}, u32[]{:S(2)}, u32[]{:S(2)}) collective-permute-start(bf16[128,1024]{1,0:T(8,128)(2,1)S(1)} %get-tuple-element.34), channel_id=1, source_target_pairs={{0,2},{1,3},{2,6},{3,7},{6,4},{7,5},{4,0},{5,1},{8,10},{9,11},{10,... | collective-permute-start | bytes 786440 | tf_op jit(solution)/shard_map/ppermute | solution.py:431
  12.1 12.3 %collective-permute-start.10 = (bf16[128,1024]{1,0:T(8,128)(2,1)S(1)}, bf16[128,1024]{1,0:T(8,128)(2,1)S(1)}, u32[]{:S(2)}, u32[]{:S(2)}) collective-permute-start(bf16[128,1024]{1,0:T(8,128)(2,1)S(1)} %get-tuple-element.43), channel_id=1, source_target_pairs={{0,2},{1,3},{2,6},{3,7},{6,4},{7,5},{4,0},{5,1},{8,10},{9,11},{10,... | collective-permute-start | bytes 786440 | tf_op jit(solution)/shard_map/ppermute | solution.py:431
  13.5 8.6 %collective-permute-start.5 = (s32[2,128]{1,0:T(2,128)S(1)}, s32[2,128]{1,0:T(2,128)S(1)}, u32[]{:S(2)}, u32[]{:S(2)}) collective-permute-start(s32[2,128]{1,0:T(2,128)S(1)} %pad_add_fusion.refs_8_), channel_id=1, source_target_pairs={{0,4},{1,5},{2,0},{3,1},{4,6},{5,7},{6,2},{7,3},{8,12},{9,13},{10,... | collective-permute-start | bytes 3080 | tf_op jit(solution)/shard_map/ppermute | solution.py:442
  14.6 9.1 %collective-permute-start.4 = (s32[2,128]{1,0:T(2,128)S(1)}, s32[2,128]{1,0:T(2,128)S(1)}, u32[]{:S(2)}, u32[]{:S(2)}) collective-permute-start(s32[2,128]{1,0:T(2,128)S(1)} %pad_add_fusion.refs_8_), channel_id=1, source_target_pairs={{0,6},{1,7},{2,4},{3,5},{4,2},{5,3},{6,0},{7,1},{8,14},{9,15},{10,... | collective-permute-start | bytes 3080 | tf_op jit(solution)/shard_map/ppermute | solution.py:442
  15.7 7.9 %collective-permute-start.3 = (s32[2,128]{1,0:T(2,128)S(1)}, s32[2,128]{1,0:T(2,128)S(1)}, u32[]{:S(2)}, u32[]{:S(2)}) collective-permute-start(s32[2,128]{1,0:T(2,128)S(1)} %pad_add_fusion.refs_8_), channel_id=1, source_target_pairs={{0,2},{1,3},{2,6},{3,7},{4,0},{5,1},{6,4},{7,5},{8,10},{9,11},{10,... | collective-permute-start | bytes 3080 | tf_op jit(solution)/shard_map/ppermute | solution.py:442
  23.7 6.2 %collective-permute-start.6 = (bf16[128,1024]{1,0:T(8,128)(2,1)S(1)}, bf16[128,1024]{1,0:T(8,128)(2,1)S(1)}, u32[]{:S(2)}, u32[]{:S(2)}) collective-permute-start(bf16[128,1024]{1,0:T(8,128)(2,1)S(1)} %get-tuple-element.35), channel_id=1, source_target_pairs={{0,2},{1,3},{2,6},{3,7},{6,4},{7,5},{4,0},{5,1},{8,10},{9,11},{10,... | collective-permute-start | bytes 786440 | tf_op jit(solution)/shard_map/ppermute | solution.py:431
  24.5 11.1 %collective-permute-start.11 = (bf16[128,1024]{1,0:T(8,128)(2,1)S(1)}, bf16[128,1024]{1,0:T(8,128)(2,1)S(1)}, u32[]{:S(2)}, u32[]{:S(2)}) collective-permute-start(bf16[128,1024]{1,0:T(8,128)(2,1)S(1)} %collective-permute-done.10.refs_1_), channel_id=1, source_target_pairs={{0,2},{1,3},{2,6},{3,7},{6,4},{7,5},{4,0},{5,1},{8,10},{9,11},{10,... | collective-permute-start | bytes 786440 | tf_op jit(solution)/shard_map/ppermute | solution.py:431
  26.4 9.3 %collective-permute-start.7 = (bf16[32,1024]{1,0:T(8,128)(2,1)S(1)}, bf16[32,1024]{1,0:T(8,128)(2,1)S(1)}, u32[]{:S(2)}, u32[]{:S(2)}) collective-permute-start(bf16[32,1024]{1,0:T(8,128)(2,1)S(1)} %get-tuple-element.36), channel_id=1, source_target_pairs={{0,1},{1,0},{2,3},{3,2},{4,5},{5,4},{6,7},{7,6},{8,9},{9,8},{10,11... | collective-permute-start | bytes 196616 | tf_op jit(solution)/shard_map/ppermute | solution.py:436
  27.7 8.0 %collective-permute-start.8 = (bf16[32,1024]{1,0:T(8,128)(2,1)S(1)}, bf16[32,1024]{1,0:T(8,128)(2,1)S(1)}, u32[]{:S(2)}, u32[]{:S(2)}) collective-permute-start(bf16[32,1024]{1,0:T(8,128)(2,1)S(1)} %get-tuple-element.37), channel_id=1, source_target_pairs={{0,1},{1,0},{2,3},{3,2},{4,5},{5,4},{6,7},{7,6},{8,9},{9,8},{10,11... | collective-permute-start | bytes 196616 | tf_op jit(solution)/shard_map/ppermute | solution.py:436
  30.6 5.1 %collective-permute-start.9 = (bf16[32,1024]{1,0:T(8,128)(2,1)S(1)}, bf16[32,1024]{1,0:T(8,128)(2,1)S(1)}, u32[]{:S(2)}, u32[]{:S(2)}) collective-permute-start(bf16[32,1024]{1,0:T(8,128)(2,1)S(1)} %get-tuple-element.38), channel_id=1, source_target_pairs={{0,1},{1,0},{2,3},{3,2},{4,5},{5,4},{6,7},{7,6},{8,9},{9,8},{10,11... | collective-permute-start | bytes 196616 | tf_op jit(solution)/shard_map/ppermute | solution.py:436
  35.6 7.7 %collective-permute-start.12 = (bf16[128,1024]{1,0:T(8,128)(2,1)S(1)}, bf16[128,1024]{1,0:T(8,128)(2,1)S(1)}, u32[]{:S(2)}, u32[]{:S(2)}) collective-permute-start(bf16[128,1024]{1,0:T(8,128)(2,1)S(1)} %collective-permute-done.11.refs_2_), channel_id=1, source_target_pairs={{0,2},{1,3},{2,6},{3,7},{6,4},{7,5},{4,0},{5,1},{8,10},{9,11},{10,... | collective-permute-start | bytes 786440 | tf_op jit(solution)/shard_map/ppermute | solution.py:431
  43.9 7.9 %collective-permute-start.15 = (bf16[128,1024]{1,0:T(8,128)(2,1)S(1)}, bf16[128,1024]{1,0:T(8,128)(2,1)S(1)}, u32[]{:S(2)}, u32[]{:S(2)}) collective-permute-start(bf16[128,1024]{1,0:T(8,128)(2,1)S(1)} %get-tuple-element.57), channel_id=1, source_target_pairs={{0,1},{1,0},{2,3},{3,2},{4,5},{5,4},{6,7},{7,6},{8,9},{9,8},{10,11... | collective-permute-start | bytes 786440 | tf_op jit(solution)/shard_map/ppermute | solution.py:436
  50.6 6.4 %collective-permute-start.13 = (bf16[32,1024]{1,0:T(8,128)(2,1)S(1)}, bf16[32,1024]{1,0:T(8,128)(2,1)S(1)}, u32[]{:S(2)}, u32[]{:S(2)}) collective-permute-start(bf16[32,1024]{1,0:T(8,128)(2,1)S(1)} %get-tuple-element.53.refs_2_), channel_id=1, source_target_pairs={{1,0},{2,1},{3,2},{4,3},{5,4},{6,5},{7,6},{9,8},{10,9},{11,10},{12... | collective-permute-start | bytes 196616 | tf_op jit(solution)/shard_map/ppermute | solution.py:542
  54.8 17.4 %collective-permute-start.16 = (bf16[128,1280]{1,0:T(8,128)(2,1)S(1)}, bf16[128,1280]{1,0:T(8,128)(2,1)S(1)}, u32[]{:S(2)}, u32[]{:S(2)}) collective-permute-start(bf16[128,1280]{1,0:T(8,128)(2,1)S(1)} %get-tuple-element.59), channel_id=1, source_target_pairs={{0,1},{1,0},{2,3},{3,2},{4,5},{5,4},{6,7},{7,6},{8,9},{9,8},{10,11... | collective-permute-start | bytes 983048 | tf_op jit(solution)/shard_map/ppermute | solution.py:436
  57.7 13.7 %collective-permute-start.14 = (bf16[128,1024]{1,0:T(8,128)(2,1)}, bf16[128,1024]{1,0:T(8,128)(2,1)S(1)}, u32[]{:S(2)}, u32[]{:S(2)}) collective-permute-start(bf16[128,1024]{1,0:T(8,128)(2,1)} %add.3), channel_id=1, source_target_pairs={{8,0},{16,8},{24,16},{9,1},{17,9},{25,17},{10,2},{18,10},{26,18},{... | collective-permute-start | bytes 786440 | tf_op jit(solution)/shard_map/ppermute | solution.py:557

commit v4 on v3

--- a/solution.py
+++ b/solution.py
@@ -12,6 +12,7 @@
 F32 = jnp.float32
 BF16 = jnp.bfloat16
 HALO = 32
+CODE_ROWS = 16
 SCALE = 0.5
 REACH = 16
 
@@ -102,9 +103,11 @@
         copy.wait()
 
 
-def weight_kernel(group_size, far_w, far_mixes, far_head, far_cot, out_ref, fold_ref, mixes_ref, head_ref, cot_ref,
-                  w_ref, sems):
-    copies = start_copies([(far_w, w_ref), (far_cot, cot_ref), (far_mixes, mixes_ref), (far_head, head_ref)], sems)
+def weight_kernel(group_size, far_w, far_mixes, far_head, far_cot, far_labels, far_events, out_ref, fold_ref, mixes_ref,
+                  head_ref, cot_ref, w_ref, labels, events, sems):
+    row_count = far_cot.shape[0]
+    copies = [(far_w, w_ref), (far_labels, labels), (far_events, events), (far_cot, cot_ref.at[pl.ds(0, row_count)])]
+    copies = start_copies(copies + [(far_mixes, mixes_ref), (far_head, head_ref)], sems)
     layers, slabs = out_ref.shape[:2]
     width, groups = w_ref.shape[2:]
     rows = slabs * SLAB
@@ -117,7 +120,10 @@
     column = lax.broadcasted_iota(jnp.int32, (width, 2 * SLAB), 1)
     one_hot = (o == column % group_size + jnp.where(column >= SLAB, group_size, 0)).astype(F32).astype(BF16)
     keep = same_group(group_size)
-    finish_copies(copies[:1])
+    cot_ref[row_count:, :] = jnp.zeros((CODE_ROWS, cot_ref.shape[1]), BF16)
+    finish_copies(copies[:3])
+    code = (labels[...] + head_ref.shape[0] * events[...]).astype(F32)
+    cot_ref[row_count:, :row_count] = jnp.broadcast_to(code, (CODE_ROWS, row_count)).astype(BF16)
     for layer in range(layers):
         for k in range(3):
             for slab in range(slabs):
@@ -126,75 +132,87 @@
                 out_ref[layer, slab, cut(k), :] = jnp.where(keep, tiled, 0.0).astype(BF16)
     for k in range(3):
         fold_ref[:, cut(k, 2 * SLAB)] = spread(group_size, outputs * k, SLAB).astype(BF16)
-    finish_copies(copies[1:])
-
-
-def relay_kernel(value, *refs):
-    tail_ref, copy_ref, sems = refs[-3:]
-    copies = start_copies([(value, copy_ref)], sems)
-    tail_ref[...] = value[value.shape[0] - HALO :, :]
+    finish_copies(copies[3:])
+
+
+def relay_kernel(copied, *refs):
+    *copy_refs, tail_ref, sems = refs[-(2 + copied) :]
+    copies = start_copies(list(zip(refs[:copied], copy_refs)), sems)
+    tail_ref[...] = refs[0][refs[0].shape[0] - HALO :, :]
     finish_copies(copies)
 
 
-def forward_kernel(blocks, *refs):
-    inputs, tails, codes = refs[:blocks], refs[blocks : 2 * blocks], refs[2 * blocks : 3 * blocks]
-    weights, mixes, head, x_ref, mid_ref, pre_ref, dlogit_ref, gated_ref, code_ref, sems = refs[3 * blocks :]
-    row_count, channels = inputs[0].shape
-    slabs = channels // SLAB
+def short_rows(places, begin, end, x_ref, mid_ref, weights, mixes, gated_ref):
+    channels, length = x_ref.shape[2], end - begin
+    for slab in range(channels // SLAB):
+        for i, z in enumerate(places):
+            at = [HALO + begin - k * REACH for k in range(3)]
+            tanh, sig = gates(conv([x_ref[z, j : j + length, cut(slab)] for j in at], weights[0, slab]))
+            gated_ref[cut(i, length), cut(slab)] = (tanh * sig).astype(BF16)
+    mixed = nn(gated_ref[: len(places) * length, :], mixes[0])
+    for i, z in enumerate(places):
+        here = x_ref[z, HALO + begin : HALO + end, :]
+        mid_ref[z + SPAN, begin:end, :] = (here.astype(F32) + mixed[cut(i, length)]).astype(BF16)
+
+
+def begin_kernel(blocks, first, count, inputs, weights, mixes, x_ref, mid_ref, gated_ref, sems):
+    row_count = inputs[0].shape[0]
+    places = [arrival(first + i, blocks) for i in range(count)]
+    copies = start_copies([(a, x_ref.at[z, pl.ds(HALO, row_count)]) for a, z in zip(inputs, places)], sems)
+    if first == 0:
+        mid_ref[0:SPAN] = jnp.zeros((SPAN,) + mid_ref.shape[1:], BF16)
+    finish_copies(copies)
+    if count <= 4:
+        short_rows(places, HALO, row_count, x_ref, mid_ref, weights, mixes, gated_ref)
+    else:
+        some(first, first + count, blocks,
+             lambda places: short_rows(places, HALO, row_count, x_ref, mid_ref, weights, mixes, gated_ref))
+
+
+def begin_some(blocks, first, count, *refs):
+    x_ref, mid_ref, gated_ref, sems = refs[-4:]
+    begin_kernel(blocks, first, count, refs[:count], refs[count], refs[count + 1], x_ref, mid_ref, gated_ref, sems)
+
+
+def forward_kernel(blocks, resident, *refs):
+    inputs, refs = ([], refs) if resident else (refs[:blocks], refs[blocks:])
+    tails, refs = refs[:blocks], refs[blocks:]
+    weights, mixes, head = refs[:3]
+    x_ref, mid_ref, pre_ref, hazard_ref, gated_ref, sems = refs[-6:]
+    row_count, channels = mid_ref.shape[1:]
     y = lax.axis_index("seq") % SPAN
-    rows_in = []
-    for p in range(blocks):
-        z = arrival(p, blocks)
-        rows_in.append((inputs[p], x_ref.at[z, pl.ds(HALO, row_count)]))
-        rows_in.append((tails[p], x_ref.at[z + 1 - y, pl.ds(0, HALO)]))
-    rows_in = start_copies(rows_in, sems)
-    for p in range(blocks):
-        code_ref[arrival(p, blocks)] = codes[p][...]
-    mid_ref[0:SPAN] = jnp.zeros((SPAN, row_count, channels), BF16)
+    copies = [(tails[p], x_ref.at[arrival(p, blocks) + 1 - y, pl.ds(0, HALO)]) for p in range(blocks)]
+    copies = start_copies(copies, sems)
+    if not resident:
+        late = sems.at[pl.ds(blocks, blocks)]
+        begin_kernel(blocks, 0, blocks, inputs, weights, mixes, x_ref, mid_ref, gated_ref, late)
 
     @pl.when(y == 0)
     def _():
         x_ref[0, :HALO, :] = jnp.zeros((HALO, channels), BF16)
 
-    finish_copies(rows_in)
-
-    def gate(first, count, layer, tap):
-        for slab in range(slabs):
+    finish_copies(copies)
+
+    def short(first, count):
+        places = [first + i for i in range(count)]
+        short_rows(places, 0, HALO, x_ref, mid_ref, weights, mixes, gated_ref)
+
+    chunks(blocks, short)
+
+    def long(first, count):
+        for slab in range(channels // SLAB):
             for i in range(count):
-                pre = conv([tap(first + i, k, cut(slab)) for k in range(3)], weights[layer, slab])
-                if layer:
-                    pre_ref[first + i, :, cut(slab, 2 * SLAB)] = pre
+                pre = conv([mid_ref[first + i + SPAN - k, :, cut(slab)] for k in range(3)], weights[1, slab])
+                pre_ref[first + i, :, cut(slab, 2 * SLAB)] = pre
                 tanh, sig = gates(pre)
-                gated_ref[i * row_count : (i + 1) * row_count, cut(slab)] = (tanh * sig).astype(BF16)
-
-    def short_tap(z, k, column):
-        return x_ref[z, HALO - k * REACH : HALO - k * REACH + row_count, column]
-
-    def short(first, count):
-        gate(first, count, 0, short_tap)
-        mixed = nn(gated_ref[...], mixes[0]).reshape(count, row_count, channels)
-        here = pl.ds(first, count)
-        mid_ref[pl.ds(first + SPAN, count)] = (x_ref[here, HALO:, :].astype(F32) + mixed).astype(BF16)
-
-    chunks(blocks, short)
-
-    def long_tap(z, k, column):
-        return mid_ref[z + SPAN - k, :, column]
-
-    def long(first, count):
-        gate(first, count, 1, long_tap)
+                gated_ref[cut(i, row_count), cut(slab)] = (tanh * sig).astype(BF16)
 
         @pl.when(on_last_section())
         def _():
+            mixed = nn(gated_ref[...], mixes[1])
             for i in range(count):
-                z = first + i
-                here = slice(i * row_count, (i + 1) * row_count)
-                top = (mid_ref[z + SPAN].astype(F32) + nn(gated_ref[here, :], mixes[1])).astype(BF16)
-                logits = nt(head[...], top)
-                bins = lax.broadcasted_iota(jnp.int32, logits.shape, 0)
-                label, event = code_ref[z, 0:1, :], code_ref[z, 1:2, :].astype(F32)
-                dlogit = jnp.where(bins <= label, jax.nn.sigmoid(logits), 0.0) - jnp.where(bins == label, event, 0.0)
-                dlogit_ref[z] = dlogit.astype(BF16)
+                top = (mid_ref[first + i + SPAN].astype(F32) + mixed[cut(i, row_count)]).astype(BF16)
+                hazard_ref[first + i] = jax.nn.sigmoid(nt(head[...], top))
 
     chunks(blocks, long)
 
@@ -222,10 +240,27 @@
     send_ref[...] = total_ref[pl.ds(other, share), :].astype(BF16)
 
 
-def add_loss(z, dlogit_ref, head, g_ref):
+def fetch_cotangents(cots, first, blocks, g_ref, code_ref, sems):
+    row_count = g_ref.shape[1]
+    copies = []
+    for i, cot in enumerate(cots):
+        z = arrival(first + i, blocks)
+        copies.append((cot.at[pl.ds(0, row_count)], g_ref.at[z]))
+        copies.append((cot.at[pl.ds(row_count, CODE_ROWS), pl.ds(0, row_count)], code_ref.at[z]))
+    return start_copies(copies, sems)
+
+
+def add_loss(places, code_ref, hazard_ref, head, g_ref):
     @pl.when(on_last_section())
     def _():
-        g_ref[z] = (g_ref[z].astype(F32) + tn(dlogit_ref[z], head[...])).astype(BF16)
+        for z in places:
+            hazard = hazard_ref[z]
+            bins = lax.broadcasted_iota(jnp.int32, hazard.shape, 0).astype(F32)
+            code = code_ref[z, 0:1, :].astype(F32)
+            event = jnp.where(code >= hazard.shape[0], 1.0, 0.0)
+            label = code - hazard.shape[0] * event
+            dlogit = jnp.where(bins <= label, hazard, 0.0) - jnp.where(bins == label, event, 0.0)
+            g_ref[z] = (g_ref[z].astype(F32) + tn(dlogit.astype(BF16), head[...])).astype(BF16)
 
 
 def gate_cotangent(places, g_ref, pre_ref, mixes, d_ref):
@@ -261,14 +296,13 @@
 
 def early_kernel(blocks, early, *refs):
     cots = refs[:early]
-    pre_ref, dlogit_ref, head, mixes, g_ref, d_ref, total_ref, sems = refs[early:]
-    copies = start_copies([(cots[p], g_ref.at[arrival(p, blocks)]) for p in range(early)], sems)
+    pre_ref, hazard_ref, head, mixes, g_ref, d_ref, total_ref, code_ref, sems = refs[early:]
+    copies = fetch_cotangents(cots, 0, blocks, g_ref, code_ref, sems)
     total_ref[...] = jnp.zeros(total_ref.shape, F32)
     finish_copies(copies)
 
     def one(places):
-        for z in places:
-            add_loss(z, dlogit_ref, head, g_ref)
+        add_loss(places, code_ref, hazard_ref, head, g_ref)
         gate_cotangent(places, g_ref, pre_ref, mixes, d_ref)
         mix_sums(places, g_ref, pre_ref, total_ref)
 
@@ -277,16 +311,14 @@
 
 def mix_kernel(blocks, early, *refs):
     cots, refs = refs[: blocks - early], refs[blocks - early :]
-    pre_ref, dlogit_ref, head = refs[:3]
-    g_ref, mine_ref, own_ref, send_ref, total_ref, sems = refs[-6:]
-    copies = [(cot, g_ref.at[arrival(early + i, blocks)]) for i, cot in enumerate(cots)]
-    copies = start_copies(copies, sems)
+    pre_ref, hazard_ref, head = refs[:3]
+    g_ref, mine_ref, own_ref, send_ref, total_ref, code_ref, sems = refs[-7:]
+    copies = fetch_cotangents(cots, early, blocks, g_ref, code_ref, sems)
     total_ref[...] = refs[3][...] if early else jnp.zeros(total_ref.shape, F32)
     finish_copies(copies)
 
     def one(places):
-        for z in places:
-            add_loss(z, dlogit_ref, head, g_ref)
+        add_loss(places, code_ref, hazard_ref, head, g_ref)
         mix_sums(places, g_ref, pre_ref, total_ref)
 
     some(early, blocks, blocks, one)
@@ -372,7 +404,8 @@
     split_pair(pair, total_ref, own_ref, send_ref)
 
 
-def finish_kernel(group_size, mix1, own0, got_mix1, got0, mix_ref, conv_ref):
+def finish_kernel(group_size, mix1, own0, got_mix1, got0, last_cot, other_cot, mix_ref, conv_ref, cot_ref):
+    cot_ref[...] = jnp.where(on_last_section(), last_cot[...].astype(F32), other_cot[...].astype(F32)).astype(BF16)
     channels = mix_ref.shape[2]
     width = 2 * group_size
     total = own0[...] + got0[...].astype(F32)
@@ -384,27 +417,24 @@
             conv_ref[layer, k] = total[:, begin : begin + width]
 
 
-def add_kernel(own_ref, pushed_ref, out_ref):
-    rest = out_ref.shape[0] - HALO
-    out_ref[:rest, :] = own_ref[:rest, :].astype(BF16)
-    out_ref[rest:, :] = (own_ref[rest:, :] + pushed_ref[...].astype(F32)).astype(BF16)
-
-
-def choose_kernel(last_ref, other_ref, out_ref):
-    out_ref[...] = jnp.where(on_last_section(), last_ref[...].astype(F32), other_ref[...].astype(F32)).astype(BF16)
+def add_kernel(own_ref, pushed_ref, *out_refs):
+    rest = own_ref.shape[0] - HALO
+    for out_ref in out_refs:
+        out_ref[:rest, :] = own_ref[:rest, :].astype(BF16)
+        out_ref[rest:, :] = (own_ref[rest:, :] + pushed_ref[...].astype(F32)).astype(BF16)
 
 
 VMEM = pl.BlockSpec(memory_space=pltpu.VMEM)
 ANY = pl.BlockSpec(memory_space=pl.ANY)
 
 
-def call(resident, kernel, outs, arrays, scratch=(), name=None, aliases={}, far=(), near=True, final=False, us=0.1):
+def call(resident, kernel, outs, arrays, scratch=(), name=None, aliases={}, far=(), near=True, final=(), us=0.1):
     if resident and near:
         arrays = [a if i in far else pltpu.with_memory_space_constraint(a, pltpu.VMEM) for i, a in enumerate(arrays)]
-    make = pltpu.VMEM if resident and near and not final else jax.ShapeDtypeStruct
+    make = [jax.ShapeDtypeStruct if i in final or not (resident and near) else pltpu.VMEM for i in range(len(outs))]
     return pl.pallas_call(
         kernel,
-        out_shape=[make(shape, kind) for shape, kind in outs],
+        out_shape=[of(shape, kind) for of, (shape, kind) in zip(make, outs)],
         in_specs=[ANY if i in far else VMEM for i in range(len(arrays))],
         out_specs=[VMEM] * len(outs),
         scratch_shapes=[pltpu.VMEM(*s) if isinstance(s, tuple) else s for s in scratch],
@@ -435,22 +465,17 @@
     def swap(value):
         return lax.ppermute(value, "seq", [(b, b + 1 - 2 * (b % 2)) for b in range(seq)])
 
-    def direct(value, steps):
-        pairs = [(source, source) for source in range(blocks)]
-        for _ in range(steps):
-            pairs = [(source, dict(hops)[target]) for source, target in pairs]
-        return lax.ppermute(value, "seq", [(a * SPAN + y, b * SPAN + y) for a, b in pairs for y in range(SPAN)])
-
     resident = blocks <= 4
     run = functools.partial(call, resident)
-    def relay(value, *others):
+
+    def relay(copied, *others):
         return run(
-            relay_kernel,
-            [((HALO, channels), BF16), ((row_count, channels), BF16)],
-            [value, *others],
-            [pltpu.SemaphoreType.DMA((1,))],
+            functools.partial(relay_kernel, copied),
+            [(a.shape, BF16) for a in others[:copied]] + [((HALO, channels), BF16)],
+            list(others),
+            [pltpu.SemaphoreType.DMA((max(copied, 1),))],
             name="relay",
-            far=range(1, 1 + len(others)),
+            far=range(1, len(others)),
             us=0.3,
         )
 
@@ -459,54 +484,89 @@
 
     head = far(hazard_head.T)
     tails = [swap(first_input[row_count - HALO :])]
-    codes = [jnp.stack([labels, events])]
     taps = far(kernel_weight[0].transpose(0, 1, 3, 4, 2).reshape(2, 3, -1, groups))
     mixes, far_cot = far(blend_weight[0]), far(cot)
+    sent_rows = row_count + CODE_ROWS
     weights, fold, mixes, head, own_cot = run(
         functools.partial(weight_kernel, group_size),
-        [((2, slabs, 3 * SLAB, 2 * SLAB), BF16), ((SLAB, 6 * SLAB), BF16), (mixes.shape, BF16), (head.shape, BF16), (cot.shape, BF16)],
-        [taps, mixes, head, far_cot],
-        [(taps.shape, BF16), pltpu.SemaphoreType.DMA((4,))],
+        [
+            ((2, slabs, 3 * SLAB, 2 * SLAB), BF16),
+            ((SLAB, 6 * SLAB), BF16),
+            (mixes.shape, BF16),
+            (head.shape, BF16),
+            ((sent_rows, channels), BF16),
+        ],
+        [taps, mixes, head, far_cot, far(labels[None]), far(events[None])],
+        [(taps.shape, BF16)] + [((1, row_count), jnp.int32)] * 2 + [pltpu.SemaphoreType.DMA((6,))],
         name="weights",
-        far=(0, 1, 2, 3),
+        far=range(6),
         us=3.5,
     )
-    inputs, cots = [first_input], [cot]
-    codes += [direct(codes[0], p) for p in range(1, blocks)]
-    before = {1: [tails[0], fold], 2: codes[1:]}
+    gated = ((min(blocks, 4) * row_count, channels), BF16)
+    x_rows = ((blocks + 1, HALO + row_count, channels), BF16)
+    mid_rows = ((blocks + SPAN, row_count, channels), BF16)
+
+    def begin(first, count, values, begun):
+        operands = [*values, weights, mixes, *begun]
+        return run(
+            functools.partial(begin_some, blocks, first, count),
+            [x_rows, mid_rows],
+            operands,
+            [gated, pltpu.SemaphoreType.DMA((count,))],
+            name="begin",
+            far=range(count),
+            aliases={count + 2: 0, count + 3: 1} if begun else {},
+            us=0.6 * count,
+        )
+
+    begun = []
+    inputs, cots = [far(first_input)], [own_cot]
     sent_input = first_input
-    cots.append(step(own_cot))
     for p in range(1, blocks):
         inputs.append(step(sent_input))
-        if p > 1:
-            cots.append(step(cots[-1]))
-        tail, sent_input = relay(inputs[-1], *before.get(p, []))
+        if p == 1:
+            sent_input, tail = relay(1, inputs[1], tails[0], fold)
+            sent_cot = own_cot
+        elif p < blocks - 1:
+            sent_input, tail = relay(1, inputs[p])
+            if resident and p == blocks - 2:
+                begun = begin(0, blocks - 1, inputs, [])
+                sent_cot, _ = relay(1, sent_cot, begun[1])
+        else:
+            (tail,) = relay(0, inputs[p])
         tails.append(swap(tail))
-    rows = min(blocks, 4) * row_count
-    x, mid, pre, dlogit = run(
-        functools.partial(forward_kernel, blocks),
+        sent_cot = step(sent_cot)
+        cots.append(sent_cot)
+    if resident:
+        begun = begin(blocks - 1, 1, inputs[-1:], begun)
+        inputs = []
+    operands = [*inputs, *tails, weights, mixes, head, *begun]
+    x, mid, pre, hazard = run(
+        functools.partial(forward_kernel, blocks, resident),
         [
-            ((blocks + 1, HALO + row_count, channels), BF16),
-            ((blocks + SPAN, row_count, channels), BF16),
+            x_rows,
+            mid_rows,
             ((blocks, row_count, 2 * channels), BF16),
-            ((blocks, head.shape[0], row_count), BF16),
+            ((blocks, head.shape[0], row_count), F32),
         ],
-        [far(first_input), *inputs[1:], *tails, *codes, weights, mixes, head],
-        [((rows, channels), BF16), ((blocks, 2, row_count), jnp.int32), pltpu.SemaphoreType.DMA((2 * blocks,))],
+        operands,
+        [gated, pltpu.SemaphoreType.DMA((2 * blocks,))],
         name="forward",
-        far=range(2 * blocks),
-        us=5,
+        far=range(len(inputs) + blocks),
+        aliases={len(operands) - 2: 0, len(operands) - 1: 1} if resident else {},
+        us=3,
     )
     wide = max(channels // blocks, SLAB)
     block_rows = ((blocks, row_count, channels), BF16)
     early = blocks - 1 if resident else 0
     d_rows = ((blocks + SPAN, row_count, 2 * channels), BF16)
+    codes = ((blocks, CODE_ROWS, row_count), BF16)
     if early:
         g, d, total = run(
             functools.partial(early_kernel, blocks, early),
             [block_rows, d_rows, ((wide, channels), F32)],
-            [far_cot, *cots[1:early], pre, dlogit, head, mixes],
-            [pltpu.SemaphoreType.DMA((early,))],
+            [*cots[:early], pre, hazard, head, mixes],
+            [codes, pltpu.SemaphoreType.DMA((2 * early,))],
             name="early",
             far=range(early),
             us=4,
@@ -515,8 +575,8 @@
     g, mine, mix1, send_mix1 = run(
         functools.partial(mix_kernel, blocks, early),
         [block_rows, ((row_count, channels), BF16), ((share, channels), F32), ((share, channels), BF16)],
-        [*late, pre, dlogit, head] + ([total, g] if early else []),
-        [((wide, channels), F32), pltpu.SemaphoreType.DMA((len(late),))],
+        [*late, pre, hazard, head] + ([total, g] if early else []),
+        [((wide, channels), F32), codes, pltpu.SemaphoreType.DMA((2 * len(late),))],
         name="long_mix",
         aliases={len(late) + 4: 0} if early else {},
         far=range(len(late)),
@@ -548,20 +608,19 @@
         [((wide, sums), F32)],
         name="short_backward",
         far=(7, 8) if early else (6, 7),
-        us=2.5,
+        us=8,
     )
     got0 = swap(send0)
     rows_out = ((row_count, channels), BF16)
-    (input_gradient,) = run(add_kernel, [rows_out], [own_sum, pushed], name="add", final=True, us=0.4)
+    input_gradient, sent_gradient = run(add_kernel, [rows_out] * 2, [own_sum, pushed], name="add", final=(0,), us=0.4)
     count = lax.axis_size("section")
-    received = lax.ppermute(input_gradient, "section", [(s, s - 1) for s in range(1, count)])
-    (next_cot,) = run(choose_kernel, [rows_out], [mine, received], name="choose", final=True, us=0.4)
-    mix_share, conv_share = run(
+    received = lax.ppermute(sent_gradient, "section", [(s, s - 1) for s in range(1, count)])
+    mix_share, conv_share, next_cot = run(
         functools.partial(finish_kernel, group_size),
-        [((share, 2, channels), F32), ((2, 3, share, 2 * group_size), F32)],
-        [mix1, own0, got_mix1, got0],
+        [((share, 2, channels), F32), ((2, 3, share, 2 * group_size), F32), rows_out],
+        [mix1, own0, got_mix1, got0, mine, received],
         name="finish",
-        final=True,
+        final=(0, 1, 2),
         us=1.4,
     )
     conv_share = conv_share.reshape(2, 3, share // group_size, group_size, 2 * group_size)

time: 73.8 us -> 69.7 us (0.944)
  starting transfers between devices: 27.6 us -> 22.2 us
    ppermute x6, waiting for transfers between devices: 6.02 us -> 14.7 us  [step(): lax.ppermute(value, 'seq', [(a * SPAN + y, b * SPAN + y) for a, b in hops...]
    ppermute x4 -> x1, waiting for transfers between devices: 13.3 us -> 5.14 us  [body(): lax.ppermute(sent_gradient, 'section', [(s, s - 1) for s in range(1, coun...]
    ppermute x4 -> x1, starting transfers between devices: 10.6 us -> 6.12 us  [body(): lax.ppermute(sent_gradient, 'section', [(s, s - 1) for s in range(1, coun...]
    ppermute x6, starting transfers between devices: 7.36 us -> 5.98 us  [swap(): lax.ppermute(value, 'seq', [(b, b + 1 - 2 * (b % 2)) for b in range(seq)])]
    pallas_call x13 -> x15, Pallas kernels: 25 us -> 25.7 us  [call(): pl.pallas_call(kernel, out_shape=[of(shape, kind) for of, (shape, kind) i...]
  transfers between devices with their start and end apart: 17 -> 14, of which waited for: 6 -> 7; matrix products, arithmetic and copies ran while one was open for 1% -> 1% of each run, Pallas kernels for 31% -> 34%
where the time goes in v4:
time: 69.7 us; the launch traced here: 69.4 us
  Pallas kernels  25.7 us (37%)
  starting transfers between devices  22.2 us (32%)
  waiting for transfers between devices  19.9 us (29%)
  local copies, waits for them, and re-layouts  0.88 us (1%)
  between operations  0.77 us (1%)
    pallas_call x15, Pallas kernels, call(): pl.pallas_call(kernel, out_shape=[of(shape, kind) for of, (shape, kind) i...  25.7 us
    ppermute x6, waiting for transfers between devices, step(): lax.ppermute(value, 'seq', [(a * SPAN + y, b * SPAN + y) for a, b in hops...  14.7 us
    ppermute x6, starting transfers between devices, step(): lax.ppermute(value, 'seq', [(a * SPAN + y, b * SPAN + y) for a, b in hops...  8.82 us
    ppermute x1, starting transfers between devices, body(): lax.ppermute(sent_gradient, 'section', [(s, s - 1) for s in range(1, coun...  6.12 us
    ppermute x6, starting transfers between devices, swap(): lax.ppermute(value, 'seq', [(b, b + 1 - 2 * (b % 2)) for b in range(seq)])  5.98 us
    ppermute x1, waiting for transfers between devices, body(): lax.ppermute(sent_gradient, 'section', [(s, s - 1) for s in range(1, coun...  5.14 us
  transfers between devices with their start and end apart: 14, of which 7 were waited for; matrix products, arithmetic and copies ran while one was open for 1% of the time, Pallas kernels for 34%

profile of v4, /device:TPU:1, one launch (start us, length us, event | category | flops | bytes accessed | tf_op | source)
XLA Modules:
  0.0 69.4 jit_solution(16267431335136935485)
XLA Ops:
  0.6 2.2 %collective-permute-start.1 = (bf16[128,1024]{1,0:T(8,128)(2,1)}, bf16[128,1024]{1,0:T(8,128)(2,1)S(1)}, u32[]{:S(2)}, u32[]{:S(2)}) collective-permute-start(bf16[128,1024]{1,0:T(8,128)(2,1)} %bitcast.17), channel_id=1, source_target_pairs={{0,2},{1,3},{2,6},{3,7},{6,4},{7,5},{4,0},{5,1},{8,10},{9,11},{10,... | collective-permute-start | bytes 786440 | tf_op jit(solution)/shard_map/ppermute | solution.py:461
  2.8 0.9 %slice_bitcast_fusion = bf16[32,1024]{1,0:T(8,128)(2,1)S(1)} fusion(bf16[1,128,1024]{2,1,0:T(8,128)(2,1)} %param.7), kind=kLoop, calls=%fused_computation | loop fusion | bytes 131072 | tf_op jit(solution)/shard_map/slice | solution.py:486
  3.7 1.2 %collective-permute-start = (bf16[32,1024]{1,0:T(8,128)(2,1)S(1)}, bf16[32,1024]{1,0:T(8,128)(2,1)S(1)}, u32[]{:S(2)}, u32[]{:S(2)}) collective-permute-start(bf16[32,1024]{1,0:T(8,128)(2,1)S(1)} %slice_bitcast_fusion), channel_id=1, source_target_pairs={{0,1},{1,0},{2,3},{3,2},{4,5},{5,4},{6,7},{7,6},{8,9},{9,8},{10,11... | collective-permute-start | bytes 196616 | tf_op jit(solution)/shard_map/ppermute | solution.py:466
  4.9 4.8 %weights.1 = (bf16[2,8,384,256]{3,2,1,0:T(8,128)(2,1)S(1)}, bf16[128,768]{1,0:T(8,128)(2,1)S(1)}, bf16[2,1024,1024]{2,1,0:T(8,128)(2,1)S(1)}, bf16[64,1024]{1,0:T(8,128)(2,1)S(1)}, bf16[144,1024]{1,0:T(8,128)(2,1)S(1)}) custom-call(bf16[2,3,512,64]{3,2,1,0:T(8,128)(2,1)} %bitcast.20, bf16[2,1024,1024]{2,1,0:T(8,128)(2,1)} %bitcast.19, ...), custom_call_target="tpu_custom_call" | custom-call | flops 1924999936 | tf_op jit(solution)/shard_map/weights/pallas_call | solution.py:435
  9.7 0.0 collective-permute-done.refs_1_.refs_0_
  9.7 0.4 collective-permute-done.1.refs_0_.refs_1_
  10.1 2.0 %collective-permute-start.3 = (bf16[128,1024]{1,0:T(8,128)(2,1)S(1)}, bf16[128,1024]{1,0:T(8,128)(2,1)S(1)}, u32[]{:S(2)}, u32[]{:S(2)}) collective-permute-start(bf16[128,1024]{1,0:T(8,128)(2,1)S(1)} %get-tuple-element.42), channel_id=1, source_target_pairs={{0,2},{1,3},{2,6},{3,7},{6,4},{7,5},{4,0},{5,1},{8,10},{9,11},{10,... | collective-permute-start | bytes 786440 | tf_op jit(solution)/shard_map/ppermute | solution.py:461
  12.1 1.4 %collective-permute-start.7 = (bf16[144,1024]{1,0:T(8,128)(2,1)S(1)}, bf16[144,1024]{1,0:T(8,128)(2,1)S(1)}, u32[]{:S(2)}, u32[]{:S(2)}) collective-permute-start(bf16[144,1024]{1,0:T(8,128)(2,1)S(1)} %get-tuple-element.53.refs_0_), channel_id=1, source_target_pairs={{0,2},{1,3},{2,6},{3,7},{6,4},{7,5},{4,0},{5,1},{8,10},{9,11},{10,... | collective-permute-start | bytes 884744 | tf_op jit(solution)/shard_map/ppermute | solution.py:461
  13.5 4.1 %collective-permute-done.3.refs_0_.refs_2_ = bf16[128,1024]{1,0:T(8,128)(2,1)S(1)} collective-permute-done((bf16[128,1024]{1,0:T(8,128)(2,1)S(1)}, bf16[128,1024]{1,0:T(8,128)(2,1)S(1)}, u32[]{:S(2)}, u32[]{:S(2)}) %collective-permute-start.3) | collective-permute-done | bytes 262176 | tf_op jit(solution)/shard_map/ppermute | solution.py:461
  17.7 1.1 %collective-permute-start.5 = (bf16[128,1024]{1,0:T(8,128)(2,1)S(1)}, bf16[128,1024]{1,0:T(8,128)(2,1)S(1)}, u32[]{:S(2)}, u32[]{:S(2)}) collective-permute-start(bf16[128,1024]{1,0:T(8,128)(2,1)S(1)} %get-tuple-element.44), channel_id=1, source_target_pairs={{0,2},{1,3},{2,6},{3,7},{6,4},{7,5},{4,0},{5,1},{8,10},{9,11},{10,... | collective-permute-start | bytes 786440 | tf_op jit(solution)/shard_map/ppermute | solution.py:461
  18.8 2.7 %begin.2 = (bf16[5,160,1024]{2,1,0:T(8,128)(2,1)S(1)}, bf16[6,128,1024]{2,1,0:T(8,128)(2,1)S(1)}) custom-call(bf16[128,1024]{1,0:T(8,128)(2,1)} %bitcast.18, bf16[128,1024]{1,0:T(8,128)(2,1)S(1)} %collective-permute-done.1.refs_0_.refs_1_, bf16[128,1024]{1,0:T(8,128)(2,1)S(1)} %collective-permute-done.3.refs_0_.refs_2_, ...), custom_call_target="tpu_custom_call" | custom-call | flops 990000000 | tf_op jit(solution)/shard_map/begin/pallas_call | solution.py:435
  21.4 2.5 %collective-permute-done.7.refs_0_.refs_1_ = bf16[144,1024]{1,0:T(8,128)(2,1)S(1)} collective-permute-done((bf16[144,1024]{1,0:T(8,128)(2,1)S(1)}, bf16[144,1024]{1,0:T(8,128)(2,1)S(1)}, u32[]{:S(2)}, u32[]{:S(2)}) %collective-permute-start.7) | collective-permute-done | bytes 294944 | tf_op jit(solution)/shard_map/ppermute | solution.py:461
  23.9 0.7 %relay.7 = (bf16[144,1024]{1,0:T(8,128)(2,1)S(1)}, bf16[32,1024]{1,0:T(8,128)(2,1)}) custom-call(bf16[144,1024]{1,0:T(8,128)(2,1)S(1)} %collective-permute-done.7.refs_0_.refs_1_, bf16[6,128,1024]{2,1,0:T(8,128)(2,1)S(1)} %get-tuple-element.49.refs_4_.refs_1_), custom_call_target="tpu_custom_call" | custom-call | flops 165000000 | tf_op jit(solution)/shard_map/relay/pallas_call | solution.py:435
  24.7 1.1 %collective-permute-start.8 = (bf16[144,1024]{1,0:T(8,128)(2,1)S(1)}, bf16[144,1024]{1,0:T(8,128)(2,1)S(1)}, u32[]{:S(2)}, u32[]{:S(2)}) collective-permute-start(bf16[144,1024]{1,0:T(8,128)(2,1)S(1)} %get-tuple-element.54), channel_id=1, source_target_pairs={{0,2},{1,3},{2,6},{3,7},{6,4},{7,5},{4,0},{5,1},{8,10},{9,11},{10,... | collective-permute-start | bytes 884744 | tf_op jit(solution)/shard_map/ppermute | solution.py:461
  25.8 0.2 collective-permute-start.2
  26.0 1.2 %collective-permute-start.4 = (bf16[32,1024]{1,0:T(8,128)(2,1)S(1)}, bf16[32,1024]{1,0:T(8,128)(2,1)S(1)}, u32[]{:S(2)}, u32[]{:S(2)}) collective-permute-start(bf16[32,1024]{1,0:T(8,128)(2,1)S(1)} %get-tuple-element.43), channel_id=1, source_target_pairs={{0,1},{1,0},{2,3},{3,2},{4,5},{5,4},{6,7},{7,6},{8,9},{9,8},{10,11... | collective-permute-start | bytes 196616 | tf_op jit(solution)/shard_map/ppermute | solution.py:466
  27.2 2.3 %collective-permute-done.5.refs_0_ = bf16[128,1024]{1,0:T(8,128)(2,1)S(1)} collective-permute-done((bf16[128,1024]{1,0:T(8,128)(2,1)S(1)}, bf16[128,1024]{1,0:T(8,128)(2,1)S(1)}, u32[]{:S(2)}, u32[]{:S(2)}) %collective-permute-start.5) | collective-permute-done | bytes 262176 | tf_op jit(solution)/shard_map/ppermute | solution.py:461
  29.6 0.7 %collective-permute-start.6 = (bf16[32,1024]{1,0:T(8,128)(2,1)S(1)}, bf16[32,1024]{1,0:T(8,128)(2,1)S(1)}, u32[]{:S(2)}, u32[]{:S(2)}) collective-permute-start(bf16[32,1024]{1,0:T(8,128)(2,1)S(1)} %relay.6), channel_id=1, source_target_pairs={{0,1},{1,0},{2,3},{3,2},{4,5},{5,4},{6,7},{7,6},{8,9},{9,8},{10,11... | collective-permute-start | bytes 196616 | tf_op jit(solution)/shard_map/ppermute | solution.py:466
  30.3 0.8 %begin.3 = (bf16[5,160,1024]{2,1,0:T(8,128)(2,1)S(1)}, bf16[6,128,1024]{2,1,0:T(8,128)(2,1)S(1)}) custom-call(bf16[128,1024]{1,0:T(8,128)(2,1)S(1)} %collective-permute-done.5.refs_0_, bf16[2,8,384,256]{3,2,1,0:T(8,128)(2,1)S(1)} %get-tuple-element.45.refs_3_.refs_1_.refs_4_.weights, ...), custom_call_target="tpu_custom_call", output_to_operand_aliasing={{0}: (3, {}), {1}: (4, {})} | custom-call | flops 330000000 | tf_op jit(solution)/shard_map/begin/pallas_call | solution.py:435
  31.1 4.7 %collective-permute-done.8.refs_2_ = bf16[144,1024]{1,0:T(8,128)(2,1)S(1)} collective-permute-done((bf16[144,1024]{1,0:T(8,128)(2,1)S(1)}, bf16[144,1024]{1,0:T(8,128)(2,1)S(1)}, u32[]{:S(2)}, u32[]{:S(2)}) %collective-permute-start.8) | collective-permute-done | bytes 294944 | tf_op jit(solution)/shard_map/ppermute | solution.py:461
  35.9 1.1 %collective-permute-start.9 = (bf16[144,1024]{1,0:T(8,128)(2,1)S(1)}, bf16[144,1024]{1,0:T(8,128)(2,1)S(1)}, u32[]{:S(2)}, u32[]{:S(2)}) collective-permute-start(bf16[144,1024]{1,0:T(8,128)(2,1)S(1)} %collective-permute-done.8.refs_2_), channel_id=1, source_target_pairs={{0,2},{1,3},{2,6},{3,7},{6,4},{7,5},{4,0},{5,1},{8,10},{9,11},{10,... | collective-permute-start | bytes 884744 | tf_op jit(solution)/shard_map/ppermute | solution.py:461
  36.9 0.0 collective-permute-done.2.refs_1_
  36.9 0.0 collective-permute-done.4.refs_2_
  36.9 0.0 collective-permute-done.6.refs_3_
  37.0 3.1 %forward.1 = (bf16[5,160,1024]{2,1,0:T(8,128)(2,1)S(1)}, bf16[6,128,1024]{2,1,0:T(8,128)(2,1)S(1)}, bf16[4,128,2048]{2,1,0:T(8,128)(2,1)S(1)}, f32[4,64,128]{2,1,0:T(8,128)S(1)}) custom-call(bf16[32,1024]{1,0:T(8,128)(2,1)S(1)} %collective-permute-done.refs_1_.refs_0_, ...), custom_call_target="tpu_custom_call", output_to_operand_aliasing={{0}: (7, {}), {1}: (8, {})} | custom-call | flops 1650000000 | tf_op jit(solution)/shard_map/forward/pallas_call | solution.py:435
  40.1 2.4 %early.1 = (bf16[4,128,1024]{2,1,0:T(8,128)(2,1)S(1)}, bf16[6,128,2048]{2,1,0:T(8,128)(2,1)S(1)}, f32[256,1024]{1,0:T(8,128)S(1)}) custom-call(bf16[144,1024]{1,0:T(8,128)(2,1)S(1)} %get-tuple-element.53.refs_0_, bf16[144,1024]{1,0:T(8,128)(2,1)S(1)} %collective-permute-done.7.refs_0_.refs_1_, bf16[144,1024]{1,0:T(8,128)(2,1)S(1)} %collective-permute-done.8.refs_2_, ...), custom_call_target="tpu_custom_call" | custom-call | flops 2200000000 | tf_op jit(solution)/shard_map/early/pallas_call | solution.py:435
  42.5 0.6 collective-permute-done.9.refs_0_
  43.1 0.6 long_mix.1
  43.7 0.4 collective-permute-start.11
  44.1 2.7 %long_backward.1 = (bf16[4,128,1024]{2,1,0:T(8,128)(2,1)S(1)}, bf16[6,128,2048]{2,1,0:T(8,128)(2,1)S(1)}) custom-call(bf16[4,128,1024]{2,1,0:T(8,128)(2,1)S(1)} %get-tuple-element.59.g_ref, bf16[6,128,1024]{2,1,0:T(8,128)(2,1)S(1)} %get-tuple-element.60.mid_ref.refs_0_, ...), custom_call_target="tpu_custom_call", output_to_operand_aliasing={{1}: (6, {})} | custom-call | flops 1870000000 | tf_op jit(solution)/shard_map/long_backward/pallas_call | solution.py:435
  46.9 2.7 %own_backward.1 = (bf16[32,1024]{1,0:T(8,128)(2,1)S(1)}, f32[128,1024]{1,0:T(8,128)S(1)}) custom-call(bf16[5,160,1024]{2,1,0:T(8,128)(2,1)S(1)} %get-tuple-element.52.x_ref, bf16[4,128,1024]{2,1,0:T(8,128)(2,1)S(1)} %get-tuple-element.62.between_ref, bf16[2,8,384,256]{3,2,1,0:T(8,128)(2,1)S(1)} %get-tuple-element.45.refs_3_.refs_1_.refs_4_.weights, ...), custom_call_target="tpu_custom_call" | custom-call | flops 1484999936 | tf_op jit(solution)/shard_map/own_backward/pallas_call | solution.py:435
  49.6 1.3 %collective-permute-start.10 = (bf16[32,1024]{1,0:T(8,128)(2,1)S(1)}, bf16[32,1024]{1,0:T(8,128)(2,1)S(1)}, u32[]{:S(2)}, u32[]{:S(2)}) collective-permute-start(bf16[32,1024]{1,0:T(8,128)(2,1)S(1)} %get-tuple-element.64.refs_2_), channel_id=1, source_target_pairs={{1,0},{2,1},{3,2},{4,3},{5,4},{6,5},{7,6},{9,8},{10,9},{11,10},{12... | collective-permute-start | bytes 196616 | tf_op jit(solution)/shard_map/ppermute | solution.py:602
  50.9 0.0 collective-permute-done.11.refs_3_.got_mix1
  50.9 2.9 %short_backward.1 = (f32[128,1280]{1,0:T(8,128)S(1)}, bf16[128,1280]{1,0:T(8,128)(2,1)S(1)}) custom-call(bf16[5,160,1024]{2,1,0:T(8,128)(2,1)S(1)} %get-tuple-element.52.x_ref, bf16[4,128,1024]{2,1,0:T(8,128)(2,1)S(1)} %get-tuple-element.62.between_ref, bf16[2,8,384,256]{3,2,1,0:T(8,128)(2,1)S(1)} %get-tuple-element.45.refs_3_.refs_1_.refs_4_.weights, ...), custom_call_target="tpu_custom_call" | custom-call | flops 4400000000 | tf_op jit(solution)/shard_map/short_backward/pallas_call | solution.py:435
  53.8 2.2 %collective-permute-start.12 = (bf16[128,1280]{1,0:T(8,128)(2,1)S(1)}, bf16[128,1280]{1,0:T(8,128)(2,1)S(1)}, u32[]{:S(2)}, u32[]{:S(2)}) collective-permute-start(bf16[128,1280]{1,0:T(8,128)(2,1)S(1)} %get-tuple-element.70), channel_id=1, source_target_pairs={{0,1},{1,0},{2,3},{3,2},{4,5},{5,4},{6,7},{7,6},{8,9},{9,8},{10,11... | collective-permute-start | bytes 983048 | tf_op jit(solution)/shard_map/ppermute | solution.py:466
  56.0 0.0 collective-permute-done.10.pushed_ref
  56.0 0.7 %add.1 = (bf16[128,1024]{1,0:T(8,128)(2,1)}, bf16[128,1024]{1,0:T(8,128)(2,1)S(1)}) custom-call(f32[128,1024]{1,0:T(8,128)S(1)} %get-tuple-element.63.own_ref, bf16[32,1024]{1,0:T(8,128)(2,1)S(1)} %collective-permute-done.10.pushed_ref), custom_call_target="tpu_custom_call" | custom-call | flops 220000000 | tf_op jit(solution)/shard_map/add/pallas_call | solution.py:435
  56.7 6.1 %collective-permute-start.13 = (bf16[128,1024]{1,0:T(8,128)(2,1)S(1)}, bf16[128,1024]{1,0:T(8,128)(2,1)S(1)}, u32[]{:S(2)}, u32[]{:S(2)}) collective-permute-start(bf16[128,1024]{1,0:T(8,128)(2,1)S(1)} %get-tuple-element.72), channel_id=1, source_target_pairs={{8,0},{16,8},{24,16},{9,1},{17,9},{25,17},{10,2},{18,10},{26,18},{... | collective-permute-start | bytes 786440 | tf_op jit(solution)/shard_map/ppermute | solution.py:617
  62.9 5.1 %collective-permute-done.13.other_cot = bf16[128,1024]{1,0:T(8,128)(2,1)S(1)} collective-permute-done((bf16[128,1024]{1,0:T(8,128)(2,1)S(1)}, bf16[128,1024]{1,0:T(8,128)(2,1)S(1)}, u32[]{:S(2)}, u32[]{:S(2)}) %collective-permute-start.13) | collective-permute-done | bytes 262176 | tf_op jit(solution)/shard_map/ppermute | solution.py:617
  68.0 0.0 collective-permute-done.12.got0
  68.0 1.4 %finish.1 = (f32[128,2,1024]{2,1,0:T(2,128)}, f32[2,3,128,32]{3,2,1,0:T(8,128)}, bf16[128,1024]{1,0:T(8,128)(2,1)}) custom-call(f32[128,1024]{1,0:T(8,128)S(1)} %get-tuple-element.66.mix1, f32[128,1280]{1,0:T(8,128)S(1)} %get-tuple-element.69.own0, bf16[128,1024]{1,0:T(8,128)(2,1)S(1)} %collective-permute-done.11.refs_3_.got_mix1, ...), custom_call_target="tpu_custom_call" | custom-call | flops 770000000 | tf_op jit(solution)/shard_map/finish/pallas_call | solution.py:435
  (3 shorter events, 0.1 us)
Async XLA Ops:
  0.6 9.4 %collective-permute-start.1 = (bf16[128,1024]{1,0:T(8,128)(2,1)}, bf16[128,1024]{1,0:T(8,128)(2,1)S(1)}, u32[]{:S(2)}, u32[]{:S(2)}) collective-permute-start(bf16[128,1024]{1,0:T(8,128)(2,1)} %bitcast.17), channel_id=1, source_target_pairs={{0,2},{1,3},{2,6},{3,7},{6,4},{7,5},{4,0},{5,1},{8,10},{9,11},{10,... | collective-permute-start | bytes 786440 | tf_op jit(solution)/shard_map/ppermute | solution.py:461
  3.7 6.0 %collective-permute-start = (bf16[32,1024]{1,0:T(8,128)(2,1)S(1)}, bf16[32,1024]{1,0:T(8,128)(2,1)S(1)}, u32[]{:S(2)}, u32[]{:S(2)}) collective-permute-start(bf16[32,1024]{1,0:T(8,128)(2,1)S(1)} %slice_bitcast_fusion), channel_id=1, source_target_pairs={{0,1},{1,0},{2,3},{3,2},{4,5},{5,4},{6,7},{7,6},{8,9},{9,8},{10,11... | collective-permute-start | bytes 196616 | tf_op jit(solution)/shard_map/ppermute | solution.py:466
  10.1 7.5 %collective-permute-start.3 = (bf16[128,1024]{1,0:T(8,128)(2,1)S(1)}, bf16[128,1024]{1,0:T(8,128)(2,1)S(1)}, u32[]{:S(2)}, u32[]{:S(2)}) collective-permute-start(bf16[128,1024]{1,0:T(8,128)(2,1)S(1)} %get-tuple-element.42), channel_id=1, source_target_pairs={{0,2},{1,3},{2,6},{3,7},{6,4},{7,5},{4,0},{5,1},{8,10},{9,11},{10,... | collective-permute-start | bytes 786440 | tf_op jit(solution)/shard_map/ppermute | solution.py:461
  12.1 11.8 %collective-permute-start.7 = (bf16[144,1024]{1,0:T(8,128)(2,1)S(1)}, bf16[144,1024]{1,0:T(8,128)(2,1)S(1)}, u32[]{:S(2)}, u32[]{:S(2)}) collective-permute-start(bf16[144,1024]{1,0:T(8,128)(2,1)S(1)} %get-tuple-element.53.refs_0_), channel_id=1, source_target_pairs={{0,2},{1,3},{2,6},{3,7},{6,4},{7,5},{4,0},{5,1},{8,10},{9,11},{10,... | collective-permute-start | bytes 884744 | tf_op jit(solution)/shard_map/ppermute | solution.py:461
  17.7 11.9 %collective-permute-start.5 = (bf16[128,1024]{1,0:T(8,128)(2,1)S(1)}, bf16[128,1024]{1,0:T(8,128)(2,1)S(1)}, u32[]{:S(2)}, u32[]{:S(2)}) collective-permute-start(bf16[128,1024]{1,0:T(8,128)(2,1)S(1)} %get-tuple-element.44), channel_id=1, source_target_pairs={{0,2},{1,3},{2,6},{3,7},{6,4},{7,5},{4,0},{5,1},{8,10},{9,11},{10,... | collective-permute-start | bytes 786440 | tf_op jit(solution)/shard_map/ppermute | solution.py:461
  24.7 11.2 %collective-permute-start.8 = (bf16[144,1024]{1,0:T(8,128)(2,1)S(1)}, bf16[144,1024]{1,0:T(8,128)(2,1)S(1)}, u32[]{:S(2)}, u32[]{:S(2)}) collective-permute-start(bf16[144,1024]{1,0:T(8,128)(2,1)S(1)} %get-tuple-element.54), channel_id=1, source_target_pairs={{0,2},{1,3},{2,6},{3,7},{6,4},{7,5},{4,0},{5,1},{8,10},{9,11},{10,... | collective-permute-start | bytes 884744 | tf_op jit(solution)/shard_map/ppermute | solution.py:461
  25.8 11.2 %collective-permute-start.2 = (bf16[32,1024]{1,0:T(8,128)(2,1)S(1)}, bf16[32,1024]{1,0:T(8,128)(2,1)S(1)}, u32[]{:S(2)}, u32[]{:S(2)}) collective-permute-start(bf16[32,1024]{1,0:T(8,128)(2,1)S(1)} %get-tuple-element.41), channel_id=1, source_target_pairs={{0,1},{1,0},{2,3},{3,2},{4,5},{5,4},{6,7},{7,6},{8,9},{9,8},{10,11... | collective-permute-start | bytes 196616 | tf_op jit(solution)/shard_map/ppermute | solution.py:466
  26.0 11.0 %collective-permute-start.4 = (bf16[32,1024]{1,0:T(8,128)(2,1)S(1)}, bf16[32,1024]{1,0:T(8,128)(2,1)S(1)}, u32[]{:S(2)}, u32[]{:S(2)}) collective-permute-start(bf16[32,1024]{1,0:T(8,128)(2,1)S(1)} %get-tuple-element.43), channel_id=1, source_target_pairs={{0,1},{1,0},{2,3},{3,2},{4,5},{5,4},{6,7},{7,6},{8,9},{9,8},{10,11... | collective-permute-start | bytes 196616 | tf_op jit(solution)/shard_map/ppermute | solution.py:466
  29.6 7.4 %collective-permute-start.6 = (bf16[32,1024]{1,0:T(8,128)(2,1)S(1)}, bf16[32,1024]{1,0:T(8,128)(2,1)S(1)}, u32[]{:S(2)}, u32[]{:S(2)}) collective-permute-start(bf16[32,1024]{1,0:T(8,128)(2,1)S(1)} %relay.6), channel_id=1, source_target_pairs={{0,1},{1,0},{2,3},{3,2},{4,5},{5,4},{6,7},{7,6},{8,9},{9,8},{10,11... | collective-permute-start | bytes 196616 | tf_op jit(solution)/shard_map/ppermute | solution.py:466
  35.9 7.3 %collective-permute-start.9 = (bf16[144,1024]{1,0:T(8,128)(2,1)S(1)}, bf16[144,1024]{1,0:T(8,128)(2,1)S(1)}, u32[]{:S(2)}, u32[]{:S(2)}) collective-permute-start(bf16[144,1024]{1,0:T(8,128)(2,1)S(1)} %collective-permute-done.8.refs_2_), channel_id=1, source_target_pairs={{0,2},{1,3},{2,6},{3,7},{6,4},{7,5},{4,0},{5,1},{8,10},{9,11},{10,... | collective-permute-start | bytes 884744 | tf_op jit(solution)/shard_map/ppermute | solution.py:461
  43.7 7.1 %collective-permute-start.11 = (bf16[128,1024]{1,0:T(8,128)(2,1)S(1)}, bf16[128,1024]{1,0:T(8,128)(2,1)S(1)}, u32[]{:S(2)}, u32[]{:S(2)}) collective-permute-start(bf16[128,1024]{1,0:T(8,128)(2,1)S(1)} %get-tuple-element.68), channel_id=1, source_target_pairs={{0,1},{1,0},{2,3},{3,2},{4,5},{5,4},{6,7},{7,6},{8,9},{9,8},{10,11... | collective-permute-start | bytes 786440 | tf_op jit(solution)/shard_map/ppermute | solution.py:466
  49.6 6.4 %collective-permute-start.10 = (bf16[32,1024]{1,0:T(8,128)(2,1)S(1)}, bf16[32,1024]{1,0:T(8,128)(2,1)S(1)}, u32[]{:S(2)}, u32[]{:S(2)}) collective-permute-start(bf16[32,1024]{1,0:T(8,128)(2,1)S(1)} %get-tuple-element.64.refs_2_), channel_id=1, source_target_pairs={{1,0},{2,1},{3,2},{4,3},{5,4},{6,5},{7,6},{9,8},{10,9},{11,10},{12... | collective-permute-start | bytes 196616 | tf_op jit(solution)/shard_map/ppermute | solution.py:602
  53.8 14.2 %collective-permute-start.12 = (bf16[128,1280]{1,0:T(8,128)(2,1)S(1)}, bf16[128,1280]{1,0:T(8,128)(2,1)S(1)}, u32[]{:S(2)}, u32[]{:S(2)}) collective-permute-start(bf16[128,1280]{1,0:T(8,128)(2,1)S(1)} %get-tuple-element.70), channel_id=1, source_target_pairs={{0,1},{1,0},{2,3},{3,2},{4,5},{5,4},{6,7},{7,6},{8,9},{9,8},{10,11... | collective-permute-start | bytes 983048 | tf_op jit(solution)/shard_map/ppermute | solution.py:466
  56.7 11.3 %collective-permute-start.13 = (bf16[128,1024]{1,0:T(8,128)(2,1)S(1)}, bf16[128,1024]{1,0:T(8,128)(2,1)S(1)}, u32[]{:S(2)}, u32[]{:S(2)}) collective-permute-start(bf16[128,1024]{1,0:T(8,128)(2,1)S(1)} %get-tuple-element.72), channel_id=1, source_target_pairs={{8,0},{16,8},{24,16},{9,1},{17,9},{25,17},{10,2},{18,10},{26,18},{... | collective-permute-start | bytes 786440 | tf_op jit(solution)/shard_map/ppermute | solution.py:617

commit v5 on v4

--- a/solution.py
+++ b/solution.py
@@ -84,7 +84,8 @@
 def arrival(p, blocks):
     z = lax.axis_index("seq") // SPAN
     place = jnp.where(z % 2 == 1, (z + 1) // 2, jnp.where(z == 0, 0, blocks - z // 2))
-    return ring_place(lax.rem(place - p + blocks, blocks), blocks)
+    hops = jnp.where(jnp.asarray(p) % 2 == 1, (p + 1) // 2, blocks - p // 2)
+    return ring_place(lax.rem(place - hops + 2 * blocks, blocks), blocks)
 
 
 def on_last_section():
@@ -326,10 +327,9 @@
     split_pair(g_ref.shape[2] // blocks, total_ref, own_ref, send_ref)
 
 
-def long_conv_sums(blocks, group_size, mid_ref, d_ref, fold, total_ref, columns):
-    row_count, channels = mid_ref.shape[1:]
+def long_conv_sums(blocks, group_size, mid_ref, d_ref, fold, total_ref, columns, first_slab, wide):
+    row_count = mid_ref.shape[1]
     rows = blocks * row_count
-    _, wide, first_slab = pair_slabs(channels, blocks)
     for i in range(wide):
         slab = first_slab + i
         taps = [mid_ref[2 - k : 2 - k + blocks, :, lanes(slab)].reshape(rows, SLAB) for k in range(3)]
@@ -357,7 +357,8 @@
 
     chunks(blocks, back)
     if not early:
-        long_conv_sums(blocks, group_size, mid_ref, d_ref, fold, last_ref, slice(0, SLAB))
+        _, wide, first_slab = pair_slabs(channels, blocks)
+        long_conv_sums(blocks, group_size, mid_ref, d_ref, fold, last_ref, slice(0, SLAB), first_slab, wide)
 
 
 def own_kernel(x_ref, between_ref, weights, mixes, push_ref, sum_ref):
@@ -380,10 +381,8 @@
             sum_ref[:, cut(slab)] = between_ref[z, :, cut(slab)].astype(F32) + moved[0] + extended[HALO:]
 
 
-def short_kernel(blocks, group_size, x_ref, between_ref, weights, mixes, fold, *refs):
-    *long_refs, _, _, own_ref, send_ref, total_ref = refs
+def short_sums(blocks, group_size, first_slab, wide, x_ref, between_ref, weights, mixes, fold, total_ref):
     row_count, channels = between_ref.shape[1:]
-    pair, wide, first_slab = pair_slabs(channels, blocks)
     rows = blocks * row_count
     between = between_ref[...].reshape(rows, channels)
     for i in range(wide):
@@ -396,12 +395,27 @@
         dpre = gate_grad(tanh, sig, nt(between, mixes[0, lanes(slab), :]))
         total_ref[cut(i), :channels] = tn((tanh * sig).astype(BF16), between)
         total_ref[cut(i), channels : channels + SLAB] = weight_sums(group_size, taps, dpre, fold[...])
+
+
+def short_kernel(blocks, group_size, x_ref, between_ref, weights, mixes, fold, last, *refs):
+    own_ref, send_ref, total_ref = refs[-3:]
+    channels = between_ref.shape[2]
+    pair, wide, first_slab = pair_slabs(channels, blocks)
+    short_sums(blocks, group_size, first_slab, wide, x_ref, between_ref, weights, mixes, fold, total_ref)
+    total_ref[:, channels + SLAB :] = last[...]
+    split_pair(pair, total_ref, own_ref, send_ref)
+
+
+def half_kernel(blocks, group_size, partner, x_ref, between_ref, weights, mixes, fold, mid_ref, d_ref, *refs):
+    out_ref, total_ref = refs[-2:]
+    channels, share = between_ref.shape[2], out_ref.shape[0]
+    place = lax.axis_index("seq")
+    owner = place + (1 - 2 * (place % SPAN) if partner else 0)
+    first_slab, wide = owner * share // SLAB, share // SLAB
+    short_sums(blocks, group_size, first_slab, wide, x_ref, between_ref, weights, mixes, fold, total_ref)
     last = slice(channels + SLAB, channels + 2 * SLAB)
-    if len(long_refs) > 1:
-        long_conv_sums(blocks, group_size, *long_refs, fold, total_ref, last)
-    else:
-        total_ref[:, last] = long_refs[0][...]
-    split_pair(pair, total_ref, own_ref, send_ref)
+    long_conv_sums(blocks, group_size, mid_ref, d_ref, fold, total_ref, last, first_slab, wide)
+    out_ref[...] = total_ref[...].astype(out_ref.dtype)
 
 
 def finish_kernel(group_size, mix1, own0, got_mix1, got0, last_cot, other_cot, mix_ref, conv_ref, cot_ref):
@@ -417,7 +431,7 @@
             conv_ref[layer, k] = total[:, begin : begin + width]
 
 
-def add_kernel(own_ref, pushed_ref, *out_refs):
+def add_kernel(own_ref, pushed_ref, _, *out_refs):
     rest = own_ref.shape[0] - HALO
     for out_ref in out_refs:
         out_ref[:rest, :] = own_ref[:rest, :].astype(BF16)
@@ -457,10 +471,9 @@
     ring = [0] + list(range(1, blocks, 2)) + [b for b in range(blocks - 1, 0, -1) if b % 2 == 0]
     hops = list(zip(ring, ring[1:] + ring[:1]))
 
-    def step(value):
-        return lax.ppermute(
-            value, "seq", [(a * SPAN + y, b * SPAN + y) for a, b in hops for y in range(SPAN)]
-        )
+    def step(value, p):
+        pairs = [(a, b) if p % 2 else (b, a) for a, b in hops]
+        return lax.ppermute(value, "seq", [(a * SPAN + y, b * SPAN + y) for a, b in pairs for y in range(SPAN)])
 
     def swap(value):
         return lax.ppermute(value, "seq", [(b, b + 1 - 2 * (b % 2)) for b in range(seq)])
@@ -521,24 +534,28 @@
 
     begun = []
     inputs, cots = [far(first_input)], [own_cot]
-    sent_input = first_input
+    relayed, sent_cot = [first_input, first_input], own_cot
     for p in range(1, blocks):
-        inputs.append(step(sent_input))
+        inputs.append(step(relayed[p - 1], p))
         if p == 1:
-            sent_input, tail = relay(1, inputs[1], tails[0], fold)
-            sent_cot = own_cot
-        elif p < blocks - 1:
-            sent_input, tail = relay(1, inputs[p])
-            if resident and p == blocks - 2:
-                begun = begin(0, blocks - 1, inputs, [])
-                sent_cot, _ = relay(1, sent_cot, begun[1])
+            sent_input, tail = relay(1, inputs[1], fold)
+            relayed.append(sent_input)
         else:
+            if p == 2:
+                sent_cot, _ = relay(1, own_cot, inputs[p], tails[0])
             (tail,) = relay(0, inputs[p])
+            relayed.append(inputs[p])
         tails.append(swap(tail))
-        sent_cot = step(sent_cot)
-        cots.append(sent_cot)
     if resident:
+        begun = begin(0, blocks - 1, inputs[:-1], [])
         begun = begin(blocks - 1, 1, inputs[-1:], begun)
+    relayed = [sent_cot, sent_cot]
+    for p in range(1, blocks):
+        if p == 2 and resident:
+            relayed[1], _ = relay(1, sent_cot, tail)
+        cots.append(step(relayed[p - 1], p))
+        relayed.append(cots[p])
+    if resident:
         inputs = []
     operands = [*inputs, *tails, weights, mixes, head, *begun]
     x, mid, pre, hazard = run(
@@ -601,18 +618,41 @@
     )
     pushed = lax.ppermute(push, "seq", [(b, b - 1) for b in range(1, seq)])
     sums = channels + 2 * SLAB
-    own0, send0 = run(
-        functools.partial(short_kernel, blocks, group_size),
-        [((share, sums), F32), ((share, sums), BF16)],
-        [x, between, weights, mixes, fold] + ([mid, last] if early else [last]) + [push, got_mix1],
-        [((wide, sums), F32)],
-        name="short_backward",
-        far=(7, 8) if early else (6, 7),
-        us=8,
-    )
+    if early:
+        half = functools.partial(half_kernel, blocks, group_size)
+        held = [x, between, weights, mixes, fold, mid, last]
+        (send0,) = run(
+            functools.partial(half, True),
+            [((share, sums), BF16)],
+            [*held, push, got_mix1],
+            [((share, sums), F32)],
+            name="short_partner",
+            far=(7, 8),
+            us=4,
+        )
+    else:
+        own0, send0 = run(
+            functools.partial(short_kernel, blocks, group_size),
+            [((share, sums), F32), ((share, sums), BF16)],
+            [x, between, weights, mixes, fold, last],
+            [((wide, sums), F32)],
+            name="short_backward",
+        )
     got0 = swap(send0)
     rows_out = ((row_count, channels), BF16)
-    input_gradient, sent_gradient = run(add_kernel, [rows_out] * 2, [own_sum, pushed], name="add", final=(0,), us=0.4)
+    input_gradient, sent_gradient = run(
+        add_kernel, [rows_out] * 2, [own_sum, pushed, send0], name="add", final=(0,), far=(2,), us=0.4
+    )
+    if early:
+        (own0,) = run(
+            functools.partial(half, False),
+            [((share, sums), F32)],
+            [*held, sent_gradient],
+            [((share, sums), F32)],
+            name="short_own",
+            far=(7,),
+            us=8,
+        )
     count = lax.axis_size("section")
     received = lax.ppermute(sent_gradient, "section", [(s, s - 1) for s in range(1, count)])
     mix_share, conv_share, next_cot = run(

time: 69.7 us -> 67.3 us (0.966)
  waiting for transfers between devices: 19.9 us -> 14.8 us
  starting transfers between devices: 22.2 us -> 24.2 us
  Pallas kernels: 25.7 us -> 26.4 us
    ppermute x6, waiting for transfers between devices: 14.7 us -> 8.25 us  [step(): lax.ppermute(value, 'seq', [(a * SPAN + y, b * SPAN + y) for a, b in pair...]
    ppermute x6, waiting for transfers between devices: 0.02 us -> 2.18 us  [swap(): lax.ppermute(value, 'seq', [(b, b + 1 - 2 * (b % 2)) for b in range(seq)])]
    ppermute x1, starting transfers between devices: 6.12 us -> 7.59 us  [body(): lax.ppermute(sent_gradient, 'section', [(s, s - 1) for s in range(1, coun...]
    ppermute x1, waiting for transfers between devices: 5.14 us -> 3.7 us  [body(): lax.ppermute(sent_gradient, 'section', [(s, s - 1) for s in range(1, coun...]
    ppermute x6, starting transfers between devices: 5.98 us -> 6.76 us  [swap(): lax.ppermute(value, 'seq', [(b, b + 1 - 2 * (b % 2)) for b in range(seq)])]
    pallas_call x15 -> x17, Pallas kernels: 25.7 us -> 26.4 us  [call(): pl.pallas_call(kernel, out_shape=[of(shape, kind) for of, (shape, kind) i...]
  transfers between devices with their start and end apart: 14 -> 14, of which waited for: 7 -> 7; matrix products, arithmetic and copies ran while one was open for 1% -> 1% of each run, Pallas kernels for 34% -> 36%
where the time goes in v5:
time: 67.3 us; the launch traced here: 67 us
  Pallas kernels  26.4 us (39%)
  starting transfers between devices  24.2 us (36%)
  waiting for transfers between devices  14.8 us (22%)
  local copies, waits for them, and re-layouts  0.84 us (1%)
  between operations  0.81 us (1%)
    pallas_call x17, Pallas kernels, call(): pl.pallas_call(kernel, out_shape=[of(shape, kind) for of, (shape, kind) i...  26.4 us
    ppermute x6, starting transfers between devices, step(): lax.ppermute(value, 'seq', [(a * SPAN + y, b * SPAN + y) for a, b in pair...  8.51 us
    ppermute x6, waiting for transfers between devices, step(): lax.ppermute(value, 'seq', [(a * SPAN + y, b * SPAN + y) for a, b in pair...  8.25 us
    ppermute x1, starting transfers between devices, body(): lax.ppermute(sent_gradient, 'section', [(s, s - 1) for s in range(1, coun...  7.59 us
    ppermute x6, starting transfers between devices, swap(): lax.ppermute(value, 'seq', [(b, b + 1 - 2 * (b % 2)) for b in range(seq)])  6.76 us
    ppermute x1, waiting for transfers between devices, body(): lax.ppermute(sent_gradient, 'section', [(s, s - 1) for s in range(1, coun...  3.7 us
    ppermute x6, waiting for transfers between devices, swap(): lax.ppermute(value, 'seq', [(b, b + 1 - 2 * (b % 2)) for b in range(seq)])  2.18 us
  transfers between devices with their start and end apart: 14, of which 7 were waited for; matrix products, arithmetic and copies ran while one was open for 1% of the time, Pallas kernels for 36%

profile of v5, /device:TPU:1, one launch (start us, length us, event | category | flops | bytes accessed | tf_op | source)
XLA Modules:
  0.0 67.0 jit_solution(10670717092634720079)
XLA Ops:
  0.6 2.2 %collective-permute-start.1 = (bf16[128,1024]{1,0:T(8,128)(2,1)}, bf16[128,1024]{1,0:T(8,128)(2,1)S(1)}, u32[]{:S(2)}, u32[]{:S(2)}) collective-permute-start(bf16[128,1024]{1,0:T(8,128)(2,1)} %bitcast.17), channel_id=1, source_target_pairs={{0,2},{1,3},{2,6},{3,7},{6,4},{7,5},{4,0},{5,1},{8,10},{9,11},{10,... | collective-permute-start | bytes 786440 | tf_op jit(solution)/shard_map/ppermute | solution.py:476
  2.8 1.1 %collective-permute-start.3 = (bf16[128,1024]{1,0:T(8,128)(2,1)}, bf16[128,1024]{1,0:T(8,128)(2,1)S(1)}, u32[]{:S(2)}, u32[]{:S(2)}) collective-permute-start(bf16[128,1024]{1,0:T(8,128)(2,1)} %bitcast.18), channel_id=1, source_target_pairs={{2,0},{3,1},{6,2},{7,3},{4,6},{5,7},{0,4},{1,5},{10,8},{11,9},{14,... | collective-permute-start | bytes 786440 | tf_op jit(solution)/shard_map/ppermute | solution.py:476
  3.9 4.8 %weights.1 = (bf16[2,8,384,256]{3,2,1,0:T(8,128)(2,1)S(1)}, bf16[128,768]{1,0:T(8,128)(2,1)S(1)}, bf16[2,1024,1024]{2,1,0:T(8,128)(2,1)S(1)}, bf16[64,1024]{1,0:T(8,128)(2,1)S(1)}, bf16[144,1024]{1,0:T(8,128)(2,1)S(1)}) custom-call(bf16[2,3,512,64]{3,2,1,0:T(8,128)(2,1)} %bitcast.21, bf16[2,1024,1024]{2,1,0:T(8,128)(2,1)} %bitcast.20, ...), custom_call_target="tpu_custom_call" | custom-call | flops 1924999936 | tf_op jit(solution)/shard_map/weights/pallas_call | solution.py:449
  8.7 1.5 %collective-permute-done.1.refs_0_.refs_1_ = bf16[128,1024]{1,0:T(8,128)(2,1)S(1)} collective-permute-done((bf16[128,1024]{1,0:T(8,128)(2,1)}, bf16[128,1024]{1,0:T(8,128)(2,1)S(1)}, u32[]{:S(2)}, u32[]{:S(2)}) %collective-permute-start.1) | collective-permute-done | bytes 262176 | tf_op jit(solution)/shard_map/ppermute | solution.py:476
  10.2 1.2 %collective-permute-start.5 = (bf16[128,1024]{1,0:T(8,128)(2,1)S(1)}, bf16[128,1024]{1,0:T(8,128)(2,1)S(1)}, u32[]{:S(2)}, u32[]{:S(2)}) collective-permute-start(bf16[128,1024]{1,0:T(8,128)(2,1)S(1)} %get-tuple-element.39), channel_id=1, source_target_pairs={{0,2},{1,3},{2,6},{3,7},{6,4},{7,5},{4,0},{5,1},{8,10},{9,11},{10,... | collective-permute-start | bytes 786440 | tf_op jit(solution)/shard_map/ppermute | solution.py:476
  11.3 0.8 %slice_bitcast_fusion = bf16[32,1024]{1,0:T(8,128)(2,1)S(1)} fusion(bf16[1,128,1024]{2,1,0:T(8,128)(2,1)} %param.7), kind=kLoop, calls=%fused_computation | loop fusion | bytes 131072 | tf_op jit(solution)/shard_map/slice | solution.py:499
  12.1 1.2 %collective-permute-start = (bf16[32,1024]{1,0:T(8,128)(2,1)S(1)}, bf16[32,1024]{1,0:T(8,128)(2,1)S(1)}, u32[]{:S(2)}, u32[]{:S(2)}) collective-permute-start(bf16[32,1024]{1,0:T(8,128)(2,1)S(1)} %slice_bitcast_fusion), channel_id=1, source_target_pairs={{0,1},{1,0},{2,3},{3,2},{4,5},{5,4},{6,7},{7,6},{8,9},{9,8},{10,11... | collective-permute-start | bytes 196616 | tf_op jit(solution)/shard_map/ppermute | solution.py:479
  13.4 2.2 %collective-permute-done.refs_0_.refs_2_ = bf16[32,1024]{1,0:T(8,128)(2,1)S(1)} collective-permute-done((bf16[32,1024]{1,0:T(8,128)(2,1)S(1)}, bf16[32,1024]{1,0:T(8,128)(2,1)S(1)}, u32[]{:S(2)}, u32[]{:S(2)}) %collective-permute-start) | collective-permute-done | bytes 65568 | tf_op jit(solution)/shard_map/ppermute | solution.py:479
  15.6 1.0 %collective-permute-done.3.refs_0_.refs_2_.refs_1_ = bf16[128,1024]{1,0:T(8,128)(2,1)S(1)} collective-permute-done((bf16[128,1024]{1,0:T(8,128)(2,1)}, bf16[128,1024]{1,0:T(8,128)(2,1)S(1)}, u32[]{:S(2)}, u32[]{:S(2)}) %collective-permute-start.3) | collective-permute-done | bytes 262176 | tf_op jit(solution)/shard_map/ppermute | solution.py:476
  16.5 0.7 %relay.8 = (bf16[144,1024]{1,0:T(8,128)(2,1)S(1)}, bf16[32,1024]{1,0:T(8,128)(2,1)}) custom-call(bf16[144,1024]{1,0:T(8,128)(2,1)S(1)} %get-tuple-element.48.refs_0_, bf16[128,1024]{1,0:T(8,128)(2,1)S(1)} %collective-permute-done.3.refs_0_.refs_2_.refs_1_, bf16[32,1024]{1,0:T(8,128)(2,1)S(1)} %collective-permute-done.refs_0_.refs_2_), custom_call_target="tpu_custom_call" | custom-call | flops 165000000 | tf_op jit(solution)/shard_map/relay/pallas_call | solution.py:449
  17.2 2.5 %collective-permute-start.7 = (bf16[144,1024]{1,0:T(8,128)(2,1)S(1)}, bf16[144,1024]{1,0:T(8,128)(2,1)S(1)}, u32[]{:S(2)}, u32[]{:S(2)}) collective-permute-start(bf16[144,1024]{1,0:T(8,128)(2,1)S(1)} %get-tuple-element.49.refs_0_), channel_id=1, source_target_pairs={{0,2},{1,3},{2,6},{3,7},{6,4},{7,5},{4,0},{5,1},{8,10},{9,11},{10,... | collective-permute-start | bytes 884744 | tf_op jit(solution)/shard_map/ppermute | solution.py:476
  19.8 3.5 %collective-permute-done.5.refs_0_ = bf16[128,1024]{1,0:T(8,128)(2,1)S(1)} collective-permute-done((bf16[128,1024]{1,0:T(8,128)(2,1)S(1)}, bf16[128,1024]{1,0:T(8,128)(2,1)S(1)}, u32[]{:S(2)}, u32[]{:S(2)}) %collective-permute-start.5) | collective-permute-done | bytes 262176 | tf_op jit(solution)/shard_map/ppermute | solution.py:476
  23.2 0.7 %relay.9 = (bf16[144,1024]{1,0:T(8,128)(2,1)S(1)}, bf16[32,1024]{1,0:T(8,128)(2,1)}) custom-call(bf16[144,1024]{1,0:T(8,128)(2,1)S(1)} %get-tuple-element.49.refs_0_, bf16[32,1024]{1,0:T(8,128)(2,1)S(1)} %relay.7.refs_1_), custom_call_target="tpu_custom_call" | custom-call | flops 165000000 | tf_op jit(solution)/shard_map/relay/pallas_call | solution.py:449
  23.9 0.1 collective-permute-start.9
  24.0 1.3 %collective-permute-start.4 = (bf16[32,1024]{1,0:T(8,128)(2,1)S(1)}, bf16[32,1024]{1,0:T(8,128)(2,1)S(1)}, u32[]{:S(2)}, u32[]{:S(2)}) collective-permute-start(bf16[32,1024]{1,0:T(8,128)(2,1)S(1)} %relay.6), channel_id=1, source_target_pairs={{0,1},{1,0},{2,3},{3,2},{4,5},{5,4},{6,7},{7,6},{8,9},{9,8},{10,11... | collective-permute-start | bytes 196616 | tf_op jit(solution)/shard_map/ppermute | solution.py:479
  25.3 0.2 collective-permute-start.2
  25.6 1.2 %collective-permute-start.6 = (bf16[32,1024]{1,0:T(8,128)(2,1)S(1)}, bf16[32,1024]{1,0:T(8,128)(2,1)S(1)}, u32[]{:S(2)}, u32[]{:S(2)}) collective-permute-start(bf16[32,1024]{1,0:T(8,128)(2,1)S(1)} %relay.7.refs_1_), channel_id=1, source_target_pairs={{0,1},{1,0},{2,3},{3,2},{4,5},{5,4},{6,7},{7,6},{8,9},{9,8},{10,11... | collective-permute-start | bytes 196616 | tf_op jit(solution)/shard_map/ppermute | solution.py:479
  26.8 2.7 %begin.2 = (bf16[5,160,1024]{2,1,0:T(8,128)(2,1)S(1)}, bf16[6,128,1024]{2,1,0:T(8,128)(2,1)S(1)}) custom-call(bf16[128,1024]{1,0:T(8,128)(2,1)} %bitcast.19, bf16[128,1024]{1,0:T(8,128)(2,1)S(1)} %collective-permute-done.1.refs_0_.refs_1_, bf16[128,1024]{1,0:T(8,128)(2,1)S(1)} %collective-permute-done.3.refs_0_.refs_2_.refs_1_, ...), custom_call_target="tpu_custom_call" | custom-call | flops 990000000 | tf_op jit(solution)/shard_map/begin/pallas_call | solution.py:449
  29.5 0.9 %begin.3 = (bf16[5,160,1024]{2,1,0:T(8,128)(2,1)S(1)}, bf16[6,128,1024]{2,1,0:T(8,128)(2,1)S(1)}) custom-call(bf16[128,1024]{1,0:T(8,128)(2,1)S(1)} %collective-permute-done.5.refs_0_, bf16[2,8,384,256]{3,2,1,0:T(8,128)(2,1)S(1)} %get-tuple-element.40.refs_3_.refs_1_.refs_4_.weights, ...), custom_call_target="tpu_custom_call", output_to_operand_aliasing={{0}: (3, {}), {1}: (4, {})} | custom-call | flops 330000000 | tf_op jit(solution)/shard_map/begin/pallas_call | solution.py:449
  30.4 0.0 collective-permute-done.7.refs_1_
  30.4 1.5 %collective-permute-start.8 = (bf16[144,1024]{1,0:T(8,128)(2,1)S(1)}, bf16[144,1024]{1,0:T(8,128)(2,1)S(1)}, u32[]{:S(2)}, u32[]{:S(2)}) collective-permute-start(bf16[144,1024]{1,0:T(8,128)(2,1)S(1)} %collective-permute-done.7.refs_1_), channel_id=1, source_target_pairs={{0,2},{1,3},{2,6},{3,7},{6,4},{7,5},{4,0},{5,1},{8,10},{9,11},{10,... | collective-permute-start | bytes 884744 | tf_op jit(solution)/shard_map/ppermute | solution.py:476
  31.9 0.0 collective-permute-done.4.refs_2_
  31.9 0.0 collective-permute-done.2.refs_1_
  31.9 0.0 collective-permute-done.6.refs_3_
  31.9 3.1 %forward.1 = (bf16[5,160,1024]{2,1,0:T(8,128)(2,1)S(1)}, bf16[6,128,1024]{2,1,0:T(8,128)(2,1)S(1)}, bf16[4,128,2048]{2,1,0:T(8,128)(2,1)S(1)}, f32[4,64,128]{2,1,0:T(8,128)S(1)}) custom-call(bf16[32,1024]{1,0:T(8,128)(2,1)S(1)} %collective-permute-done.refs_0_.refs_2_, ...), custom_call_target="tpu_custom_call", output_to_operand_aliasing={{0}: (7, {}), {1}: (8, {})} | custom-call | flops 1650000000 | tf_op jit(solution)/shard_map/forward/pallas_call | solution.py:449
  35.0 0.0 collective-permute-done.9.refs_2_
  35.1 2.4 %early.1 = (bf16[4,128,1024]{2,1,0:T(8,128)(2,1)S(1)}, bf16[6,128,2048]{2,1,0:T(8,128)(2,1)S(1)}, f32[256,1024]{1,0:T(8,128)S(1)}) custom-call(bf16[144,1024]{1,0:T(8,128)(2,1)S(1)} %get-tuple-element.48.refs_0_, bf16[144,1024]{1,0:T(8,128)(2,1)S(1)} %collective-permute-done.7.refs_1_, bf16[144,1024]{1,0:T(8,128)(2,1)S(1)} %collective-permute-done.9.refs_2_, ...), custom_call_target="tpu_custom_call" | custom-call | flops 2200000000 | tf_op jit(solution)/shard_map/early/pallas_call | solution.py:449
  37.5 2.4 %collective-permute-done.8.refs_0_ = bf16[144,1024]{1,0:T(8,128)(2,1)S(1)} collective-permute-done((bf16[144,1024]{1,0:T(8,128)(2,1)S(1)}, bf16[144,1024]{1,0:T(8,128)(2,1)S(1)}, u32[]{:S(2)}, u32[]{:S(2)}) %collective-permute-start.8) | collective-permute-done | bytes 294944 | tf_op jit(solution)/shard_map/ppermute | solution.py:476
  39.9 0.6 long_mix.1
  40.5 0.6 collective-permute-start.11
  41.1 2.7 %long_backward.1 = (bf16[4,128,1024]{2,1,0:T(8,128)(2,1)S(1)}, bf16[6,128,2048]{2,1,0:T(8,128)(2,1)S(1)}) custom-call(bf16[4,128,1024]{2,1,0:T(8,128)(2,1)S(1)} %get-tuple-element.55.g_ref, bf16[6,128,1024]{2,1,0:T(8,128)(2,1)S(1)} %get-tuple-element.56.mid_ref, ...), custom_call_target="tpu_custom_call", output_to_operand_aliasing={{1}: (6, {})} | custom-call | flops 1870000000 | tf_op jit(solution)/shard_map/long_backward/pallas_call | solution.py:449
  43.8 2.7 %own_backward.1 = (bf16[32,1024]{1,0:T(8,128)(2,1)S(1)}, f32[128,1024]{1,0:T(8,128)S(1)}) custom-call(bf16[5,160,1024]{2,1,0:T(8,128)(2,1)S(1)} %get-tuple-element.47.x_ref, bf16[4,128,1024]{2,1,0:T(8,128)(2,1)S(1)} %get-tuple-element.58.between_ref, bf16[2,8,384,256]{3,2,1,0:T(8,128)(2,1)S(1)} %get-tuple-element.40.refs_3_.refs_1_.refs_4_.weights, ...), custom_call_target="tpu_custom_call" | custom-call | flops 1484999936 | tf_op jit(solution)/shard_map/own_backward/pallas_call | solution.py:449
  46.5 1.3 %collective-permute-start.10 = (bf16[32,1024]{1,0:T(8,128)(2,1)S(1)}, bf16[32,1024]{1,0:T(8,128)(2,1)S(1)}, u32[]{:S(2)}, u32[]{:S(2)}) collective-permute-start(bf16[32,1024]{1,0:T(8,128)(2,1)S(1)} %get-tuple-element.60.refs_0_), channel_id=1, source_target_pairs={{1,0},{2,1},{3,2},{4,3},{5,4},{6,5},{7,6},{9,8},{10,9},{11,10},{12... | collective-permute-start | bytes 196616 | tf_op jit(solution)/shard_map/ppermute | solution.py:619
  47.8 0.0 collective-permute-done.11.refs_1_.got_mix1
  47.8 1.4 %short_partner.1._ = bf16[128,1280]{1,0:T(8,128)(2,1)S(1)} custom-call(bf16[5,160,1024]{2,1,0:T(8,128)(2,1)S(1)} %get-tuple-element.47.x_ref, bf16[4,128,1024]{2,1,0:T(8,128)(2,1)S(1)} %get-tuple-element.58.between_ref, bf16[2,8,384,256]{3,2,1,0:T(8,128)(2,1)S(1)} %get-tuple-element.40.refs_3_.refs_1_.refs_4_.weights, ...), custom_call_target="tpu_custom_call" | custom-call | flops 2200000000 | tf_op jit(solution)/shard_map/short_partner/pallas_call | solution.py:449
  49.3 2.1 %collective-permute-start.12 = (bf16[128,1280]{1,0:T(8,128)(2,1)S(1)}, bf16[128,1280]{1,0:T(8,128)(2,1)S(1)}, u32[]{:S(2)}, u32[]{:S(2)}) collective-permute-start(bf16[128,1280]{1,0:T(8,128)(2,1)S(1)} %short_partner.1._), channel_id=1, source_target_pairs={{0,1},{1,0},{2,3},{3,2},{4,5},{5,4},{6,7},{7,6},{8,9},{9,8},{10,11... | collective-permute-start | bytes 983048 | tf_op jit(solution)/shard_map/ppermute | solution.py:479
  51.4 0.7 %collective-permute-done.10.pushed_ref = bf16[32,1024]{1,0:T(8,128)(2,1)S(1)} collective-permute-done((bf16[32,1024]{1,0:T(8,128)(2,1)S(1)}, bf16[32,1024]{1,0:T(8,128)(2,1)S(1)}, u32[]{:S(2)}, u32[]{:S(2)}) %collective-permute-start.10) | collective-permute-done | bytes 65568 | tf_op jit(solution)/shard_map/ppermute | solution.py:619
  52.1 0.7 %add.1 = (bf16[128,1024]{1,0:T(8,128)(2,1)}, bf16[128,1024]{1,0:T(8,128)(2,1)S(1)}) custom-call(f32[128,1024]{1,0:T(8,128)S(1)} %get-tuple-element.59.own_ref, bf16[32,1024]{1,0:T(8,128)(2,1)S(1)} %collective-permute-done.10.pushed_ref, bf16[128,1280]{1,0:T(8,128)(2,1)S(1)} %short_partner.1._), custom_call_target="tpu_custom_call" | custom-call | flops 220000000 | tf_op jit(solution)/shard_map/add/pallas_call | solution.py:449
  52.8 7.6 %collective-permute-start.13 = (bf16[128,1024]{1,0:T(8,128)(2,1)S(1)}, bf16[128,1024]{1,0:T(8,128)(2,1)S(1)}, u32[]{:S(2)}, u32[]{:S(2)}) collective-permute-start(bf16[128,1024]{1,0:T(8,128)(2,1)S(1)} %get-tuple-element.65.refs_0_), channel_id=1, source_target_pairs={{8,0},{16,8},{24,16},{9,1},{17,9},{25,17},{10,2},{18,10},{26,18},{... | collective-permute-start | bytes 786440 | tf_op jit(solution)/shard_map/ppermute | solution.py:657
  60.4 1.4 %short_own.1.own0 = f32[128,1280]{1,0:T(8,128)S(1)} custom-call(bf16[5,160,1024]{2,1,0:T(8,128)(2,1)S(1)} %get-tuple-element.47.x_ref, bf16[4,128,1024]{2,1,0:T(8,128)(2,1)S(1)} %get-tuple-element.58.between_ref, bf16[2,8,384,256]{3,2,1,0:T(8,128)(2,1)S(1)} %get-tuple-element.40.refs_3_.refs_1_.refs_4_.weights, ...), custom_call_target="tpu_custom_call" | custom-call | flops 4400000000 | tf_op jit(solution)/shard_map/short_own/pallas_call | solution.py:449
  61.9 3.7 %collective-permute-done.13.other_cot = bf16[128,1024]{1,0:T(8,128)(2,1)S(1)} collective-permute-done((bf16[128,1024]{1,0:T(8,128)(2,1)S(1)}, bf16[128,1024]{1,0:T(8,128)(2,1)S(1)}, u32[]{:S(2)}, u32[]{:S(2)}) %collective-permute-start.13) | collective-permute-done | bytes 262176 | tf_op jit(solution)/shard_map/ppermute | solution.py:657
  65.6 0.0 collective-permute-done.12.got0
  65.6 1.4 %finish.1 = (f32[128,2,1024]{2,1,0:T(2,128)}, f32[2,3,128,32]{3,2,1,0:T(8,128)}, bf16[128,1024]{1,0:T(8,128)(2,1)}) custom-call(f32[128,1024]{1,0:T(8,128)S(1)} %get-tuple-element.64.mix1, f32[128,1280]{1,0:T(8,128)S(1)} %short_own.1.own0, bf16[128,1024]{1,0:T(8,128)(2,1)S(1)} %collective-permute-done.11.refs_1_.got_mix1, ...), custom_call_target="tpu_custom_call" | custom-call | flops 770000000 | tf_op jit(solution)/shard_map/finish/pallas_call | solution.py:449
  (3 shorter events, 0.1 us)
Async XLA Ops:
  0.6 9.5 %collective-permute-start.1 = (bf16[128,1024]{1,0:T(8,128)(2,1)}, bf16[128,1024]{1,0:T(8,128)(2,1)S(1)}, u32[]{:S(2)}, u32[]{:S(2)}) collective-permute-start(bf16[128,1024]{1,0:T(8,128)(2,1)} %bitcast.17), channel_id=1, source_target_pairs={{0,2},{1,3},{2,6},{3,7},{6,4},{7,5},{4,0},{5,1},{8,10},{9,11},{10,... | collective-permute-start | bytes 786440 | tf_op jit(solution)/shard_map/ppermute | solution.py:476
  2.8 13.7 %collective-permute-start.3 = (bf16[128,1024]{1,0:T(8,128)(2,1)}, bf16[128,1024]{1,0:T(8,128)(2,1)S(1)}, u32[]{:S(2)}, u32[]{:S(2)}) collective-permute-start(bf16[128,1024]{1,0:T(8,128)(2,1)} %bitcast.18), channel_id=1, source_target_pairs={{2,0},{3,1},{6,2},{7,3},{4,6},{5,7},{0,4},{1,5},{10,8},{11,9},{14,... | collective-permute-start | bytes 786440 | tf_op jit(solution)/shard_map/ppermute | solution.py:476
  10.2 13.1 %collective-permute-start.5 = (bf16[128,1024]{1,0:T(8,128)(2,1)S(1)}, bf16[128,1024]{1,0:T(8,128)(2,1)S(1)}, u32[]{:S(2)}, u32[]{:S(2)}) collective-permute-start(bf16[128,1024]{1,0:T(8,128)(2,1)S(1)} %get-tuple-element.39), channel_id=1, source_target_pairs={{0,2},{1,3},{2,6},{3,7},{6,4},{7,5},{4,0},{5,1},{8,10},{9,11},{10,... | collective-permute-start | bytes 786440 | tf_op jit(solution)/shard_map/ppermute | solution.py:476
  12.1 3.4 %collective-permute-start = (bf16[32,1024]{1,0:T(8,128)(2,1)S(1)}, bf16[32,1024]{1,0:T(8,128)(2,1)S(1)}, u32[]{:S(2)}, u32[]{:S(2)}) collective-permute-start(bf16[32,1024]{1,0:T(8,128)(2,1)S(1)} %slice_bitcast_fusion), channel_id=1, source_target_pairs={{0,1},{1,0},{2,3},{3,2},{4,5},{5,4},{6,7},{7,6},{8,9},{9,8},{10,11... | collective-permute-start | bytes 196616 | tf_op jit(solution)/shard_map/ppermute | solution.py:479
  17.2 13.1 %collective-permute-start.7 = (bf16[144,1024]{1,0:T(8,128)(2,1)S(1)}, bf16[144,1024]{1,0:T(8,128)(2,1)S(1)}, u32[]{:S(2)}, u32[]{:S(2)}) collective-permute-start(bf16[144,1024]{1,0:T(8,128)(2,1)S(1)} %get-tuple-element.49.refs_0_), channel_id=1, source_target_pairs={{0,2},{1,3},{2,6},{3,7},{6,4},{7,5},{4,0},{5,1},{8,10},{9,11},{10,... | collective-permute-start | bytes 884744 | tf_op jit(solution)/shard_map/ppermute | solution.py:476
  23.9 11.1 %collective-permute-start.9 = (bf16[144,1024]{1,0:T(8,128)(2,1)S(1)}, bf16[144,1024]{1,0:T(8,128)(2,1)S(1)}, u32[]{:S(2)}, u32[]{:S(2)}) collective-permute-start(bf16[144,1024]{1,0:T(8,128)(2,1)S(1)} %get-tuple-element.52), channel_id=1, source_target_pairs={{2,0},{3,1},{6,2},{7,3},{4,6},{5,7},{0,4},{1,5},{10,8},{11,9},{14,... | collective-permute-start | bytes 884744 | tf_op jit(solution)/shard_map/ppermute | solution.py:476
  24.0 7.8 %collective-permute-start.4 = (bf16[32,1024]{1,0:T(8,128)(2,1)S(1)}, bf16[32,1024]{1,0:T(8,128)(2,1)S(1)}, u32[]{:S(2)}, u32[]{:S(2)}) collective-permute-start(bf16[32,1024]{1,0:T(8,128)(2,1)S(1)} %relay.6), channel_id=1, source_target_pairs={{0,1},{1,0},{2,3},{3,2},{4,5},{5,4},{6,7},{7,6},{8,9},{9,8},{10,11... | collective-permute-start | bytes 196616 | tf_op jit(solution)/shard_map/ppermute | solution.py:479
  25.3 6.5 %collective-permute-start.2 = (bf16[32,1024]{1,0:T(8,128)(2,1)S(1)}, bf16[32,1024]{1,0:T(8,128)(2,1)S(1)}, u32[]{:S(2)}, u32[]{:S(2)}) collective-permute-start(bf16[32,1024]{1,0:T(8,128)(2,1)S(1)} %get-tuple-element.38), channel_id=1, source_target_pairs={{0,1},{1,0},{2,3},{3,2},{4,5},{5,4},{6,7},{7,6},{8,9},{9,8},{10,11... | collective-permute-start | bytes 196616 | tf_op jit(solution)/shard_map/ppermute | solution.py:479
  25.6 6.3 %collective-permute-start.6 = (bf16[32,1024]{1,0:T(8,128)(2,1)S(1)}, bf16[32,1024]{1,0:T(8,128)(2,1)S(1)}, u32[]{:S(2)}, u32[]{:S(2)}) collective-permute-start(bf16[32,1024]{1,0:T(8,128)(2,1)S(1)} %relay.7.refs_1_), channel_id=1, source_target_pairs={{0,1},{1,0},{2,3},{3,2},{4,5},{5,4},{6,7},{7,6},{8,9},{9,8},{10,11... | collective-permute-start | bytes 196616 | tf_op jit(solution)/shard_map/ppermute | solution.py:479
  30.4 9.5 %collective-permute-start.8 = (bf16[144,1024]{1,0:T(8,128)(2,1)S(1)}, bf16[144,1024]{1,0:T(8,128)(2,1)S(1)}, u32[]{:S(2)}, u32[]{:S(2)}) collective-permute-start(bf16[144,1024]{1,0:T(8,128)(2,1)S(1)} %collective-permute-done.7.refs_1_), channel_id=1, source_target_pairs={{0,2},{1,3},{2,6},{3,7},{6,4},{7,5},{4,0},{5,1},{8,10},{9,11},{10,... | collective-permute-start | bytes 884744 | tf_op jit(solution)/shard_map/ppermute | solution.py:476
  40.5 7.3 %collective-permute-start.11 = (bf16[128,1024]{1,0:T(8,128)(2,1)S(1)}, bf16[128,1024]{1,0:T(8,128)(2,1)S(1)}, u32[]{:S(2)}, u32[]{:S(2)}) collective-permute-start(bf16[128,1024]{1,0:T(8,128)(2,1)S(1)} %get-tuple-element.62), channel_id=1, source_target_pairs={{0,1},{1,0},{2,3},{3,2},{4,5},{5,4},{6,7},{7,6},{8,9},{9,8},{10,11... | collective-permute-start | bytes 786440 | tf_op jit(solution)/shard_map/ppermute | solution.py:479
  46.5 5.6 %collective-permute-start.10 = (bf16[32,1024]{1,0:T(8,128)(2,1)S(1)}, bf16[32,1024]{1,0:T(8,128)(2,1)S(1)}, u32[]{:S(2)}, u32[]{:S(2)}) collective-permute-start(bf16[32,1024]{1,0:T(8,128)(2,1)S(1)} %get-tuple-element.60.refs_0_), channel_id=1, source_target_pairs={{1,0},{2,1},{3,2},{4,3},{5,4},{6,5},{7,6},{9,8},{10,9},{11,10},{12... | collective-permute-start | bytes 196616 | tf_op jit(solution)/shard_map/ppermute | solution.py:619
  49.3 16.3 %collective-permute-start.12 = (bf16[128,1280]{1,0:T(8,128)(2,1)S(1)}, bf16[128,1280]{1,0:T(8,128)(2,1)S(1)}, u32[]{:S(2)}, u32[]{:S(2)}) collective-permute-start(bf16[128,1280]{1,0:T(8,128)(2,1)S(1)} %short_partner.1._), channel_id=1, source_target_pairs={{0,1},{1,0},{2,3},{3,2},{4,5},{5,4},{6,7},{7,6},{8,9},{9,8},{10,11... | collective-permute-start | bytes 983048 | tf_op jit(solution)/shard_map/ppermute | solution.py:479
  52.8 12.7 %collective-permute-start.13 = (bf16[128,1024]{1,0:T(8,128)(2,1)S(1)}, bf16[128,1024]{1,0:T(8,128)(2,1)S(1)}, u32[]{:S(2)}, u32[]{:S(2)}) collective-permute-start(bf16[128,1024]{1,0:T(8,128)(2,1)S(1)} %get-tuple-element.65.refs_0_), channel_id=1, source_target_pairs={{8,0},{16,8},{24,16},{9,1},{17,9},{25,17},{10,2},{18,10},{26,18},{... | collective-permute-start | bytes 786440 | tf_op jit(solution)/shard_map/ppermute | solution.py:657

commit v6 on v5

--- a/solution.py
+++ b/solution.py
@@ -285,7 +285,7 @@
         for z in places:
             tanh, sig = gates(pre_ref[z, :, lanes(first_slab + i, 2 * SLAB)])
             gated.append((tanh * sig).astype(BF16))
-        total_ref[cut(i), :] += tn(jnp.concatenate(gated, axis=0), g)
+        total_ref[cut(i), :channels] += tn(jnp.concatenate(gated, axis=0), g)
 
 
 def some(first, end, blocks, step):
@@ -299,6 +299,7 @@
     cots = refs[:early]
     pre_ref, hazard_ref, head, mixes, g_ref, d_ref, total_ref, code_ref, sems = refs[early:]
     copies = fetch_cotangents(cots, 0, blocks, g_ref, code_ref, sems)
+    d_ref[blocks:] = jnp.zeros((SPAN,) + d_ref.shape[1:], BF16)
     total_ref[...] = jnp.zeros(total_ref.shape, F32)
     finish_copies(copies)
 
@@ -310,19 +311,31 @@
     some(0, early, blocks, one)
 
 
-def mix_kernel(blocks, early, *refs):
+def mix_kernel(blocks, early, group_size, *refs):
     cots, refs = refs[: blocks - early], refs[blocks - early :]
     pre_ref, hazard_ref, head = refs[:3]
-    g_ref, mine_ref, own_ref, send_ref, total_ref, code_ref, sems = refs[-7:]
+    mine_ref, own_ref, send_ref, total_ref, code_ref, sems = refs[-6:]
+    g_ref = refs[-8] if early else refs[-7]
     copies = fetch_cotangents(cots, early, blocks, g_ref, code_ref, sems)
-    total_ref[...] = refs[3][...] if early else jnp.zeros(total_ref.shape, F32)
+    channels = g_ref.shape[2]
+    if early:
+        total_ref[:, :channels] = refs[3][...]
+        mid_ref, mixes, fold, d_ref = refs[6], refs[7], refs[8], refs[-7]
+    else:
+        total_ref[...] = jnp.zeros(total_ref.shape, F32)
     finish_copies(copies)
 
     def one(places):
         add_loss(places, code_ref, hazard_ref, head, g_ref)
+        if early:
+            gate_cotangent(places, g_ref, pre_ref, mixes, d_ref)
         mix_sums(places, g_ref, pre_ref, total_ref)
 
     some(early, blocks, blocks, one)
+    if early:
+        _, wide, first_slab = pair_slabs(channels, blocks)
+        last = slice(channels, channels + SLAB)
+        long_conv_sums(blocks, group_size, mid_ref, d_ref, fold, total_ref, last, first_slab, wide)
     mine_ref[...] = g_ref[lax.axis_index("seq") // SPAN]
     split_pair(g_ref.shape[2] // blocks, total_ref, own_ref, send_ref)
 
@@ -338,12 +351,15 @@
 
 
 def long_kernel(blocks, early, group_size, g_ref, mid_ref, pre_ref, weights, mixes, fold, *refs):
-    between_ref, last_ref = refs[-3:-1] if early else refs[:2]
-    d_ref = last_ref if early else refs[2]
+    if early:
+        d_ref, between_ref = refs
+    else:
+        between_ref, last_ref, d_ref = refs
     row_count, channels = g_ref.shape[1:]
     slabs = channels // SLAB
-    d_ref[blocks:] = jnp.zeros((SPAN,) + d_ref.shape[1:], BF16)
-    some(early, blocks, blocks, lambda places: gate_cotangent(places, g_ref, pre_ref, mixes, d_ref))
+    if not early:
+        d_ref[blocks:] = jnp.zeros((SPAN,) + d_ref.shape[1:], BF16)
+        some(0, blocks, blocks, lambda places: gate_cotangent(places, g_ref, pre_ref, mixes, d_ref))
 
     def back(first, count):
         rows = count * row_count
@@ -406,15 +422,13 @@
     split_pair(pair, total_ref, own_ref, send_ref)
 
 
-def half_kernel(blocks, group_size, partner, x_ref, between_ref, weights, mixes, fold, mid_ref, d_ref, *refs):
+def half_kernel(blocks, group_size, partner, x_ref, between_ref, weights, mixes, fold, *refs):
     out_ref, total_ref = refs[-2:]
     channels, share = between_ref.shape[2], out_ref.shape[0]
     place = lax.axis_index("seq")
     owner = place + (1 - 2 * (place % SPAN) if partner else 0)
     first_slab, wide = owner * share // SLAB, share // SLAB
     short_sums(blocks, group_size, first_slab, wide, x_ref, between_ref, weights, mixes, fold, total_ref)
-    last = slice(channels + SLAB, channels + 2 * SLAB)
-    long_conv_sums(blocks, group_size, mid_ref, d_ref, fold, total_ref, last, first_slab, wide)
     out_ref[...] = total_ref[...].astype(out_ref.dtype)
 
 
@@ -424,11 +438,12 @@
     width = 2 * group_size
     total = own0[...] + got0[...].astype(F32)
     mix_ref[:, 0, :] = total[:, :channels]
-    mix_ref[:, 1, :] = mix1[...] + got_mix1[...].astype(F32)
+    total1 = mix1[...] + got_mix1[...].astype(F32)
+    mix_ref[:, 1, :] = total1[:, :channels]
+    convs = (total[:, channels:], total1[:, channels:] if total1.shape[1] > channels else total[:, channels + SLAB :])
     for layer in range(2):
         for k in range(3):
-            begin = channels + SLAB * layer + width * k
-            conv_ref[layer, k] = total[:, begin : begin + width]
+            conv_ref[layer, k] = convs[layer][:, width * k : width * (k + 1)]
 
 
 def add_kernel(own_ref, pushed_ref, _, *out_refs):
@@ -589,25 +604,27 @@
             us=4,
         )
     late = cots[early:]
-    g, mine, mix1, send_mix1 = run(
-        functools.partial(mix_kernel, blocks, early),
-        [block_rows, ((row_count, channels), BF16), ((share, channels), F32), ((share, channels), BF16)],
-        [*late, pre, hazard, head] + ([total, g] if early else []),
-        [((wide, channels), F32), codes, pltpu.SemaphoreType.DMA((2 * len(late),))],
+    sums1 = channels + SLAB * bool(early)
+    g, *d_out, mine, mix1, send_mix1 = run(
+        functools.partial(mix_kernel, blocks, early, group_size),
+        [block_rows]
+        + [d_rows] * bool(early)
+        + [((row_count, channels), BF16), ((share, sums1), F32), ((share, sums1), BF16)],
+        [*late, pre, hazard, head] + ([total, g, d, mid, mixes, fold] if early else []),
+        [((wide, sums1), F32), codes, pltpu.SemaphoreType.DMA((2 * len(late),))],
         name="long_mix",
-        aliases={len(late) + 4: 0} if early else {},
+        aliases={len(late) + 4: 0, len(late) + 5: 1} if early else {},
         far=range(len(late)),
-        us=0.7,
+        us=1.7,
     )
     got_mix1 = swap(send_mix1)
-    between, last = run(
+    between, *last = run(
         functools.partial(long_kernel, blocks, early, group_size),
-        [block_rows, d_rows if early else ((wide, SLAB), F32)],
-        [g, mid, pre, weights, mixes, fold] + ([d] if early else []),
-        [((8, SLAB), F32) if early else d_rows],
+        [block_rows] + ([] if early else [((wide, SLAB), F32)]),
+        [g, mid, pre, weights, mixes, fold, *d_out],
+        [] if early else [d_rows],
         name="long_backward",
-        aliases={6: 1} if early else {},
-        us=3.4,
+        us=2,
     )
     push, own_sum = run(
         own_kernel,
@@ -617,24 +634,24 @@
         us=2.7,
     )
     pushed = lax.ppermute(push, "seq", [(b, b - 1) for b in range(1, seq)])
-    sums = channels + 2 * SLAB
+    sums = channels + SLAB * (1 if early else 2)
     if early:
         half = functools.partial(half_kernel, blocks, group_size)
-        held = [x, between, weights, mixes, fold, mid, last]
+        held = [x, between, weights, mixes, fold]
         (send0,) = run(
             functools.partial(half, True),
             [((share, sums), BF16)],
             [*held, push, got_mix1],
             [((share, sums), F32)],
             name="short_partner",
-            far=(7, 8),
+            far=(5, 6),
             us=4,
         )
     else:
         own0, send0 = run(
             functools.partial(short_kernel, blocks, group_size),
             [((share, sums), F32), ((share, sums), BF16)],
-            [x, between, weights, mixes, fold, last],
+            [x, between, weights, mixes, fold, *last],
             [((wide, sums), F32)],
             name="short_backward",
         )
@@ -650,7 +667,7 @@
             [*held, sent_gradient],
             [((share, sums), F32)],
             name="short_own",
-            far=(7,),
+            far=(5,),
             us=8,
         )
     count = lax.axis_size("section")

time: 67.3 us -> 67.8 us (level)
  waiting for transfers between devices: 14.8 us -> 15.6 us
    ppermute x1, waiting for transfers between devices: 0.67 us -> 1.36 us  [body(): pushed = lax.ppermute(push, 'seq', [(b, b - 1) for b in range(1, seq)])]
  transfers between devices with their start and end apart: 14 -> 14, of which waited for: 7 -> 7; matrix products, arithmetic and copies ran while one was open for 1% -> 1% of each run, Pallas kernels for 36% -> 34%
where the time goes in v6:
time: 67.8 us; the launch traced here: 67.6 us
  Pallas kernels  26.5 us (39%)
  starting transfers between devices  23.8 us (35%)
  waiting for transfers between devices  15.6 us (23%)
  local copies, waits for them, and re-layouts  0.84 us (1%)
  between operations  0.81 us (1%)
    pallas_call x17, Pallas kernels, call(): pl.pallas_call(kernel, out_shape=[of(shape, kind) for of, (shape, kind) i...  26.5 us
    ppermute x6, starting transfers between devices, step(): lax.ppermute(value, 'seq', [(a * SPAN + y, b * SPAN + y) for a, b in pair...  8.51 us
    ppermute x6, waiting for transfers between devices, step(): lax.ppermute(value, 'seq', [(a * SPAN + y, b * SPAN + y) for a, b in pair...  8.17 us
    ppermute x1, starting transfers between devices, body(): lax.ppermute(sent_gradient, 'section', [(s, s - 1) for s in range(1, coun...  7.22 us
    ppermute x6, starting transfers between devices, swap(): lax.ppermute(value, 'seq', [(b, b + 1 - 2 * (b % 2)) for b in range(seq)])  6.76 us
    ppermute x1, waiting for transfers between devices, body(): lax.ppermute(sent_gradient, 'section', [(s, s - 1) for s in range(1, coun...  3.92 us
    ppermute x6, waiting for transfers between devices, swap(): lax.ppermute(value, 'seq', [(b, b + 1 - 2 * (b % 2)) for b in range(seq)])  2.18 us
    ppermute x1, waiting for transfers between devices, body(): pushed = lax.ppermute(push, 'seq', [(b, b - 1) for b in range(1, seq)])  1.36 us
  transfers between devices with their start and end apart: 14, of which 7 were waited for; matrix products, arithmetic and copies ran while one was open for 1% of the time, Pallas kernels for 34%

profile of v6, /device:TPU:1, one launch (start us, length us, event | category | flops | bytes accessed | tf_op | source)
XLA Modules:
  0.0 67.6 jit_solution(14150725240466084456)
XLA Ops:
  0.6 2.2 %collective-permute-start.1 = (bf16[128,1024]{1,0:T(8,128)(2,1)}, bf16[128,1024]{1,0:T(8,128)(2,1)S(1)}, u32[]{:S(2)}, u32[]{:S(2)}) collective-permute-start(bf16[128,1024]{1,0:T(8,128)(2,1)} %bitcast.17), channel_id=1, source_target_pairs={{0,2},{1,3},{2,6},{3,7},{6,4},{7,5},{4,0},{5,1},{8,10},{9,11},{10,... | collective-permute-start | bytes 786440 | tf_op jit(solution)/shard_map/ppermute | solution.py:491
  2.8 1.1 %collective-permute-start.3 = (bf16[128,1024]{1,0:T(8,128)(2,1)}, bf16[128,1024]{1,0:T(8,128)(2,1)S(1)}, u32[]{:S(2)}, u32[]{:S(2)}) collective-permute-start(bf16[128,1024]{1,0:T(8,128)(2,1)} %bitcast.18), channel_id=1, source_target_pairs={{2,0},{3,1},{6,2},{7,3},{4,6},{5,7},{0,4},{1,5},{10,8},{11,9},{14,... | collective-permute-start | bytes 786440 | tf_op jit(solution)/shard_map/ppermute | solution.py:491
  3.9 4.8 %weights.1 = (bf16[2,8,384,256]{3,2,1,0:T(8,128)(2,1)S(1)}, bf16[128,768]{1,0:T(8,128)(2,1)S(1)}, bf16[2,1024,1024]{2,1,0:T(8,128)(2,1)S(1)}, bf16[64,1024]{1,0:T(8,128)(2,1)S(1)}, bf16[144,1024]{1,0:T(8,128)(2,1)S(1)}) custom-call(bf16[2,3,512,64]{3,2,1,0:T(8,128)(2,1)} %bitcast.21, bf16[2,1024,1024]{2,1,0:T(8,128)(2,1)} %bitcast.20, ...), custom_call_target="tpu_custom_call" | custom-call | flops 1924999936 | tf_op jit(solution)/shard_map/weights/pallas_call | solution.py:464
  8.7 1.5 %collective-permute-done.1.refs_0_.refs_1_ = bf16[128,1024]{1,0:T(8,128)(2,1)S(1)} collective-permute-done((bf16[128,1024]{1,0:T(8,128)(2,1)}, bf16[128,1024]{1,0:T(8,128)(2,1)S(1)}, u32[]{:S(2)}, u32[]{:S(2)}) %collective-permute-start.1) | collective-permute-done | bytes 262176 | tf_op jit(solution)/shard_map/ppermute | solution.py:491
  10.2 1.2 %collective-permute-start.5 = (bf16[128,1024]{1,0:T(8,128)(2,1)S(1)}, bf16[128,1024]{1,0:T(8,128)(2,1)S(1)}, u32[]{:S(2)}, u32[]{:S(2)}) collective-permute-start(bf16[128,1024]{1,0:T(8,128)(2,1)S(1)} %get-tuple-element.38), channel_id=1, source_target_pairs={{0,2},{1,3},{2,6},{3,7},{6,4},{7,5},{4,0},{5,1},{8,10},{9,11},{10,... | collective-permute-start | bytes 786440 | tf_op jit(solution)/shard_map/ppermute | solution.py:491
  11.3 0.8 %slice_bitcast_fusion = bf16[32,1024]{1,0:T(8,128)(2,1)S(1)} fusion(bf16[1,128,1024]{2,1,0:T(8,128)(2,1)} %param.7), kind=kLoop, calls=%fused_computation | loop fusion | bytes 131072 | tf_op jit(solution)/shard_map/slice | solution.py:514
  12.1 1.2 %collective-permute-start = (bf16[32,1024]{1,0:T(8,128)(2,1)S(1)}, bf16[32,1024]{1,0:T(8,128)(2,1)S(1)}, u32[]{:S(2)}, u32[]{:S(2)}) collective-permute-start(bf16[32,1024]{1,0:T(8,128)(2,1)S(1)} %slice_bitcast_fusion), channel_id=1, source_target_pairs={{0,1},{1,0},{2,3},{3,2},{4,5},{5,4},{6,7},{7,6},{8,9},{9,8},{10,11... | collective-permute-start | bytes 196616 | tf_op jit(solution)/shard_map/ppermute | solution.py:494
  13.4 2.2 %collective-permute-done.refs_0_.refs_2_ = bf16[32,1024]{1,0:T(8,128)(2,1)S(1)} collective-permute-done((bf16[32,1024]{1,0:T(8,128)(2,1)S(1)}, bf16[32,1024]{1,0:T(8,128)(2,1)S(1)}, u32[]{:S(2)}, u32[]{:S(2)}) %collective-permute-start) | collective-permute-done | bytes 65568 | tf_op jit(solution)/shard_map/ppermute | solution.py:494
  15.6 1.0 %collective-permute-done.3.refs_0_.refs_2_.refs_1_ = bf16[128,1024]{1,0:T(8,128)(2,1)S(1)} collective-permute-done((bf16[128,1024]{1,0:T(8,128)(2,1)}, bf16[128,1024]{1,0:T(8,128)(2,1)S(1)}, u32[]{:S(2)}, u32[]{:S(2)}) %collective-permute-start.3) | collective-permute-done | bytes 262176 | tf_op jit(solution)/shard_map/ppermute | solution.py:491
  16.5 0.7 %relay.8 = (bf16[144,1024]{1,0:T(8,128)(2,1)S(1)}, bf16[32,1024]{1,0:T(8,128)(2,1)}) custom-call(bf16[144,1024]{1,0:T(8,128)(2,1)S(1)} %get-tuple-element.47.refs_0_, bf16[128,1024]{1,0:T(8,128)(2,1)S(1)} %collective-permute-done.3.refs_0_.refs_2_.refs_1_, bf16[32,1024]{1,0:T(8,128)(2,1)S(1)} %collective-permute-done.refs_0_.refs_2_), custom_call_target="tpu_custom_call" | custom-call | flops 165000000 | tf_op jit(solution)/shard_map/relay/pallas_call | solution.py:464
  17.2 2.5 %collective-permute-start.7 = (bf16[144,1024]{1,0:T(8,128)(2,1)S(1)}, bf16[144,1024]{1,0:T(8,128)(2,1)S(1)}, u32[]{:S(2)}, u32[]{:S(2)}) collective-permute-start(bf16[144,1024]{1,0:T(8,128)(2,1)S(1)} %get-tuple-element.48.refs_0_), channel_id=1, source_target_pairs={{0,2},{1,3},{2,6},{3,7},{6,4},{7,5},{4,0},{5,1},{8,10},{9,11},{10,... | collective-permute-start | bytes 884744 | tf_op jit(solution)/shard_map/ppermute | solution.py:491
  19.8 3.5 %collective-permute-done.5.refs_0_ = bf16[128,1024]{1,0:T(8,128)(2,1)S(1)} collective-permute-done((bf16[128,1024]{1,0:T(8,128)(2,1)S(1)}, bf16[128,1024]{1,0:T(8,128)(2,1)S(1)}, u32[]{:S(2)}, u32[]{:S(2)}) %collective-permute-start.5) | collective-permute-done | bytes 262176 | tf_op jit(solution)/shard_map/ppermute | solution.py:491
  23.2 0.7 %relay.9 = (bf16[144,1024]{1,0:T(8,128)(2,1)S(1)}, bf16[32,1024]{1,0:T(8,128)(2,1)}) custom-call(bf16[144,1024]{1,0:T(8,128)(2,1)S(1)} %get-tuple-element.48.refs_0_, bf16[32,1024]{1,0:T(8,128)(2,1)S(1)} %relay.7.refs_1_), custom_call_target="tpu_custom_call" | custom-call | flops 165000000 | tf_op jit(solution)/shard_map/relay/pallas_call | solution.py:464
  23.9 0.1 collective-permute-start.9
  24.0 1.3 %collective-permute-start.4 = (bf16[32,1024]{1,0:T(8,128)(2,1)S(1)}, bf16[32,1024]{1,0:T(8,128)(2,1)S(1)}, u32[]{:S(2)}, u32[]{:S(2)}) collective-permute-start(bf16[32,1024]{1,0:T(8,128)(2,1)S(1)} %relay.6), channel_id=1, source_target_pairs={{0,1},{1,0},{2,3},{3,2},{4,5},{5,4},{6,7},{7,6},{8,9},{9,8},{10,11... | collective-permute-start | bytes 196616 | tf_op jit(solution)/shard_map/ppermute | solution.py:494
  25.3 0.2 collective-permute-start.2
  25.6 1.2 %collective-permute-start.6 = (bf16[32,1024]{1,0:T(8,128)(2,1)S(1)}, bf16[32,1024]{1,0:T(8,128)(2,1)S(1)}, u32[]{:S(2)}, u32[]{:S(2)}) collective-permute-start(bf16[32,1024]{1,0:T(8,128)(2,1)S(1)} %relay.7.refs_1_), channel_id=1, source_target_pairs={{0,1},{1,0},{2,3},{3,2},{4,5},{5,4},{6,7},{7,6},{8,9},{9,8},{10,11... | collective-permute-start | bytes 196616 | tf_op jit(solution)/shard_map/ppermute | solution.py:494
  26.8 2.7 %begin.2 = (bf16[5,160,1024]{2,1,0:T(8,128)(2,1)S(1)}, bf16[6,128,1024]{2,1,0:T(8,128)(2,1)S(1)}) custom-call(bf16[128,1024]{1,0:T(8,128)(2,1)} %bitcast.19, bf16[128,1024]{1,0:T(8,128)(2,1)S(1)} %collective-permute-done.1.refs_0_.refs_1_, bf16[128,1024]{1,0:T(8,128)(2,1)S(1)} %collective-permute-done.3.refs_0_.refs_2_.refs_1_, ...), custom_call_target="tpu_custom_call" | custom-call | flops 990000000 | tf_op jit(solution)/shard_map/begin/pallas_call | solution.py:464
  29.5 0.9 %begin.3 = (bf16[5,160,1024]{2,1,0:T(8,128)(2,1)S(1)}, bf16[6,128,1024]{2,1,0:T(8,128)(2,1)S(1)}) custom-call(bf16[128,1024]{1,0:T(8,128)(2,1)S(1)} %collective-permute-done.5.refs_0_, bf16[2,8,384,256]{3,2,1,0:T(8,128)(2,1)S(1)} %get-tuple-element.39.refs_3_.refs_1_.refs_4_.weights, ...), custom_call_target="tpu_custom_call", output_to_operand_aliasing={{0}: (3, {}), {1}: (4, {})} | custom-call | flops 330000000 | tf_op jit(solution)/shard_map/begin/pallas_call | solution.py:464
  30.4 0.0 collective-permute-done.7.refs_1_
  30.4 1.5 %collective-permute-start.8 = (bf16[144,1024]{1,0:T(8,128)(2,1)S(1)}, bf16[144,1024]{1,0:T(8,128)(2,1)S(1)}, u32[]{:S(2)}, u32[]{:S(2)}) collective-permute-start(bf16[144,1024]{1,0:T(8,128)(2,1)S(1)} %collective-permute-done.7.refs_1_), channel_id=1, source_target_pairs={{0,2},{1,3},{2,6},{3,7},{6,4},{7,5},{4,0},{5,1},{8,10},{9,11},{10,... | collective-permute-start | bytes 884744 | tf_op jit(solution)/shard_map/ppermute | solution.py:491
  31.9 0.0 collective-permute-done.4.refs_2_
  31.9 0.0 collective-permute-done.2.refs_1_
  31.9 0.0 collective-permute-done.6.refs_3_
  31.9 3.1 %forward.1 = (bf16[5,160,1024]{2,1,0:T(8,128)(2,1)S(1)}, bf16[6,128,1024]{2,1,0:T(8,128)(2,1)S(1)}, bf16[4,128,2048]{2,1,0:T(8,128)(2,1)S(1)}, f32[4,64,128]{2,1,0:T(8,128)S(1)}) custom-call(bf16[32,1024]{1,0:T(8,128)(2,1)S(1)} %collective-permute-done.refs_0_.refs_2_, ...), custom_call_target="tpu_custom_call", output_to_operand_aliasing={{0}: (7, {}), {1}: (8, {})} | custom-call | flops 1650000000 | tf_op jit(solution)/shard_map/forward/pallas_call | solution.py:464
  35.0 0.0 collective-permute-done.9.refs_2_
  35.1 2.5 %early.1 = (bf16[4,128,1024]{2,1,0:T(8,128)(2,1)S(1)}, bf16[6,128,2048]{2,1,0:T(8,128)(2,1)S(1)}, f32[256,1024]{1,0:T(8,128)S(1)}) custom-call(bf16[144,1024]{1,0:T(8,128)(2,1)S(1)} %get-tuple-element.47.refs_0_, bf16[144,1024]{1,0:T(8,128)(2,1)S(1)} %collective-permute-done.7.refs_1_, bf16[144,1024]{1,0:T(8,128)(2,1)S(1)} %collective-permute-done.9.refs_2_, ...), custom_call_target="tpu_custom_call" | custom-call | flops 2200000000 | tf_op jit(solution)/shard_map/early/pallas_call | solution.py:464
  37.6 2.3 %collective-permute-done.8.refs_0_ = bf16[144,1024]{1,0:T(8,128)(2,1)S(1)} collective-permute-done((bf16[144,1024]{1,0:T(8,128)(2,1)S(1)}, bf16[144,1024]{1,0:T(8,128)(2,1)S(1)}, u32[]{:S(2)}, u32[]{:S(2)}) %collective-permute-start.8) | collective-permute-done | bytes 294944 | tf_op jit(solution)/shard_map/ppermute | solution.py:491
  39.9 2.0 %long_mix.1 = (bf16[4,128,1024]{2,1,0:T(8,128)(2,1)S(1)}, bf16[6,128,2048]{2,1,0:T(8,128)(2,1)S(1)}, bf16[128,1024]{1,0:T(8,128)(2,1)S(1)}, f32[128,1152]{1,0:T(8,128)S(1)}, bf16[128,1152]{1,0:T(8,128)(2,1)S(1)}) custom-call(bf16[144,1024]{1,0:T(8,128)(2,1)S(1)} %collective-permute-done.8.refs_0_, ...), custom_call_target="tpu_custom_call", output_to_operand_aliasing={{0}: (5, {}), {1}: (6, {})} | custom-call | flops 935000000 | tf_op jit(solution)/shard_map/long_mix/pallas_call | solution.py:464
  41.9 0.6 collective-permute-start.11
  42.5 1.8 %long_backward.1.between_ref = bf16[4,128,1024]{2,1,0:T(8,128)(2,1)S(1)} custom-call(bf16[4,128,1024]{2,1,0:T(8,128)(2,1)S(1)} %get-tuple-element.56.g_ref, bf16[6,128,1024]{2,1,0:T(8,128)(2,1)S(1)} %get-tuple-element.55.refs_7_.mid_ref, bf16[4,128,2048]{2,1,0:T(8,128)(2,1)S(1)} %get-tuple-element.49.refs_3_.refs_1_.pre_ref, ...), custom_call_target="tpu_custom_call" | custom-call | flops 1100000000 | tf_op jit(solution)/shard_map/long_backward/pallas_call | solution.py:464
  44.3 2.7 %own_backward.1 = (bf16[32,1024]{1,0:T(8,128)(2,1)S(1)}, f32[128,1024]{1,0:T(8,128)S(1)}) custom-call(bf16[5,160,1024]{2,1,0:T(8,128)(2,1)S(1)} %get-tuple-element.46.x_ref, bf16[4,128,1024]{2,1,0:T(8,128)(2,1)S(1)} %long_backward.1.between_ref, bf16[2,8,384,256]{3,2,1,0:T(8,128)(2,1)S(1)} %get-tuple-element.39.refs_3_.refs_1_.refs_4_.weights, ...), custom_call_target="tpu_custom_call" | custom-call | flops 1484999936 | tf_op jit(solution)/shard_map/own_backward/pallas_call | solution.py:464
  47.0 1.3 %collective-permute-start.10 = (bf16[32,1024]{1,0:T(8,128)(2,1)S(1)}, bf16[32,1024]{1,0:T(8,128)(2,1)S(1)}, u32[]{:S(2)}, u32[]{:S(2)}) collective-permute-start(bf16[32,1024]{1,0:T(8,128)(2,1)S(1)} %get-tuple-element.59.refs_0_), channel_id=1, source_target_pairs={{1,0},{2,1},{3,2},{4,3},{5,4},{6,5},{7,6},{9,8},{10,9},{11,10},{12... | collective-permute-start | bytes 196616 | tf_op jit(solution)/shard_map/ppermute | solution.py:636
  48.3 0.0 collective-permute-done.11.refs_1_.got_mix1
  48.3 1.2 %short_partner.1._ = bf16[128,1152]{1,0:T(8,128)(2,1)S(1)} custom-call(bf16[5,160,1024]{2,1,0:T(8,128)(2,1)S(1)} %get-tuple-element.46.x_ref, bf16[4,128,1024]{2,1,0:T(8,128)(2,1)S(1)} %long_backward.1.between_ref, bf16[2,8,384,256]{3,2,1,0:T(8,128)(2,1)S(1)} %get-tuple-element.39.refs_3_.refs_1_.refs_4_.weights, ...), custom_call_target="tpu_custom_call" | custom-call | flops 2200000000 | tf_op jit(solution)/shard_map/short_partner/pallas_call | solution.py:464
  49.6 2.1 %collective-permute-start.12 = (bf16[128,1152]{1,0:T(8,128)(2,1)S(1)}, bf16[128,1152]{1,0:T(8,128)(2,1)S(1)}, u32[]{:S(2)}, u32[]{:S(2)}) collective-permute-start(bf16[128,1152]{1,0:T(8,128)(2,1)S(1)} %short_partner.1._), channel_id=1, source_target_pairs={{0,1},{1,0},{2,3},{3,2},{4,5},{5,4},{6,7},{7,6},{8,9},{9,8},{10,11... | collective-permute-start | bytes 884744 | tf_op jit(solution)/shard_map/ppermute | solution.py:494
  51.7 1.4 %collective-permute-done.10.pushed_ref = bf16[32,1024]{1,0:T(8,128)(2,1)S(1)} collective-permute-done((bf16[32,1024]{1,0:T(8,128)(2,1)S(1)}, bf16[32,1024]{1,0:T(8,128)(2,1)S(1)}, u32[]{:S(2)}, u32[]{:S(2)}) %collective-permute-start.10) | collective-permute-done | bytes 65568 | tf_op jit(solution)/shard_map/ppermute | solution.py:636
  53.1 0.7 %add.1 = (bf16[128,1024]{1,0:T(8,128)(2,1)}, bf16[128,1024]{1,0:T(8,128)(2,1)S(1)}) custom-call(f32[128,1024]{1,0:T(8,128)S(1)} %get-tuple-element.58.own_ref, bf16[32,1024]{1,0:T(8,128)(2,1)S(1)} %collective-permute-done.10.pushed_ref, bf16[128,1152]{1,0:T(8,128)(2,1)S(1)} %short_partner.1._), custom_call_target="tpu_custom_call" | custom-call | flops 220000000 | tf_op jit(solution)/shard_map/add/pallas_call | solution.py:464
  53.8 7.2 %collective-permute-start.13 = (bf16[128,1024]{1,0:T(8,128)(2,1)S(1)}, bf16[128,1024]{1,0:T(8,128)(2,1)S(1)}, u32[]{:S(2)}, u32[]{:S(2)}) collective-permute-start(bf16[128,1024]{1,0:T(8,128)(2,1)S(1)} %get-tuple-element.63.refs_0_), channel_id=1, source_target_pairs={{8,0},{16,8},{24,16},{9,1},{17,9},{25,17},{10,2},{18,10},{26,18},{... | collective-permute-start | bytes 786440 | tf_op jit(solution)/shard_map/ppermute | solution.py:674
  61.0 1.2 %short_own.1.own0 = f32[128,1152]{1,0:T(8,128)S(1)} custom-call(bf16[5,160,1024]{2,1,0:T(8,128)(2,1)S(1)} %get-tuple-element.46.x_ref, bf16[4,128,1024]{2,1,0:T(8,128)(2,1)S(1)} %long_backward.1.between_ref, bf16[2,8,384,256]{3,2,1,0:T(8,128)(2,1)S(1)} %get-tuple-element.39.refs_3_.refs_1_.refs_4_.weights, ...), custom_call_target="tpu_custom_call" | custom-call | flops 4400000000 | tf_op jit(solution)/shard_map/short_own/pallas_call | solution.py:464
  62.3 3.9 %collective-permute-done.13.other_cot = bf16[128,1024]{1,0:T(8,128)(2,1)S(1)} collective-permute-done((bf16[128,1024]{1,0:T(8,128)(2,1)S(1)}, bf16[128,1024]{1,0:T(8,128)(2,1)S(1)}, u32[]{:S(2)}, u32[]{:S(2)}) %collective-permute-start.13) | collective-permute-done | bytes 262176 | tf_op jit(solution)/shard_map/ppermute | solution.py:674
  66.2 0.0 collective-permute-done.12.got0
  66.2 1.4 %finish.1 = (f32[128,2,1024]{2,1,0:T(2,128)}, f32[2,3,128,32]{3,2,1,0:T(8,128)}, bf16[128,1024]{1,0:T(8,128)(2,1)}) custom-call(f32[128,1152]{1,0:T(8,128)S(1)} %get-tuple-element.62.mix1, f32[128,1152]{1,0:T(8,128)S(1)} %short_own.1.own0, bf16[128,1152]{1,0:T(8,128)(2,1)S(1)} %collective-permute-done.11.refs_1_.got_mix1, ...), custom_call_target="tpu_custom_call" | custom-call | flops 770000000 | tf_op jit(solution)/shard_map/finish/pallas_call | solution.py:464
  (3 shorter events, 0.1 us)
Async XLA Ops:
  0.6 9.5 %collective-permute-start.1 = (bf16[128,1024]{1,0:T(8,128)(2,1)}, bf16[128,1024]{1,0:T(8,128)(2,1)S(1)}, u32[]{:S(2)}, u32[]{:S(2)}) collective-permute-start(bf16[128,1024]{1,0:T(8,128)(2,1)} %bitcast.17), channel_id=1, source_target_pairs={{0,2},{1,3},{2,6},{3,7},{6,4},{7,5},{4,0},{5,1},{8,10},{9,11},{10,... | collective-permute-start | bytes 786440 | tf_op jit(solution)/shard_map/ppermute | solution.py:491
  2.8 13.7 %collective-permute-start.3 = (bf16[128,1024]{1,0:T(8,128)(2,1)}, bf16[128,1024]{1,0:T(8,128)(2,1)S(1)}, u32[]{:S(2)}, u32[]{:S(2)}) collective-permute-start(bf16[128,1024]{1,0:T(8,128)(2,1)} %bitcast.18), channel_id=1, source_target_pairs={{2,0},{3,1},{6,2},{7,3},{4,6},{5,7},{0,4},{1,5},{10,8},{11,9},{14,... | collective-permute-start | bytes 786440 | tf_op jit(solution)/shard_map/ppermute | solution.py:491
  10.2 13.1 %collective-permute-start.5 = (bf16[128,1024]{1,0:T(8,128)(2,1)S(1)}, bf16[128,1024]{1,0:T(8,128)(2,1)S(1)}, u32[]{:S(2)}, u32[]{:S(2)}) collective-permute-start(bf16[128,1024]{1,0:T(8,128)(2,1)S(1)} %get-tuple-element.38), channel_id=1, source_target_pairs={{0,2},{1,3},{2,6},{3,7},{6,4},{7,5},{4,0},{5,1},{8,10},{9,11},{10,... | collective-permute-start | bytes 786440 | tf_op jit(solution)/shard_map/ppermute | solution.py:491
  12.1 3.4 %collective-permute-start = (bf16[32,1024]{1,0:T(8,128)(2,1)S(1)}, bf16[32,1024]{1,0:T(8,128)(2,1)S(1)}, u32[]{:S(2)}, u32[]{:S(2)}) collective-permute-start(bf16[32,1024]{1,0:T(8,128)(2,1)S(1)} %slice_bitcast_fusion), channel_id=1, source_target_pairs={{0,1},{1,0},{2,3},{3,2},{4,5},{5,4},{6,7},{7,6},{8,9},{9,8},{10,11... | collective-permute-start | bytes 196616 | tf_op jit(solution)/shard_map/ppermute | solution.py:494
  17.2 13.1 %collective-permute-start.7 = (bf16[144,1024]{1,0:T(8,128)(2,1)S(1)}, bf16[144,1024]{1,0:T(8,128)(2,1)S(1)}, u32[]{:S(2)}, u32[]{:S(2)}) collective-permute-start(bf16[144,1024]{1,0:T(8,128)(2,1)S(1)} %get-tuple-element.48.refs_0_), channel_id=1, source_target_pairs={{0,2},{1,3},{2,6},{3,7},{6,4},{7,5},{4,0},{5,1},{8,10},{9,11},{10,... | collective-permute-start | bytes 884744 | tf_op jit(solution)/shard_map/ppermute | solution.py:491
  23.9 11.1 %collective-permute-start.9 = (bf16[144,1024]{1,0:T(8,128)(2,1)S(1)}, bf16[144,1024]{1,0:T(8,128)(2,1)S(1)}, u32[]{:S(2)}, u32[]{:S(2)}) collective-permute-start(bf16[144,1024]{1,0:T(8,128)(2,1)S(1)} %get-tuple-element.51), channel_id=1, source_target_pairs={{2,0},{3,1},{6,2},{7,3},{4,6},{5,7},{0,4},{1,5},{10,8},{11,9},{14,... | collective-permute-start | bytes 884744 | tf_op jit(solution)/shard_map/ppermute | solution.py:491
  24.0 7.8 %collective-permute-start.4 = (bf16[32,1024]{1,0:T(8,128)(2,1)S(1)}, bf16[32,1024]{1,0:T(8,128)(2,1)S(1)}, u32[]{:S(2)}, u32[]{:S(2)}) collective-permute-start(bf16[32,1024]{1,0:T(8,128)(2,1)S(1)} %relay.6), channel_id=1, source_target_pairs={{0,1},{1,0},{2,3},{3,2},{4,5},{5,4},{6,7},{7,6},{8,9},{9,8},{10,11... | collective-permute-start | bytes 196616 | tf_op jit(solution)/shard_map/ppermute | solution.py:494
  25.3 6.5 %collective-permute-start.2 = (bf16[32,1024]{1,0:T(8,128)(2,1)S(1)}, bf16[32,1024]{1,0:T(8,128)(2,1)S(1)}, u32[]{:S(2)}, u32[]{:S(2)}) collective-permute-start(bf16[32,1024]{1,0:T(8,128)(2,1)S(1)} %get-tuple-element.37), channel_id=1, source_target_pairs={{0,1},{1,0},{2,3},{3,2},{4,5},{5,4},{6,7},{7,6},{8,9},{9,8},{10,11... | collective-permute-start | bytes 196616 | tf_op jit(solution)/shard_map/ppermute | solution.py:494
  25.6 6.3 %collective-permute-start.6 = (bf16[32,1024]{1,0:T(8,128)(2,1)S(1)}, bf16[32,1024]{1,0:T(8,128)(2,1)S(1)}, u32[]{:S(2)}, u32[]{:S(2)}) collective-permute-start(bf16[32,1024]{1,0:T(8,128)(2,1)S(1)} %relay.7.refs_1_), channel_id=1, source_target_pairs={{0,1},{1,0},{2,3},{3,2},{4,5},{5,4},{6,7},{7,6},{8,9},{9,8},{10,11... | collective-permute-start | bytes 196616 | tf_op jit(solution)/shard_map/ppermute | solution.py:494
  30.4 9.5 %collective-permute-start.8 = (bf16[144,1024]{1,0:T(8,128)(2,1)S(1)}, bf16[144,1024]{1,0:T(8,128)(2,1)S(1)}, u32[]{:S(2)}, u32[]{:S(2)}) collective-permute-start(bf16[144,1024]{1,0:T(8,128)(2,1)S(1)} %collective-permute-done.7.refs_1_), channel_id=1, source_target_pairs={{0,2},{1,3},{2,6},{3,7},{6,4},{7,5},{4,0},{5,1},{8,10},{9,11},{10,... | collective-permute-start | bytes 884744 | tf_op jit(solution)/shard_map/ppermute | solution.py:491
  41.9 6.4 %collective-permute-start.11 = (bf16[128,1152]{1,0:T(8,128)(2,1)S(1)}, bf16[128,1152]{1,0:T(8,128)(2,1)S(1)}, u32[]{:S(2)}, u32[]{:S(2)}) collective-permute-start(bf16[128,1152]{1,0:T(8,128)(2,1)S(1)} %get-tuple-element.60), channel_id=1, source_target_pairs={{0,1},{1,0},{2,3},{3,2},{4,5},{5,4},{6,7},{7,6},{8,9},{9,8},{10,11... | collective-permute-start | bytes 884744 | tf_op jit(solution)/shard_map/ppermute | solution.py:494
  47.0 6.1 %collective-permute-start.10 = (bf16[32,1024]{1,0:T(8,128)(2,1)S(1)}, bf16[32,1024]{1,0:T(8,128)(2,1)S(1)}, u32[]{:S(2)}, u32[]{:S(2)}) collective-permute-start(bf16[32,1024]{1,0:T(8,128)(2,1)S(1)} %get-tuple-element.59.refs_0_), channel_id=1, source_target_pairs={{1,0},{2,1},{3,2},{4,3},{5,4},{6,5},{7,6},{9,8},{10,9},{11,10},{12... | collective-permute-start | bytes 196616 | tf_op jit(solution)/shard_map/ppermute | solution.py:636
  49.6 16.6 %collective-permute-start.12 = (bf16[128,1152]{1,0:T(8,128)(2,1)S(1)}, bf16[128,1152]{1,0:T(8,128)(2,1)S(1)}, u32[]{:S(2)}, u32[]{:S(2)}) collective-permute-start(bf16[128,1152]{1,0:T(8,128)(2,1)S(1)} %short_partner.1._), channel_id=1, source_target_pairs={{0,1},{1,0},{2,3},{3,2},{4,5},{5,4},{6,7},{7,6},{8,9},{9,8},{10,11... | collective-permute-start | bytes 884744 | tf_op jit(solution)/shard_map/ppermute | solution.py:494
  53.8 12.4 %collective-permute-start.13 = (bf16[128,1024]{1,0:T(8,128)(2,1)S(1)}, bf16[128,1024]{1,0:T(8,128)(2,1)S(1)}, u32[]{:S(2)}, u32[]{:S(2)}) collective-permute-start(bf16[128,1024]{1,0:T(8,128)(2,1)S(1)} %get-tuple-element.63.refs_0_), channel_id=1, source_target_pairs={{8,0},{16,8},{24,16},{9,1},{17,9},{25,17},{10,2},{18,10},{26,18},{... | collective-permute-start | bytes 786440 | tf_op jit(solution)/shard_map/ppermute | solution.py:674
